TPU v7x, 512 devices: a whole 4x8x8 slice. The times are simulated.
512 devices in a mesh: tensor: 16 (over z_hi, x, core), dp: 8 (over y), tenant: 4 (over z_lo).
Axes of the slice: x: 4, y: 8, z: 8 (z_hi: 2, z_lo: 4; z = z_hi * 4 + z_lo), core: 2. Of those that a mesh axis runs over, the one named last changes fastest.
Arguments:
- output_gradient: bfloat16 [32, 384, 8192], P(('dp', 'tenant'), 'tensor'), may hold values from -6 to 6
- inputs: bfloat16 [32, 384, 8192], P(('dp', 'tenant'), None, 'tensor'), may hold values from -6 to 6
- weight: bfloat16 [8192, 8192], P('tensor', ('dp', 'tenant')), may hold values from -0.0625 to 0.0625
- adapter_down_weight: bfloat16 [128, 16, 8192], P('tenant', None, 'tensor'), may hold values from -1.5 to 1.5
- adapter_up_weight: bfloat16 [128, 16, 8192], P('tenant', None, 'tensor'), may hold values from -0.0625 to 0.0625
- block_tenant_index: int32 [32, 3], P(('dp', 'tenant')), may hold values from 0 to 31
- block_live_count: int32 [32, 3], P(('dp', 'tenant')), may hold values from 1 to 128
Outputs:
- input_gradient: bfloat16 [32, 384, 8192], P(('dp', 'tenant'), None, 'tensor')
- grad_down: float32 [128, 16, 8192], P('tenant', 'dp', 'tensor')
- grad_up: float32 [128, 16, 8192], P('tenant', 'dp', 'tensor')
All inputs are finite; a program needn't handle non-finite values.
Results may differ from a plain program's by a relative error of at most 0.0065.
Values may be sent and summed in bfloat16 or wider, within the bound.
No kernel may reach another device: no remote copies, remote signals or barrier semaphores. Data moves between devices by JAX's collectives and lax.ppermute only.
A program may use at most 64 MiB of HBM per device.

v0:
```python
import jax
import jax.numpy as jnp
from jax import lax
from jax.sharding import PartitionSpec as P

adapter_scale = 2.0


def per_device(
    output_gradient,
    inputs,
    weight,
    adapter_down_weight,
    adapter_up_weight,
    block_tenant_index,
    block_live_count,
):
    gathered = lax.all_gather(output_gradient, "tensor", axis=1, tiled=True)
    nrows = gathered.shape[1]
    block_count = block_live_count.shape[1]
    block_length = nrows // block_count
    input_width = weight.shape[0]
    output_width = adapter_up_weight.shape[2]
    live_rows = (
        lax.broadcasted_iota(jnp.int32, (block_count, block_length), 1)
        < block_live_count[0][:, None]
    )
    masked = jnp.where(live_rows.reshape(nrows)[:, None], gathered[0], jnp.zeros((), jnp.bfloat16))
    frozen_base_weight = lax.dot_general(
        masked,
        lax.all_gather(weight, ("dp", "tenant"), axis=1, tiled=True),
        (((1,), (1,)), ((), ())),
        preferred_element_type=jnp.float32,
    )
    tenants_per_device = adapter_down_weight.shape[0]
    tenant_indicator = block_tenant_index[0][:, None] == lax.broadcasted_iota(
        jnp.int32, (block_count, tenants_per_device), 1
    )
    selected_down_weight = jnp.einsum(
        "xg,glj->xlj",
        tenant_indicator.astype(jnp.bfloat16),
        adapter_down_weight,
        preferred_element_type=jnp.float32,
    ).astype(jnp.bfloat16)
    selected_up_weight = jnp.einsum(
        "xg,glj->xlj",
        tenant_indicator.astype(jnp.bfloat16),
        adapter_up_weight,
        preferred_element_type=jnp.float32,
    ).astype(jnp.bfloat16)
    col_start = lax.axis_index("tensor") * output_width
    grad_cols = lax.dynamic_slice_in_dim(masked, col_start, output_width, 1).reshape(
        block_count, block_length, output_width
    )
    input_block_rows = inputs[0].reshape(block_count, block_length, input_width)
    part_in = jnp.einsum(
        "bmd,brd->bmr", input_block_rows, selected_down_weight, preferred_element_type=jnp.float32
    )
    part_out = jnp.einsum(
        "bmd,brd->bmr", grad_cols, selected_up_weight, preferred_element_type=jnp.float32
    )
    projection_input, projection_output = lax.psum((part_in, part_out), "tensor")
    projection_input = projection_input.astype(jnp.bfloat16)
    projection_output = projection_output.astype(jnp.bfloat16)
    adapter_contribution = jnp.einsum(
        "bmr,brd->bmd", projection_output, selected_down_weight, preferred_element_type=jnp.float32
    )
    input_gradient = (
        frozen_base_weight.reshape(block_count, block_length, input_width)
        + adapter_scale * adapter_contribution
    ).astype(jnp.bfloat16)
    input_gradient = input_gradient.reshape(1, nrows, input_width)
    down_partial_products = adapter_scale * jnp.einsum(
        "bmr,bmd->brd", projection_output, input_block_rows, preferred_element_type=jnp.float32
    )
    up_partial_products = adapter_scale * jnp.einsum(
        "bmr,bmd->brd", projection_input, grad_cols, preferred_element_type=jnp.float32
    )
    onehot_f = tenant_indicator.astype(jnp.float32)
    local_down = jnp.einsum("bt,brd->trd", onehot_f, down_partial_products)
    local_up = jnp.einsum("bt,brd->trd", onehot_f, up_partial_products)
    grad_down, grad_up = (
        lax.psum_scatter(local_down, "dp", scatter_dimension=1, tiled=True),
        lax.psum_scatter(local_up, "dp", scatter_dimension=1, tiled=True),
    )
    return (input_gradient, grad_down, grad_up)


def solution(mesh):
    placed = (
        P(("dp", "tenant"), "tensor", None),
        P(("dp", "tenant"), None, "tensor"),
        P("tensor", ("dp", "tenant")),
        P("tenant", None, "tensor"),
        P("tenant", None, "tensor"),
        P(("dp", "tenant"), None),
        P(("dp", "tenant"), None),
    )
    return jax.shard_map(
        per_device,
        mesh=mesh,
        in_specs=placed,
        out_specs=(
            P(("dp", "tenant"), None, "tensor"),
            P("tenant", "dp", "tensor"),
            P("tenant", "dp", "tensor"),
        ),
        check_vma=False,
    )
```

profile of v0, /device:TPU:28, one launch (start us, length us, event | category | flops | bytes accessed | tf_op | source)
XLA Modules:
  0.0 474.9 jit_solution(12328616823169734612)
XLA Ops:
  8.1 0.7 all-gather.3.cloned.1.call-update
  8.8 0.0 reduce-scatter.3.cloned.1.call-start
  8.8 0.7 fusion.26
  9.5 1.1 convolution_convert_fusion
  10.6 1.2 convolution_bitcast_fusion
  11.8 1.5 fusion.7
  13.3 100.3 %all-gather.3.cloned.1.call-done = bf16[1,384,8192]{2,1,0:T(8,128)(2,1)} async-done(((bf16[1,24,8192]{2,1,0:T(8,128)(2,1)}), bf16[1,384,8192]{2,1,0:T(8,128)(2,1)}) %all-gather.3.cloned.1.call-update) | async-done | bytes 6291472 | tf_op jit(solution)/shard_map/all_gather | solution.py:18
  113.6 1.1 dynamic-slice_select_fusion
  114.7 0.2 fusion.14
  114.9 71.5 %all-reduce = (bf16[3,128,16]{1,2,0:T(8,128)(2,1)S(1)}, bf16[3,128,16]{1,2,0:T(8,128)(2,1)S(1)}) all-reduce(f32[3,128,16]{1,2,0:T(8,128)S(1)} %fusion.14, f32[3,128,16]{1,2,0:T(8,128)S(1)} %convolution_bitcast_fusion), channel_id=1, replica_groups=mesh['tensor'=16,'dp'=8,'tenant'=4] {'tensor'}, use_global_device_ids=true, to_apply=%region_0.1 | all-reduce | flops 12288 | bytes 73728 | tf_op jit(solution)/shard_map/psum | solution.py:62
  186.4 1.2 fusion.32
  187.5 2.1 fusion.11
  189.6 0.0 reduce-scatter.5.cloned.1.call-start
  189.7 0.2 fusion.31
  189.8 1.4 fusion.10
  191.3 0.0 all-gather.5.cloned.1.call-start
  191.3 0.5 all-gather.5.cloned.1.call-update
  191.9 55.0 %reduce-scatter.3.cloned.1.call-done = f32[32,2,512]{2,0,1:T(8,128)} async-done(((f32[32,16,512]{2,0,1:T(8,128)}), f32[32,2,512]{2,0,1:T(8,128)}) %reduce-scatter.3.cloned.1.call-update) | async-done | bytes 131088 | tf_op jit(solution)/shard_map/reduce_scatter | solution.py:83
  246.9 1.7 copy.12
  248.6 46.8 %reduce-scatter.5.cloned.1.call-done = f32[32,2,512]{2,0,1:T(8,128)} async-done(((f32[32,16,512]{2,0,1:T(8,128)}), f32[32,2,512]{2,0,1:T(8,128)}) %reduce-scatter.5.cloned.1.call-update) | async-done | bytes 131088 | tf_op jit(solution)/shard_map/reduce_scatter | solution.py:84
  295.3 1.7 copy.13
  297.0 161.9 %all-gather.5.cloned.1.call-done = bf16[512,8192]{1,0:T(8,128)(2,1)} async-done(((bf16[512,256]{1,0:T(8,128)(2,1)}), bf16[512,8192]{1,0:T(8,128)(2,1)}) %all-gather.5.cloned.1.call-update) | async-done | bytes 8388624 | tf_op jit(solution)/shard_map/all_gather | solution.py:31
  458.9 7.8 %fusion = f32[3,128,512]{2,1,0:T(8,128)S(1)} fusion(bf16[512,8192]{1,0:T(8,128)(2,1)} %all-gather.5.cloned.1.call-done, bf16[3,128,8192]{2,1,0:T(8,128)(2,1)} %bitcast.33, pred[3,128]{1,0:T(4,128)(4,1)S(1)} %get-tuple-element.9), kind=kOutput, calls=%fused_computation | convolution fusion | flops 3224371200 | bytes 15466880 | tf_op jit(solution)/shard_map/dot_general | solution.py:29
  466.8 1.1 fusion.6
  (7 shorter events, 0.1 us)
Async XLA Ops:
  8.0 1.5 copy-start
  8.0 181.8 %copy-start.1 = (s32[1,3]{1,0:T(1,128)S(1)}, s32[1,3]{1,0:T(1,128)}, u32[]{:S(2)}) copy-start(s32[1,3]{1,0:T(1,128)} %param.12) | copy-start | bytes 40
  8.0 105.5 %all-gather.3.cloned.1.call-start = ((), (), s32[]{:S(2)}) async-start(), calls=%async_computation.2 | async-start | bytes 6684672 | tf_op jit(solution)/shard_map/all_gather | solution.py:18
  8.8 238.1 %reduce-scatter.3.cloned.1.call-start = ((), (), s32[]{:S(2)}) async-start(), calls=%async_computation.4 | async-start | bytes 1179648 | tf_op jit(solution)/shard_map/reduce_scatter | solution.py:83
  189.6 105.7 %reduce-scatter.5.cloned.1.call-start = ((), (), s32[]{:S(2)}) async-start(), calls=%async_computation.5 | async-start | bytes 1179648 | tf_op jit(solution)/shard_map/reduce_scatter | solution.py:84
  191.3 267.6 %all-gather.5.cloned.1.call-start = ((), (), s32[]{:S(2)}) async-start(), calls=%async_computation.3 | async-start | bytes 8650752 | tf_op jit(solution)/shard_map/all_gather | solution.py:31
Sparse Core Ops, SparseCore 0:
  12.2 101.3 all-gather.2
  189.7 57.1 reduce-scatter.2
  249.7 45.5 reduce-scatter.4
Sparse Core Ops, SparseCore 1:
  193.8 265.1 all-gather.4
where the time goes:
time: 475 us
  waiting for transfers between devices  365 us (77%)
  blocking collectives  71.5 us (15%)
  matrix products  17.6 us (4%)
  between operations  15.2 us (3%)
    all_gather x1, waiting for transfers between devices, per_device(): lax.all_gather(weight, ('dp', 'tenant'), axis=1, tiled=True)  162 us
    all_gather x1, waiting for transfers between devices, per_device(): gathered = lax.all_gather(output_gradient, 'tensor', axis=1, tiled=True)  100 us
    psum x1, blocking collectives, per_device(): lax.psum((part_in, part_out), 'tensor')  71.5 us
    reduce_scatter x1, waiting for transfers between devices, per_device(): lax.psum_scatter(local_down, 'dp', scatter_dimension=1, tiled=True)  55 us
    reduce_scatter x1, waiting for transfers between devices, per_device(): lax.psum_scatter(local_up, 'dp', scatter_dimension=1, tiled=True)  46.8 us
  transfers between devices with their start and end apart: 4, of which 4 were waited for; matrix products, arithmetic and copies ran while one was open for 2% of the time, Pallas kernels for 0%

commit v1 on v0

v1 whole, which is shorter than its diff:
```python
import jax
import jax.numpy as jnp
from jax import lax
from jax.sharding import Mesh, PartitionSpec as P

SCALE = 2.0
ZH, X, CORE, DP, TEN = 2, 4, 2, 8, 4
F32, BF16 = jnp.float32, jnp.bfloat16
TENSOR = ("zh", "x", "core")


def swap_pairs(n, bit):
    return [(i, i ^ bit) for i in range(n)]


def shift_pairs(n, offset):
    return [(i, (i + offset) % n) for i in range(n)]


def per_device(dy, inputs, weight, down, up, tenant_index, live_count):
    dy = dy[0]
    inputs = inputs[0]
    rows_here, width = dy.shape
    nrows, in_width = inputs.shape
    nblocks = live_count.shape[1]
    block = nrows // nblocks
    tenants, rank, _ = down.shape
    zh, x, core = lax.axis_index("zh"), lax.axis_index("x"), lax.axis_index("core")
    k = lax.axis_index("tenant")
    t = (zh * X + x) * CORE + core

    w_own = lax.all_gather(weight, "dp", axis=1, tiled=True)

    row = t * rows_here + lax.broadcasted_iota(jnp.int32, (rows_here, 1), 0)
    live = jnp.zeros((rows_here, 1), jnp.bool_)
    for b in range(nblocks):
        live |= (row >= b * block) & (row < b * block + live_count[0, b])
    dy = jnp.where(live, dy, jnp.zeros((), BF16))

    chunk = width // (DP * TEN)
    sets = dy.reshape(rows_here, DP, TEN, chunk).transpose(2, 0, 1, 3).reshape(TEN, rows_here, DP * chunk)
    sets = jnp.concatenate([sets, sets], axis=0)
    mine = lax.all_to_all(sets, ("zh", "tenant"), split_axis=0, concat_axis=0, tiled=True)
    group_rows = lax.all_gather(mine, "x", axis=0, tiled=False)

    hot = tenant_index[0][:, None] == lax.broadcasted_iota(jnp.int32, (nblocks, tenants), 1)
    hot = hot.astype(BF16)
    sel_down = jnp.einsum("bt,trd->brd", hot, down, preferred_element_type=F32).astype(BF16)
    sel_up = jnp.einsum("bt,trd->brd", hot, up, preferred_element_type=F32).astype(BF16)
    cols = lax.all_to_all(dy, TENSOR, split_axis=1, concat_axis=0, tiled=True)
    cols = cols.reshape(nblocks, block, -1)
    in_rows = inputs.reshape(nblocks, block, in_width)
    part_in = jnp.einsum("brd,bmd->brm", sel_down, in_rows, preferred_element_type=F32)
    part_out = jnp.einsum("brd,bmd->brm", sel_up, cols, preferred_element_type=F32)
    parts = jnp.concatenate([part_in, part_out], axis=1)
    parts = parts + lax.ppermute(parts, "core", swap_pairs(CORE, 1))
    parts = parts + lax.ppermute(parts, "x", swap_pairs(X, 1))
    parts = parts + lax.ppermute(parts, "x", swap_pairs(X, 3))
    parts = parts + lax.ppermute(parts, "zh", swap_pairs(ZH, 1))
    proj = parts.astype(BF16)
    proj_in, proj_out = proj[:, :rank], proj[:, rank:]

    w_other = lax.ppermute(w_own, "core", swap_pairs(CORE, 1))
    rows2d = group_rows.reshape(-1, DP * chunk)
    dims = (((1,), (1,)), ((), ()))
    for_other = lax.dot_general(rows2d, w_other, dims, preferred_element_type=F32).astype(BF16)
    from_other = lax.ppermute(for_other, "core", swap_pairs(CORE, 1))
    own = lax.dot_general(rows2d, w_own, dims, preferred_element_type=F32).astype(BF16)
    both = jnp.stack([own, from_other]).reshape(2, X, ZH, TEN, rows_here, in_width)

    def piece(offset):
        return lax.dynamic_index_in_dim(both, (k + offset) % TEN, 3, keepdims=False)

    total = piece(0).astype(F32)
    for offset in (2, 1, 3):
        total = total + lax.ppermute(piece(offset), "tenant", shift_pairs(TEN, offset)).astype(F32)
    total = jnp.where(core == 0, total, total[::-1])
    total = total.transpose(2, 1, 0, 3, 4).reshape(nblocks, block, in_width)
    adapter = jnp.einsum("brm,brd->bmd", proj_out, sel_down, preferred_element_type=F32)
    input_gradient = (total + SCALE * adapter).astype(BF16).reshape(1, nrows, in_width)

    g_down = SCALE * jnp.einsum("brm,bmd->brd", proj_out, in_rows, preferred_element_type=F32)
    g_up = SCALE * jnp.einsum("brm,bmd->brd", proj_in, cols, preferred_element_type=F32)
    share = rank // DP
    grads = jnp.stack([g_down, g_up]).reshape(2, nblocks, DP, share, in_width).transpose(2, 0, 1, 3, 4)
    grads = grads.reshape(DP, 2 * nblocks * share, in_width)
    ids = jnp.zeros((in_width,), F32)
    lane = lax.broadcasted_iota(jnp.int32, (in_width,), 0)
    for b in range(nblocks):
        ids = jnp.where(lane == b, tenant_index[0, b].astype(F32), ids)
    ids = jnp.broadcast_to(ids, (DP, 1, in_width))
    sent = jnp.concatenate([grads, ids], axis=1)
    got = lax.all_to_all(sent, "dp", split_axis=0, concat_axis=0, tiled=True)
    ids = got[:, -1, :nblocks].astype(jnp.int32)
    got = got[:, :-1].reshape(DP, 2, nblocks, share, in_width)
    place = (ids[None] == lax.broadcasted_iota(jnp.int32, (tenants, DP, nblocks), 0)).astype(F32)
    out = jnp.einsum("tgb,gabsd->atsd", place, got, precision=lax.Precision.HIGHEST, preferred_element_type=F32)
    return input_gradient, out[0], out[1]


def solution(mesh):
    fine = Mesh(mesh.devices.reshape(ZH, X, CORE, DP, TEN), ("zh", "x", "core", "dp", "tenant"))
    group = ("dp", "tenant")
    return jax.shard_map(
        per_device,
        mesh=fine,
        in_specs=(
            P(group, TENSOR, None),
            P(group, None, TENSOR),
            P(TENSOR, group),
            P("tenant", None, TENSOR),
            P("tenant", None, TENSOR),
            P(group, None),
            P(group, None),
        ),
        out_specs=(P(group, None, TENSOR), P("tenant", "dp", TENSOR), P("tenant", "dp", TENSOR)),
        check_vma=False,
    )
```

time: 475 us -> 182 us (0.38)
  the two profiles are of different devices: /device:TPU:28 before, /device:TPU:1 now
where the time goes in v1:
time: 182 us
  waiting for transfers between devices  60.4 us (33%)
  starting transfers between devices  47.8 us (26%)
  blocking collectives  32.4 us (18%)
  between operations  17.7 us (10%)
  matrix products  12.6 us (7%)
  local copies, waits for them, and re-layouts  6.36 us (3%)
  other arithmetic  4.27 us (2%)
    all_to_all x1, blocking collectives, per_device(): lax.all_to_all(sets, ('zh', 'tenant'), split_axis=0, concat_axis=0, tiled...  32.4 us
    ppermute x3, waiting for transfers between devices, per_device(): lax.ppermute(piece(offset), 'tenant', shift_pairs(TEN, offset)).astype(F32)  27.1 us
    all_gather x1, waiting for transfers between devices, per_device(): group_rows = lax.all_gather(mine, 'x', axis=0, tiled=False)  18.3 us
    ppermute x3, starting transfers between devices, per_device(): lax.ppermute(piece(offset), 'tenant', shift_pairs(TEN, offset)).astype(F32)  9.97 us
    all_gather x1, waiting for transfers between devices, per_device(): w_own = lax.all_gather(weight, 'dp', axis=1, tiled=True)  8.36 us
    ppermute x1, starting transfers between devices, per_device(): parts = parts + lax.ppermute(parts, 'zh', swap_pairs(ZH, 1))  7.54 us
    ppermute x1, starting transfers between devices, per_device(): w_other = lax.ppermute(w_own, 'core', swap_pairs(CORE, 1))  7.41 us
    all_to_all x1, starting transfers between devices, per_device(): cols = lax.all_to_all(dy, TENSOR, split_axis=1, concat_axis=0, tiled=True)  6.77 us
  transfers between devices with their start and end apart: 13, of which 9 were waited for; matrix products, arithmetic and copies ran while one was open for 8% of the time, Pallas kernels for 0%

profile of v1, /device:TPU:1, one launch (start us, length us, event | category | flops | bytes accessed | tf_op | source)
XLA Modules:
  0.0 181.5 jit_solution(6257342772439701672)
XLA Ops:
  8.0 1.3 squeeze.32
  9.3 1.4 fusion.33
  13.0 32.4 %all_to_all.23 = bf16[8,24,2048]{2,1,0:T(8,128)(2,1)} all-to-all(bf16[8,24,2048]{2,1,0:T(8,128)(2,1)S(1)} %pad_maximum_fusion), channel_id=1, replica_groups=mesh['zh'=2,'x'=4,'core'=2,'dp'=8,'tenant'=4] {'zh','tenant'}, dimensions={0} | all-to-all | bytes 1572864 | tf_op jit(solution)/shard_map/all_to_all | solution.py:43
  46.5 6.8 %all-to-all-start.1 = ((bf16[24,16,512]{2,0,1:T(8,128)(2,1)}), bf16[24,16,512]{2,0,1:T(8,128)(2,1)S(1)}, u32[]{:S(2)}, u32[]{:S(2)}) async-start(bf16[24,16,512]{2,0,1:T(8,128)(2,1)} %copy_select_fusion), calls=%async_computation.1 | async-start | bytes 786432 | tf_op jit(solution)/shard_map/all_to_all | solution.py:50
  53.3 8.4 %all-gather.4.cloned.1.call-done = bf16[512,2048]{1,0:T(8,128)(2,1)} async-done(((bf16[512,256]{1,0:T(8,128)(2,1)}), bf16[512,2048]{1,0:T(8,128)(2,1)}) %all-gather.4.cloned.1.call-update) | async-done | bytes 2097168 | tf_op jit(solution)/shard_map/all_gather | solution.py:32
  61.6 7.4 %collective-permute-start = (bf16[512,2048]{1,0:T(8,128)(2,1)}, bf16[512,2048]{1,0:T(8,128)(2,1)}, u32[]{:S(2)}, u32[]{:S(2)}) collective-permute-start(bf16[512,2048]{1,0:T(8,128)(2,1)} %all-gather.4.cloned.1.call-done), channel_id=1, source_target_pairs={{0,32},{32,0},{1,33},{33,1},{2,34},{34,2},{3,35},{35,3},{4,36},{36... | collective-permute-start | bytes 6291464 | tf_op jit(solution)/shard_map/ppermute | solution.py:63
  70.3 1.9 %collective-permute-start.5 = (f32[3,32,128]{2,1,0:T(8,128)S(1)}, f32[3,32,128]{2,1,0:T(8,128)S(1)}, u32[]{:S(2)}, u32[]{:S(2)}) collective-permute-start(f32[3,32,128]{2,1,0:T(8,128)S(1)} %pad_maximum_fusion.3), channel_id=1, source_target_pairs={{0,32},{32,0},{1,33},{33,1},{2,34},{34,2},{3,35},{35,3},{4,36},{36... | collective-permute-start | bytes 147464 | tf_op jit(solution)/shard_map/ppermute | solution.py:56
  73.5 1.9 %collective-permute-start.6 = (f32[3,32,128]{2,1,0:T(8,128)S(1)}, f32[3,32,128]{2,1,0:T(8,128)S(1)}, u32[]{:S(2)}, u32[]{:S(2)}) collective-permute-start(f32[3,32,128]{2,1,0:T(8,128)S(1)} %fusion.31), channel_id=1, source_target_pairs={{0,64},{64,0},{128,192},{192,128},{1,65},{65,1},{129,193},{193,129... | collective-permute-start | bytes 147464 | tf_op jit(solution)/shard_map/ppermute | solution.py:57
  75.4 2.9 %collective-permute-done.6 = f32[3,32,128]{2,1,0:T(8,128)S(1)} collective-permute-done((f32[3,32,128]{2,1,0:T(8,128)S(1)}, f32[3,32,128]{2,1,0:T(8,128)S(1)}, u32[]{:S(2)}, u32[]{:S(2)}) %collective-permute-start.6) | collective-permute-done | bytes 49184 | tf_op jit(solution)/shard_map/ppermute | solution.py:57
  78.3 3.1 %collective-permute-start.7 = (f32[3,32,128]{2,1,0:T(8,128)S(1)}, f32[3,32,128]{2,1,0:T(8,128)S(1)}, u32[]{:S(2)}, u32[]{:S(2)}) collective-permute-start(f32[3,32,128]{2,1,0:T(8,128)S(1)} %add.111), channel_id=1, source_target_pairs={{0,192},{64,128},{128,64},{192,0},{1,193},{65,129},{129,65},{193,1... | collective-permute-start | bytes 147464 | tf_op jit(solution)/shard_map/ppermute | solution.py:58
  84.4 7.5 %collective-permute-start.8 = (f32[3,32,128]{2,1,0:T(8,128)S(1)}, f32[3,32,128]{2,1,0:T(8,128)S(1)}, u32[]{:S(2)}, u32[]{:S(2)}) collective-permute-start(f32[3,32,128]{2,1,0:T(8,128)S(1)} %add.112), channel_id=1, source_target_pairs={{0,256},{256,0},{1,257},{257,1},{2,258},{258,2},{3,259},{259,3},{4... | collective-permute-start | bytes 147464 | tf_op jit(solution)/shard_map/ppermute | solution.py:59
  92.0 1.5 collective-permute-done.8
  93.6 18.3 %all-gather.6.cloned.1.call-done = bf16[32,24,2048]{2,1,0:T(8,128)(2,1)} async-done(((bf16[8,24,2048]{2,1,0:T(8,128)(2,1)}), bf16[32,24,2048]{2,1,0:T(8,128)(2,1)}) %all-gather.6.cloned.1.call-update) | async-done | bytes 3145744 | tf_op jit(solution)/shard_map/all_gather | solution.py:44
  111.9 5.3 %convolution_convert_fusion = bf16[768,512]{1,0:T(8,128)(2,1)} fusion(bf16[768,2048]{1,0:T(8,128)(2,1)} %bitcast.93, bf16[512,2048]{1,0:T(8,128)(2,1)} %collective-permute-done), kind=kOutput, calls=%fused_computation.8 | convolution fusion | flops 1611005952 | bytes 6029312 | tf_op jit(solution)/shard_map/dot_general | solution.py:66
  117.2 2.6 %collective-permute-start.1 = (bf16[768,512]{1,0:T(8,128)(2,1)}, bf16[768,512]{1,0:T(8,128)(2,1)S(1)}, u32[]{:S(2)}, u32[]{:S(2)}) collective-permute-start(bf16[768,512]{1,0:T(8,128)(2,1)} %convolution_convert_fusion), channel_id=1, source_target_pairs={{0,32},{32,0},{1,33},{33,1},{2,34},{34,2},{3,35},{35,3},{4,36},{36... | collective-permute-start | bytes 2359304 | tf_op jit(solution)/shard_map/ppermute | solution.py:67
  121.0 6.5 %all-to-all-start.2 = ((f32[8,13,512]{2,1,0:T(8,128)}), f32[8,13,512]{2,1,0:T(8,128)S(1)}, u32[]{:S(2)}, u32[]{:S(2)}) async-start(f32[8,13,512]{2,1,0:T(8,128)} %copy.68), calls=%async_computation.2 | async-start | bytes 524288 | tf_op jit(solution)/shard_map/all_to_all | solution.py:93
  127.5 4.4 %convolution_convert_fusion.1 = bf16[768,512]{1,0:T(8,128)(2,1)S(1)} fusion(bf16[768,2048]{1,0:T(8,128)(2,1)} %bitcast.94, bf16[512,2048]{1,0:T(8,128)(2,1)} %all-gather.4.cloned.1.call-done), kind=kOutput, calls=%fused_computation.9 | convolution fusion | flops 1611005952 | bytes 6029312 | tf_op jit(solution)/shard_map/dot_general | solution.py:68
  132.8 5.4 %collective-permute-start.4 = (bf16[2,4,2,24,512]{4,3,2,1,0:T(8,128)(2,1)}, bf16[2,4,2,24,512]{4,3,2,1,0:T(8,128)(2,1)S(1)}, u32[]{:S(2)}, u32[]{:S(2)}) collective-permute-start(bf16[2,4,2,24,512]{4,3,2,1,0:T(8,128)(2,1)} %get-tuple-element.20), channel_id=1, source_target_pairs={{0,3},{1,0},{2,1},{3,2},{4,7},{5,4},{6,5},{7,6},{8,11},{9,8},{10,9... | collective-permute-start | bytes 1179656 | tf_op jit(solution)/shard_map/ppermute | solution.py:76
  138.3 1.9 %collective-permute-start.3 = (bf16[2,4,2,24,512]{4,3,2,1,0:T(8,128)(2,1)}, bf16[2,4,2,24,512]{4,3,2,1,0:T(8,128)(2,1)}, u32[]{:S(2)}, u32[]{:S(2)}) collective-permute-start(bf16[2,4,2,24,512]{4,3,2,1,0:T(8,128)(2,1)} %get-tuple-element.19), channel_id=1, source_target_pairs={{0,1},{1,2},{2,3},{3,0},{4,5},{5,6},{6,7},{7,4},{8,9},{9,10},{10,1... | collective-permute-start | bytes 1179656 | tf_op jit(solution)/shard_map/ppermute | solution.py:76
  140.2 2.6 %collective-permute-start.2 = (bf16[2,4,2,24,512]{4,3,2,1,0:T(8,128)(2,1)S(1)}, bf16[2,4,2,24,512]{4,3,2,1,0:T(8,128)(2,1)}, u32[]{:S(2)}, u32[]{:S(2)}) collective-permute-start(bf16[2,4,2,24,512]{4,3,2,1,0:T(8,128)(2,1)S(1)} %get-tuple-element.18), channel_id=1, source_target_pairs={{0,2},{1,3},{2,0},{3,1},{4,6},{5,7},{6,4},{7,5},{8,10},{9,11},{10,... | collective-permute-start | bytes 1179656 | tf_op jit(solution)/shard_map/ppermute | solution.py:76
  145.0 1.8 collective-permute-done.4
  146.8 9.6 %collective-permute-done.3 = bf16[2,4,2,24,512]{4,3,2,1,0:T(8,128)(2,1)} collective-permute-done((bf16[2,4,2,24,512]{4,3,2,1,0:T(8,128)(2,1)}, bf16[2,4,2,24,512]{4,3,2,1,0:T(8,128)(2,1)}, u32[]{:S(2)}, u32[]{:S(2)}) %collective-permute-start.3) | collective-permute-done | bytes 393248 | tf_op jit(solution)/shard_map/ppermute | solution.py:76
  156.4 15.7 %collective-permute-done.2 = bf16[2,4,2,24,512]{4,3,2,1,0:T(8,128)(2,1)} collective-permute-done((bf16[2,4,2,24,512]{4,3,2,1,0:T(8,128)(2,1)S(1)}, bf16[2,4,2,24,512]{4,3,2,1,0:T(8,128)(2,1)}, u32[]{:S(2)}, u32[]{:S(2)}) %collective-permute-start.2) | collective-permute-done | bytes 393248 | tf_op jit(solution)/shard_map/ppermute | solution.py:76
  172.1 1.3 fusion.4
  (60 shorter events, 12.0 us)
Async XLA Ops:
  7.2 61.9 %copy-start = (bf16[32,16,512]{2,1,0:T(8,128)(2,1)S(1)}, bf16[32,16,512]{2,1,0:T(8,128)(2,1)}, u32[]{:S(2)}) copy-start(bf16[32,16,512]{2,1,0:T(8,128)(2,1)} %param.10) | copy-start | bytes 1572868
  7.2 54.4 %all-gather.4.cloned.1.call-start = ((), (), s32[]{:S(2)}) async-start(), calls=%async_computation.3 | async-start | bytes 2359296 | tf_op jit(solution)/shard_map/all_gather | solution.py:32
  7.9 104.0 %all-gather.6.cloned.1.call-start = ((), (), s32[]{:S(2)}) async-start(), calls=%async_computation.4 | async-start | bytes 3932160 | tf_op jit(solution)/shard_map/all_gather | solution.py:44
  12.7 32.7 %copy-start.1 = (bf16[1,24,8192]{2,1,0:T(8,128)(2,1)S(1)}, bf16[1,24,8192]{2,1,0:T(8,128)(2,1)}, u32[]{:S(2)}) copy-start(bf16[1,24,8192]{2,1,0:T(8,128)(2,1)} %param.7) | copy-start | bytes 1179652
  13.0 56.1 %copy-start.4 = (s32[1,3]{1,0:T(1,128)S(1)}, s32[1,3]{1,0:T(1,128)}, u32[]{:S(2)}) copy-start(s32[1,3]{1,0:T(1,128)} %param.12) | copy-start | bytes 40
  45.3 24.1 %copy-start.2 = (bf16[1,384,512]{2,1,0:T(8,128)(2,1)S(1)}, bf16[1,384,512]{2,1,0:T(8,128)(2,1)}, u32[]{:S(2)}) copy-start(bf16[1,384,512]{2,1,0:T(8,128)(2,1)} %param.8) | copy-start | bytes 1179652
  45.4 24.3 %copy-start.3 = (bf16[32,16,512]{2,1,0:T(8,128)(2,1)S(1)}, bf16[32,16,512]{2,1,0:T(8,128)(2,1)}, u32[]{:S(2)}) copy-start(bf16[32,16,512]{2,1,0:T(8,128)(2,1)} %param.11) | copy-start | bytes 1572868
  46.5 23.6 %all-to-all-start.1 = ((bf16[24,16,512]{2,0,1:T(8,128)(2,1)}), bf16[24,16,512]{2,0,1:T(8,128)(2,1)S(1)}, u32[]{:S(2)}, u32[]{:S(2)}) async-start(bf16[24,16,512]{2,0,1:T(8,128)(2,1)} %copy_select_fusion), calls=%async_computation.1 | async-start | bytes 786432 | tf_op jit(solution)/shard_map/all_to_all | solution.py:50
  61.6 32.0 %collective-permute-start = (bf16[512,2048]{1,0:T(8,128)(2,1)}, bf16[512,2048]{1,0:T(8,128)(2,1)}, u32[]{:S(2)}, u32[]{:S(2)}) collective-permute-start(bf16[512,2048]{1,0:T(8,128)(2,1)} %all-gather.4.cloned.1.call-done), channel_id=1, source_target_pairs={{0,32},{32,0},{1,33},{33,1},{2,34},{34,2},{3,35},{35,3},{4,36},{36... | collective-permute-start | bytes 6291464 | tf_op jit(solution)/shard_map/ppermute | solution.py:63
  70.3 3.1 %collective-permute-start.5 = (f32[3,32,128]{2,1,0:T(8,128)S(1)}, f32[3,32,128]{2,1,0:T(8,128)S(1)}, u32[]{:S(2)}, u32[]{:S(2)}) collective-permute-start(f32[3,32,128]{2,1,0:T(8,128)S(1)} %pad_maximum_fusion.3), channel_id=1, source_target_pairs={{0,32},{32,0},{1,33},{33,1},{2,34},{34,2},{3,35},{35,3},{4,36},{36... | collective-permute-start | bytes 147464 | tf_op jit(solution)/shard_map/ppermute | solution.py:56
  73.5 4.8 %collective-permute-start.6 = (f32[3,32,128]{2,1,0:T(8,128)S(1)}, f32[3,32,128]{2,1,0:T(8,128)S(1)}, u32[]{:S(2)}, u32[]{:S(2)}) collective-permute-start(f32[3,32,128]{2,1,0:T(8,128)S(1)} %fusion.31), channel_id=1, source_target_pairs={{0,64},{64,0},{128,192},{192,128},{1,65},{65,1},{129,193},{193,129... | collective-permute-start | bytes 147464 | tf_op jit(solution)/shard_map/ppermute | solution.py:57
  78.3 6.0 %collective-permute-start.7 = (f32[3,32,128]{2,1,0:T(8,128)S(1)}, f32[3,32,128]{2,1,0:T(8,128)S(1)}, u32[]{:S(2)}, u32[]{:S(2)}) collective-permute-start(f32[3,32,128]{2,1,0:T(8,128)S(1)} %add.111), channel_id=1, source_target_pairs={{0,192},{64,128},{128,64},{192,0},{1,193},{65,129},{129,65},{193,1... | collective-permute-start | bytes 147464 | tf_op jit(solution)/shard_map/ppermute | solution.py:58
  84.4 9.1 %collective-permute-start.8 = (f32[3,32,128]{2,1,0:T(8,128)S(1)}, f32[3,32,128]{2,1,0:T(8,128)S(1)}, u32[]{:S(2)}, u32[]{:S(2)}) collective-permute-start(f32[3,32,128]{2,1,0:T(8,128)S(1)} %add.112), channel_id=1, source_target_pairs={{0,256},{256,0},{1,257},{257,1},{2,258},{258,2},{3,259},{259,3},{4... | collective-permute-start | bytes 147464 | tf_op jit(solution)/shard_map/ppermute | solution.py:59
  117.2 14.6 %collective-permute-start.1 = (bf16[768,512]{1,0:T(8,128)(2,1)}, bf16[768,512]{1,0:T(8,128)(2,1)S(1)}, u32[]{:S(2)}, u32[]{:S(2)}) collective-permute-start(bf16[768,512]{1,0:T(8,128)(2,1)} %convolution_convert_fusion), channel_id=1, source_target_pairs={{0,32},{32,0},{1,33},{33,1},{2,34},{34,2},{3,35},{35,3},{4,36},{36... | collective-permute-start | bytes 2359304 | tf_op jit(solution)/shard_map/ppermute | solution.py:67
  121.0 21.8 %all-to-all-start.2 = ((f32[8,13,512]{2,1,0:T(8,128)}), f32[8,13,512]{2,1,0:T(8,128)S(1)}, u32[]{:S(2)}, u32[]{:S(2)}) async-start(f32[8,13,512]{2,1,0:T(8,128)} %copy.68), calls=%async_computation.2 | async-start | bytes 524288 | tf_op jit(solution)/shard_map/all_to_all | solution.py:93
  132.8 14.0 %collective-permute-start.4 = (bf16[2,4,2,24,512]{4,3,2,1,0:T(8,128)(2,1)}, bf16[2,4,2,24,512]{4,3,2,1,0:T(8,128)(2,1)S(1)}, u32[]{:S(2)}, u32[]{:S(2)}) collective-permute-start(bf16[2,4,2,24,512]{4,3,2,1,0:T(8,128)(2,1)} %get-tuple-element.20), channel_id=1, source_target_pairs={{0,3},{1,0},{2,1},{3,2},{4,7},{5,4},{6,5},{7,6},{8,11},{9,8},{10,9... | collective-permute-start | bytes 1179656 | tf_op jit(solution)/shard_map/ppermute | solution.py:76
  138.3 18.1 %collective-permute-start.3 = (bf16[2,4,2,24,512]{4,3,2,1,0:T(8,128)(2,1)}, bf16[2,4,2,24,512]{4,3,2,1,0:T(8,128)(2,1)}, u32[]{:S(2)}, u32[]{:S(2)}) collective-permute-start(bf16[2,4,2,24,512]{4,3,2,1,0:T(8,128)(2,1)} %get-tuple-element.19), channel_id=1, source_target_pairs={{0,1},{1,2},{2,3},{3,0},{4,5},{5,6},{6,7},{7,4},{8,9},{9,10},{10,1... | collective-permute-start | bytes 1179656 | tf_op jit(solution)/shard_map/ppermute | solution.py:76
  140.2 31.9 %collective-permute-start.2 = (bf16[2,4,2,24,512]{4,3,2,1,0:T(8,128)(2,1)S(1)}, bf16[2,4,2,24,512]{4,3,2,1,0:T(8,128)(2,1)}, u32[]{:S(2)}, u32[]{:S(2)}) collective-permute-start(bf16[2,4,2,24,512]{4,3,2,1,0:T(8,128)(2,1)S(1)} %get-tuple-element.18), channel_id=1, source_target_pairs={{0,2},{1,3},{2,0},{3,1},{4,6},{5,7},{6,4},{7,5},{8,10},{9,11},{10,... | collective-permute-start | bytes 1179656 | tf_op jit(solution)/shard_map/ppermute | solution.py:76
Sparse Core Ops, SparseCore 0:
  10.0 51.5 all-gather.3
  63.7 48.1 all-gather.5

commit v2 on v1

v2 whole, which is shorter than its diff:
```python
import functools

import jax
import jax.numpy as jnp
from jax import lax
from jax.experimental import pallas as pl
from jax.experimental.pallas import tpu as pltpu
from jax.sharding import Mesh, PartitionSpec as P

SCALE = 2.0
ZH, X, CORE, DP, KH, KL = 2, 4, 2, 8, 2, 2
TENSOR, TENANT = ("zh", "x", "core"), ("kh", "kl")
AXES = TENSOR + ("dp",) + TENANT
F32, BF16 = jnp.float32, jnp.bfloat16
GROUPS = ((0, 1, 3), (2,))
VMEM_LIMIT = 48 * 2**20


def exchange(blocks, axes):
    return lax.all_to_all(blocks, axes, split_axis=0, concat_axis=0, tiled=True)


def swap_pairs(n, bit):
    return [(i, i ^ bit) for i in range(n)]


def shift_pairs(n, offset):
    return [(i, (i + offset) % n) for i in range(n)]


def split_kernel(nblocks, block, at_ref, live_ref, dy_ref, same_ref, other_ref, cols_ref):
    rows, width = dy_ref.shape
    first, kh, kl = at_ref[0], at_ref[1], at_ref[2]
    row = first + lax.broadcasted_iota(jnp.int32, (rows, 1), 0)
    live = jnp.zeros((rows, 1), jnp.int32)
    for b in range(nblocks):
        inside = (row >= b * block) & (row < b * block + live_ref[0, b])
        live = jnp.where(inside, 1, live)
    live = live > 0
    chunk = width // (DP * KH * KL)
    wide = cols_ref.shape[2]
    for d in range(DP):
        to = slice(d * chunk, (d + 1) * chunk)
        for low in range(KL):
            parts = []
            for h in range(KH):
                at = ((d * KH + h) * KL + low) * chunk
                part = jnp.where(live, dy_ref[:, at : at + chunk].astype(F32), 0.0)
                cols_ref[at // wide, :, at % wide : at % wide + chunk] = part.astype(BF16)
                parts.append(part)
            slot = lax.rem(kl + low, KL)
            same_ref[slot, :, to] = jnp.where(kh == 0, parts[0], parts[1]).astype(BF16)
            other_ref[slot, :, to] = jnp.where(kh == 0, parts[1], parts[0]).astype(BF16)


def split_rows(dy, at, live_count, nblocks, block):
    rows, width = dy.shape
    half = jax.ShapeDtypeStruct((KL, rows, width // (KH * KL)), BF16)
    shapes = [half, half, jax.ShapeDtypeStruct((ZH * X * CORE, rows, width // (ZH * X * CORE)), BF16)]
    vmem = pl.BlockSpec(memory_space=pltpu.VMEM)
    smem = pl.BlockSpec(memory_space=pltpu.SMEM)
    return pl.pallas_call(
        functools.partial(split_kernel, nblocks, block),
        out_shape=shapes,
        in_specs=[smem, smem, vmem],
        out_specs=[vmem] * len(shapes),
        cost_estimate=pl.CostEstimate(flops=0, bytes_accessed=3 * rows * width * 2, transcendentals=0),
        compiler_params=pltpu.CompilerParams(vmem_limit_bytes=VMEM_LIMIT),
        name="split_rows",
    )(at, live_count, dy)


def base_kernel(count, w_ref, *refs):
    pieces, keep_ref, send_ref = refs[:count], refs[count], refs[count + 1]
    m = pieces[0].shape[2]
    feats, chunk = w_ref.shape[2:]
    total = None
    for h in range(KL):
        rows = [piece[:, h].reshape(KH * ZH * m, DP * chunk) for piece in pieces]
        rows = jnp.concatenate(rows, axis=0)
        for d in range(DP):
            term = lax.dot_general(
                rows[:, d * chunk : (d + 1) * chunk], w_ref[d, h], (((1,), (1,)), ((), ())), preferred_element_type=F32
            )
            total = term if total is None else total + term
    total = total.reshape(count, KH, ZH, m, feats)
    keep_ref[...] = total[:, 0].reshape(keep_ref.shape)
    send_ref[...] = total[:, 1].reshape(send_ref.shape).astype(BF16)


def base_product(weights, pieces):
    count, m, feats = len(pieces), pieces[0].shape[2], weights.shape[2]
    vmem = pl.BlockSpec(memory_space=pltpu.VMEM)
    rows = count * ZH * KH * m
    shape = (count * ZH, m, feats)
    return pl.pallas_call(
        functools.partial(base_kernel, count),
        out_shape=[jax.ShapeDtypeStruct(shape, F32), jax.ShapeDtypeStruct(shape, BF16)],
        in_specs=[vmem] * (1 + count),
        out_specs=[vmem] * 2,
        cost_estimate=pl.CostEstimate(
            flops=2 * rows * weights.size, bytes_accessed=2 * (count * pieces[0].size + weights.size + rows * feats), transcendentals=0
        ),
        compiler_params=pltpu.CompilerParams(vmem_limit_bytes=VMEM_LIMIT),
        name="base_product",
    )(weights, *pieces)


def parts_kernel(down_ref, up_ref, in_ref, cols_ref, out_ref):
    nblocks = down_ref.shape[0]
    block = in_ref.shape[0] // nblocks
    dims = (((1,), (1,)), ((), ()))
    for i, (factor, rows_ref) in enumerate(((down_ref, in_ref), (up_ref, cols_ref))):
        for b in range(nblocks):
            rows = rows_ref[b * block : (b + 1) * block, :]
            part = lax.dot_general(factor[b], rows, dims, preferred_element_type=F32)
            for to in range(out_ref.shape[0]):
                out_ref[to, i * nblocks + b] = part


def rank_parts(sel_down, sel_up, inputs, cols):
    nblocks, rank, _ = sel_down.shape
    vmem = pl.BlockSpec(memory_space=pltpu.VMEM)
    return pl.pallas_call(
        parts_kernel,
        out_shape=jax.ShapeDtypeStruct((X * CORE, 2 * nblocks, rank, inputs.shape[0] // nblocks), F32),
        in_specs=[vmem] * 4,
        out_specs=vmem,
        cost_estimate=pl.CostEstimate(flops=4 * rank * inputs.size, bytes_accessed=6 * inputs.size, transcendentals=0),
        compiler_params=pltpu.CompilerParams(vmem_limit_bytes=VMEM_LIMIT),
        name="rank_parts",
    )(sel_down, sel_up, inputs, cols)


def grads_kernel(ids_ref, own_ref, got_ref, in_ref, cols_ref, out_ref, proj_ref):
    nblocks = own_ref.shape[0] // 2
    block, wide = in_ref.shape[0] // nblocks, in_ref.shape[1]
    share = own_ref.shape[1] // DP
    proj = (own_ref[...] + got_ref[...]).astype(BF16)
    proj_ref[...] = proj[nblocks:]
    dims = (((1,), (0,)), ((), ()))
    for b in range(nblocks):
        rows = slice(b * block, (b + 1) * block)
        down = lax.dot_general(proj[nblocks + b], in_ref[rows, :], dims, preferred_element_type=F32)
        up = lax.dot_general(proj[b], cols_ref[rows, :], dims, preferred_element_type=F32)
        for i, grad in enumerate((SCALE * down, SCALE * up)):
            at = (i * nblocks + b) * share
            for to in range(DP):
                out_ref[to, at : at + share, :] = grad[to * share : (to + 1) * share]
    lane = lax.broadcasted_iota(jnp.int32, (1, wide), 1)
    ids = jnp.zeros((1, wide), F32)
    for b in range(nblocks):
        ids = jnp.where(lane == b, ids_ref[0, b].astype(F32), ids)
    for to in range(DP):
        out_ref[to, 2 * nblocks * share :, :] = ids


def block_grads(tenant_index, own, got, inputs, cols):
    count, rank, block = own.shape
    nblocks = count // 2
    wide = inputs.shape[1]
    vmem = pl.BlockSpec(memory_space=pltpu.VMEM)
    smem = pl.BlockSpec(memory_space=pltpu.SMEM)
    return pl.pallas_call(
        grads_kernel,
        out_shape=[
            jax.ShapeDtypeStruct((DP, 2 * nblocks * rank // DP + 1, wide), F32),
            jax.ShapeDtypeStruct((nblocks, rank, block), BF16),
        ],
        in_specs=[smem] + [vmem] * 4,
        out_specs=[vmem, vmem],
        cost_estimate=pl.CostEstimate(flops=4 * rank * inputs.size, bytes_accessed=6 * inputs.size, transcendentals=0),
        compiler_params=pltpu.CompilerParams(vmem_limit_bytes=VMEM_LIMIT),
        name="block_grads",
    )(tenant_index, own, got, inputs, cols)


def join_kernel(nblocks, group_sizes, where_ref, proj_ref, down_ref, *refs):
    adapter_ref, out_ref = refs[-1], refs[-2]
    m = out_ref.shape[1]
    terms = [
        SCALE
        * lax.dot_general(proj_ref[b], down_ref[b], (((0,), (0,)), ((), ())), preferred_element_type=F32)
        for b in range(nblocks)
    ]
    adapter_ref[...] = jnp.concatenate(terms, axis=0).reshape(adapter_ref.shape)
    at, place = 0, 0
    for size in group_sizes:
        keep, got = refs[at : at + 2]
        at += 2
        for p in range(size):
            for z in range(ZH):
                to = where_ref[place]
                place += 1
                total = keep[p * ZH + z] + got[p * ZH + z].astype(F32) + adapter_ref[to]
                out_ref[to] = total.astype(BF16)


def join(where, proj_out, sel_down, groups):
    m, feats = groups[0][0].shape[1:]
    blocks = ZH * X * CORE
    vmem = pl.BlockSpec(memory_space=pltpu.VMEM)
    smem = pl.BlockSpec(memory_space=pltpu.SMEM)
    parts = [part for group in groups for part in group]
    return pl.pallas_call(
        functools.partial(join_kernel, proj_out.shape[0], [group[0].shape[0] // ZH for group in groups]),
        out_shape=jax.ShapeDtypeStruct((blocks, m, feats), BF16),
        in_specs=[smem] + [vmem] * (2 + len(parts)),
        out_specs=vmem,
        scratch_shapes=[pltpu.VMEM((blocks, m, feats), F32)],
        cost_estimate=pl.CostEstimate(flops=0, bytes_accessed=10 * blocks * m * feats, transcendentals=0),
        compiler_params=pltpu.CompilerParams(vmem_limit_bytes=VMEM_LIMIT),
        name="join_rows",
    )(where, proj_out, sel_down, *parts)


def per_device(dy, inputs, weight, down, up, tenant_index, live_count):
    dy, inputs = dy[0], inputs[0]
    rows_here = dy.shape[0]
    nrows, in_width = inputs.shape
    nblocks = live_count.shape[1]
    block = nrows // nblocks
    tenants, rank, _ = down.shape
    zh, x, core = lax.axis_index("zh"), lax.axis_index("x"), lax.axis_index("core")
    kh, kl = lax.axis_index("kh"), lax.axis_index("kl")
    t = (zh * X + x) * CORE + core

    at = jnp.stack([t * rows_here, kh, kl]).astype(jnp.int32)
    same, other, cols = split_rows(dy, at, live_count, nblocks, block)

    swapped, _ = lax.optimization_barrier((lax.ppermute(weight, "kl", swap_pairs(KL, 1)), same))
    weights = lax.all_gather(jnp.stack([weight, swapped]), "dp", axis=0, tiled=False)

    from_zh = lax.ppermute(same, "zh", swap_pairs(ZH, 1))
    from_both = lax.ppermute(other, ("zh", "kh"), swap_pairs(ZH * KH, 3))
    from_kh = lax.ppermute(other, "kh", swap_pairs(KH, 1))
    mine = jnp.stack([same, from_zh, from_kh, from_both])
    hot = tenant_index[0][:, None] == lax.broadcasted_iota(jnp.int32, (nblocks, tenants), 1)
    hot = hot.astype(BF16)
    sel_down = jnp.einsum("bt,trd->brd", hot, down, preferred_element_type=F32).astype(BF16)
    sel_up = jnp.einsum("bt,trd->brd", hot, up, preferred_element_type=F32).astype(BF16)
    cols = exchange(cols, TENSOR).reshape(nrows, -1)
    parts = exchange(rank_parts(sel_down, sel_up, inputs, cols), ("x", "core"))
    parts, mine = lax.optimization_barrier((parts, mine))
    parts = parts.sum(axis=0)
    parts_got = lax.ppermute(parts, "zh", swap_pairs(ZH, 1))

    share = rank // DP
    grads, proj_out = block_grads(tenant_index, parts, parts_got, inputs, cols)
    got = exchange(grads, "dp")

    from_x = {0: mine}
    for offset in (1, 3, 2):
        from_x[offset] = lax.ppermute(mine, "x", shift_pairs(X, offset))
    for offset in (1, 3):
        from_x[offset], got = lax.optimization_barrier((from_x[offset], got))
    groups, where, swapped = [], [], []
    for offsets in GROUPS:
        pieces = []
        for offset in offsets:
            swapped.append(lax.ppermute(from_x[offset], "core", swap_pairs(CORE, 1)))
            pieces += [from_x[offset], swapped[-1]]
            for c in (core, 1 - core):
                where += [((zh + z) % ZH * X + (x + X - offset) % X) * CORE + c for z in range(ZH)]
        keep, send = base_product(weights, pieces)
        groups.append([keep, lax.ppermute(send, "kh", swap_pairs(KH, 1))])
    where = jnp.stack(where).astype(jnp.int32)

    ids = got[:, -1, :nblocks].astype(jnp.int32)
    got = got[:, :-1].reshape(DP, 2, nblocks, share, in_width)
    place = (ids[None] == lax.broadcasted_iota(jnp.int32, (tenants, DP, nblocks), 0)).astype(F32)
    out = jnp.einsum("tgb,gabsd->atsd", place, got, precision=lax.Precision.HIGHEST, preferred_element_type=F32)

    input_gradient = join(where, proj_out, sel_down, groups).reshape(1, nrows, in_width)
    return input_gradient, out[0], out[1]


def solution(mesh):
    fine = Mesh(mesh.devices.reshape(ZH, X, CORE, DP, KH, KL), AXES)
    group = ("dp",) + TENANT
    return jax.shard_map(
        per_device,
        mesh=fine,
        in_specs=(
            P(group, TENSOR, None),
            P(group, None, TENSOR),
            P(TENSOR, group),
            P(TENANT, None, TENSOR),
            P(TENANT, None, TENSOR),
            P(group, None),
            P(group, None),
        ),
        out_specs=(P(group, None, TENSOR), P(TENANT, "dp", TENSOR), P(TENANT, "dp", TENSOR)),
        check_vma=False,
    )
```

time: 182 us -> 152 us (0.84)
  starting transfers between devices: 47.8 us -> 83.1 us
  blocking collectives: 32.4 us -> 0 us
  waiting for transfers between devices: 60.4 us -> 30.6 us
  Pallas kernels: 0 us -> 13.1 us
  matrix products: 12.6 us -> 2.9 us
  between operations: 17.7 us -> 14.4 us
  local copies, waits for them, and re-layouts: 6.36 us -> 3.53 us
    all_to_all x1 -> x0, blocking collectives: 32.4 us -> none  [per_device(): lax.all_to_all(sets, ('zh', 'tenant'), split_axis=0, concat_axis=0, tiled...]
    all_gather x2 -> x1, waiting for transfers between devices: 26.6 us -> 0.02 us  [per_device(): lax.all_gather(jnp.stack([weight, swapped]), 'dp', axis=0, tiled=False)]
    ppermute x9 -> x14, starting transfers between devices: 34.5 us -> 55.5 us  [the longest x4 14.9 us: per_device(): swapped.append(lax.ppermute(from_x[offset], 'core', swap_pairs(CORE, 1)))]
    all_to_all x2 -> x3, starting transfers between devices: 13.2 us -> 27.6 us  [exchange(): return lax.all_to_all(blocks, axes, split_axis=0, concat_axis=0, tiled=True)]
    pallas_call x0 -> x6, Pallas kernels: none -> 13.1 us  [the longest x2 7.56 us: base_product(): pl.pallas_call(functools.partial(base_kernel, count), out_shape=[jax.Shap...]
    dot_general x7 -> x0, matrix products: 11.4 us -> none  [the longest x1 5.3 us: per_device(): lax.dot_general(rows2d, w_other, dims, preferred_element_type=F32)]
    ppermute x9 -> x14, waiting for transfers between devices: 33.1 us -> 25.9 us  [the longest x2 12.7 us: per_device(): groups.append([keep, lax.ppermute(send, 'kh', swap_pairs(KH, 1))])]
    all_to_all x2 -> x3, waiting for transfers between devices: 0.01 us -> 4.67 us  [exchange(): return lax.all_to_all(blocks, axes, split_axis=0, concat_axis=0, tiled=True)]
  transfers between devices with their start and end apart: 13 -> 18, of which waited for: 9 -> 7; matrix products, arithmetic and copies ran while one was open for 8% -> 4% of each run, Pallas kernels for 0% -> 8%
where the time goes in v2:
time: 152 us; the launch traced here: 151 us
  starting transfers between devices  83.1 us (55%)
  waiting for transfers between devices  30.6 us (20%)
  between operations  14.4 us (9%)
  Pallas kernels  13.1 us (9%)
  local copies, waits for them, and re-layouts  3.53 us (2%)
  other arithmetic  3.07 us (2%)
  matrix products  2.9 us (2%)
    all_to_all x3, starting transfers between devices, exchange(): return lax.all_to_all(blocks, axes, split_axis=0, concat_axis=0, tiled=True)  27.6 us
    ppermute x4, starting transfers between devices, per_device(): swapped.append(lax.ppermute(from_x[offset], 'core', swap_pairs(CORE, 1)))  14.9 us
    ppermute x2, waiting for transfers between devices, per_device(): groups.append([keep, lax.ppermute(send, 'kh', swap_pairs(KH, 1))])  12.7 us
    ppermute x3, starting transfers between devices, per_device(): from_x[offset] = lax.ppermute(mine, 'x', shift_pairs(X, offset))  9.86 us
    pallas_call x2, Pallas kernels, base_product(): pl.pallas_call(functools.partial(base_kernel, count), out_shape=[jax.Shap...  7.56 us
    ppermute x1, starting transfers between devices, per_device(): from_both = lax.ppermute(other, ('zh', 'kh'), swap_pairs(ZH * KH, 3))  7.21 us
    ppermute x1, starting transfers between devices, per_device(): parts_got = lax.ppermute(parts, 'zh', swap_pairs(ZH, 1))  6.48 us
    ppermute x2, starting transfers between devices, per_device(): groups.append([keep, lax.ppermute(send, 'kh', swap_pairs(KH, 1))])  6.18 us
  transfers between devices with their start and end apart: 18, of which 7 were waited for; matrix products, arithmetic and copies ran while one was open for 4% of the time, Pallas kernels for 8%

profile of v2, /device:TPU:1, one launch (start us, length us, event | category | flops | bytes accessed | tf_op | source)
XLA Modules:
  0.0 150.8 jit_solution(4436794046015186200)
XLA Ops:
  7.2 5.0 %collective-permute-start.4 = (bf16[512,256]{1,0:T(8,128)(2,1)}, bf16[512,256]{1,0:T(8,128)(2,1)S(1)}, u32[]{:S(2)}, u32[]{:S(2)}) collective-permute-start(bf16[512,256]{1,0:T(8,128)(2,1)} %param.9), channel_id=1, source_target_pairs={{0,1},{1,0},{2,3},{3,2},{4,5},{5,4},{6,7},{7,6},{8,9},{9,8},{10,11... | collective-permute-start | bytes 786440 | tf_op jit(solution)/shard_map/ppermute | solution.py:231
  16.2 1.8 %pad_maximum_fusion.1 = bf16[2,512,256]{2,1,0:T(8,128)(2,1)} fusion(bf16[1,512,256]{2,1,0:T(8,128)(2,1)S(1)} %bitcast.71, bf16[1,512,256]{2,1,0:T(8,128)(2,1)} %bitcast.70), kind=kLoop, calls=%fused_computation.2 | loop fusion | flops 262144 | bytes 1048576 | tf_op jit(solution)/shard_map/stack | solution.py:232
  18.0 15.6 %all-to-all-start = ((bf16[16,24,512]{2,1,0:T(8,128)(2,1)}), bf16[16,24,512]{2,1,0:T(8,128)(2,1)S(1)}, u32[]{:S(2)}, u32[]{:S(2)}) async-start(bf16[16,24,512]{2,1,0:T(8,128)(2,1)} %get-tuple-element.19), calls=%async_computation | async-start | bytes 786432 | tf_op jit(solution)/shard_map/all_to_all | solution.py:20
  33.7 7.2 %collective-permute-start.2 = (bf16[2,24,2048]{2,1,0:T(8,128)(2,1)S(1)}, bf16[2,24,2048]{2,1,0:T(8,128)(2,1)S(1)}, u32[]{:S(2)}, u32[]{:S(2)}) collective-permute-start(bf16[2,24,2048]{2,1,0:T(8,128)(2,1)S(1)} %get-tuple-element.21), channel_id=1, source_target_pairs={{0,258},{2,256},{256,2},{258,0},{1,259},{3,257},{257,3},{259,1},{4... | collective-permute-start | bytes 589832 | tf_op jit(solution)/shard_map/ppermute | solution.py:235
  40.9 2.2 %collective-permute-start.1 = (bf16[2,24,2048]{2,1,0:T(8,128)(2,1)S(1)}, bf16[2,24,2048]{2,1,0:T(8,128)(2,1)}, u32[]{:S(2)}, u32[]{:S(2)}) collective-permute-start(bf16[2,24,2048]{2,1,0:T(8,128)(2,1)S(1)} %get-tuple-element.21), channel_id=1, source_target_pairs={{0,2},{2,0},{1,3},{3,1},{4,6},{6,4},{5,7},{7,5},{8,10},{10,8},{9,1... | collective-permute-start | bytes 589832 | tf_op jit(solution)/shard_map/ppermute | solution.py:236
  43.1 3.7 %collective-permute-start = (bf16[2,24,2048]{2,1,0:T(8,128)(2,1)S(1)}, bf16[2,24,2048]{2,1,0:T(8,128)(2,1)}, u32[]{:S(2)}, u32[]{:S(2)}) collective-permute-start(bf16[2,24,2048]{2,1,0:T(8,128)(2,1)S(1)} %get-tuple-element.20), channel_id=1, source_target_pairs={{0,256},{256,0},{1,257},{257,1},{2,258},{258,2},{3,259},{259,3},{4... | collective-permute-start | bytes 589832 | tf_op jit(solution)/shard_map/ppermute | solution.py:234
  50.5 5.2 %all-to-all-start.1 = ((f32[8,6,16,128]{3,2,1,0:T(8,128)}), f32[8,6,16,128]{3,2,1,0:T(8,128)S(1)}, u32[]{:S(2)}, u32[]{:S(2)}) async-start(f32[8,6,16,128]{3,2,1,0:T(8,128)} %rank_parts.1), calls=%async_computation.1 | async-start | bytes 786432 | tf_op jit(solution)/shard_map/all_to_all | solution.py:20
  57.3 5.4 %collective-permute-done.1 = bf16[2,24,2048]{2,1,0:T(8,128)(2,1)} collective-permute-done((bf16[2,24,2048]{2,1,0:T(8,128)(2,1)S(1)}, bf16[2,24,2048]{2,1,0:T(8,128)(2,1)}, u32[]{:S(2)}, u32[]{:S(2)}) %collective-permute-start.1) | collective-permute-done | bytes 196640 | tf_op jit(solution)/shard_map/ppermute | solution.py:236
  62.7 3.1 %collective-permute-done = bf16[2,24,2048]{2,1,0:T(8,128)(2,1)} collective-permute-done((bf16[2,24,2048]{2,1,0:T(8,128)(2,1)S(1)}, bf16[2,24,2048]{2,1,0:T(8,128)(2,1)}, u32[]{:S(2)}, u32[]{:S(2)}) %collective-permute-start) | collective-permute-done | bytes 196640 | tf_op jit(solution)/shard_map/ppermute | solution.py:234
  66.9 3.1 %collective-permute-start.6 = (bf16[4,2,24,2048]{3,2,1,0:T(8,128)(2,1)S(1)}, bf16[4,2,24,2048]{3,2,1,0:T(8,128)(2,1)}, u32[]{:S(2)}, u32[]{:S(2)}) collective-permute-start(bf16[4,2,24,2048]{3,2,1,0:T(8,128)(2,1)S(1)} %pad_maximum_fusion.refs_0_), channel_id=1, source_target_pairs={{0,64},{64,128},{128,192},{192,0},{1,65},{65,129},{129,193},{193,1... | collective-permute-start | bytes 2359304 | tf_op jit(solution)/shard_map/ppermute | solution.py:254
  70.0 3.4 %collective-permute-start.8 = (bf16[4,2,24,2048]{3,2,1,0:T(8,128)(2,1)S(1)}, bf16[4,2,24,2048]{3,2,1,0:T(8,128)(2,1)}, u32[]{:S(2)}, u32[]{:S(2)}) collective-permute-start(bf16[4,2,24,2048]{3,2,1,0:T(8,128)(2,1)S(1)} %pad_maximum_fusion.refs_0_), channel_id=1, source_target_pairs={{0,192},{64,0},{128,64},{192,128},{1,193},{65,1},{129,65},{193,129... | collective-permute-start | bytes 2359304 | tf_op jit(solution)/shard_map/ppermute | solution.py:254
  73.4 3.4 %collective-permute-start.11 = (bf16[4,2,24,2048]{3,2,1,0:T(8,128)(2,1)S(1)}, bf16[4,2,24,2048]{3,2,1,0:T(8,128)(2,1)S(1)}, u32[]{:S(2)}, u32[]{:S(2)}) collective-permute-start(bf16[4,2,24,2048]{3,2,1,0:T(8,128)(2,1)S(1)} %pad_maximum_fusion.refs_0_), channel_id=1, source_target_pairs={{0,128},{64,192},{128,0},{192,64},{1,129},{65,193},{129,1},{193,65... | collective-permute-start | bytes 2359304 | tf_op jit(solution)/shard_map/ppermute | solution.py:254
  76.8 6.5 %collective-permute-start.3 = (f32[6,16,128]{2,1,0:T(8,128)S(1)}, f32[6,16,128]{2,1,0:T(8,128)S(1)}, u32[]{:S(2)}, u32[]{:S(2)}) collective-permute-start(f32[6,16,128]{2,1,0:T(8,128)S(1)} %reduce_sum.9.own_ref), channel_id=1, source_target_pairs={{0,256},{256,0},{1,257},{257,1},{2,258},{258,2},{3,259},{259,3},{4... | collective-permute-start | bytes 147464 | tf_op jit(solution)/shard_map/ppermute | solution.py:246
  83.3 2.3 %collective-permute-done.3.got_ref = f32[6,16,128]{2,1,0:T(8,128)S(1)} collective-permute-done((f32[6,16,128]{2,1,0:T(8,128)S(1)}, f32[6,16,128]{2,1,0:T(8,128)S(1)}, u32[]{:S(2)}, u32[]{:S(2)}) %collective-permute-start.3) | collective-permute-done | bytes 49184 | tf_op jit(solution)/shard_map/ppermute | solution.py:246
  87.0 6.8 %all-to-all-start.2 = ((f32[8,13,512]{2,1,0:T(8,128)}), f32[8,13,512]{2,1,0:T(8,128)S(1)}, u32[]{:S(2)}, u32[]{:S(2)}) async-start(f32[8,13,512]{2,1,0:T(8,128)} %get-tuple-element.26), calls=%async_computation.2 | async-start | bytes 524288 | tf_op jit(solution)/shard_map/all_to_all | solution.py:20
  93.8 4.7 %collective-permute-start.5 = (bf16[4,2,24,2048]{3,2,1,0:T(8,128)(2,1)S(1)}, bf16[4,2,24,2048]{3,2,1,0:T(8,128)(2,1)}, u32[]{:S(2)}, u32[]{:S(2)}) collective-permute-start(bf16[4,2,24,2048]{3,2,1,0:T(8,128)(2,1)S(1)} %pad_maximum_fusion.refs_0_), channel_id=1, source_target_pairs={{0,32},{32,0},{1,33},{33,1},{2,34},{34,2},{3,35},{35,3},{4,36},{36... | collective-permute-start | bytes 2359304 | tf_op jit(solution)/shard_map/ppermute | solution.py:261
  98.6 4.7 %all-to-all-done.2 = f32[8,13,512]{2,1,0:T(8,128)S(1)} async-done(((f32[8,13,512]{2,1,0:T(8,128)}), f32[8,13,512]{2,1,0:T(8,128)S(1)}, u32[]{:S(2)}, u32[]{:S(2)}) %all-to-all-start.2) | async-done | bytes 213024 | tf_op jit(solution)/shard_map/all_to_all | solution.py:20
  103.2 5.8 %collective-permute-start.7 = (bf16[4,2,24,2048]{3,2,1,0:T(8,128)(2,1)}, bf16[4,2,24,2048]{3,2,1,0:T(8,128)(2,1)}, u32[]{:S(2)}, u32[]{:S(2)}) collective-permute-start(bf16[4,2,24,2048]{3,2,1,0:T(8,128)(2,1)} %collective-permute-done.6.refs_2_), channel_id=1, source_target_pairs={{0,32},{32,0},{1,33},{33,1},{2,34},{34,2},{3,35},{35,3},{4,36},{36... | collective-permute-start | bytes 2359304 | tf_op jit(solution)/shard_map/ppermute | solution.py:261
  109.1 1.9 %collective-permute-start.9 = (bf16[4,2,24,2048]{3,2,1,0:T(8,128)(2,1)}, bf16[4,2,24,2048]{3,2,1,0:T(8,128)(2,1)}, u32[]{:S(2)}, u32[]{:S(2)}) collective-permute-start(bf16[4,2,24,2048]{3,2,1,0:T(8,128)(2,1)} %collective-permute-done.8.refs_4_), channel_id=1, source_target_pairs={{0,32},{32,0},{1,33},{33,1},{2,34},{34,2},{3,35},{35,3},{4,36},{36... | collective-permute-start | bytes 2359304 | tf_op jit(solution)/shard_map/ppermute | solution.py:261
  111.0 2.4 %collective-permute-start.12 = (bf16[4,2,24,2048]{3,2,1,0:T(8,128)(2,1)S(1)}, bf16[4,2,24,2048]{3,2,1,0:T(8,128)(2,1)S(1)}, u32[]{:S(2)}, u32[]{:S(2)}) collective-permute-start(bf16[4,2,24,2048]{3,2,1,0:T(8,128)(2,1)S(1)} %collective-permute-done.11.refs_0_), channel_id=1, source_target_pairs={{0,32},{32,0},{1,33},{33,1},{2,34},{34,2},{3,35},{35,3},{4,36},{36... | collective-permute-start | bytes 2359304 | tf_op jit(solution)/shard_map/ppermute | solution.py:261
  114.3 6.1 %base_product.2 = (f32[12,24,512]{2,1,0:T(8,128)S(1)}, bf16[12,24,512]{2,1,0:T(8,128)(2,1)S(1)}) custom-call(bf16[8,2,512,256]{3,2,1,0:T(8,128)(2,1)} %bitcast.57, bf16[4,2,24,2048]{3,2,1,0:T(8,128)(2,1)S(1)} %pad_maximum_fusion.refs_0_, bf16[4,2,24,2048]{3,2,1,0:T(8,128)(2,1)} %collective-permute-done.5.refs_1_, ...), custom_call_target="tpu_custom_call" | custom-call | flops 2415919104 | bytes 9502720 | tf_op jit(solution)/shard_map/base_product/pallas_call | solution.py:96
  120.4 1.9 %collective-permute-start.10 = (bf16[12,24,512]{2,1,0:T(8,128)(2,1)S(1)}, bf16[12,24,512]{2,1,0:T(8,128)(2,1)S(1)}, u32[]{:S(2)}, u32[]{:S(2)}) collective-permute-start(bf16[12,24,512]{2,1,0:T(8,128)(2,1)S(1)} %get-tuple-element.31), channel_id=1, source_target_pairs={{0,2},{2,0},{1,3},{3,1},{4,6},{6,4},{5,7},{7,5},{8,10},{10,8},{9,1... | collective-permute-start | bytes 884744 | tf_op jit(solution)/shard_map/ppermute | solution.py:266
  123.8 4.3 %collective-permute-start.13 = (bf16[4,24,512]{2,1,0:T(8,128)(2,1)S(1)}, bf16[4,24,512]{2,1,0:T(8,128)(2,1)S(1)}, u32[]{:S(2)}, u32[]{:S(2)}) collective-permute-start(bf16[4,24,512]{2,1,0:T(8,128)(2,1)S(1)} %get-tuple-element.33), channel_id=1, source_target_pairs={{0,2},{2,0},{1,3},{3,1},{4,6},{6,4},{5,7},{7,5},{8,10},{10,8},{9,1... | collective-permute-start | bytes 294920 | tf_op jit(solution)/shard_map/ppermute | solution.py:266
  129.6 12.7 %collective-permute-done.13.refs_3_ = bf16[4,24,512]{2,1,0:T(8,128)(2,1)S(1)} collective-permute-done((bf16[4,24,512]{2,1,0:T(8,128)(2,1)S(1)}, bf16[4,24,512]{2,1,0:T(8,128)(2,1)S(1)}, u32[]{:S(2)}, u32[]{:S(2)}) %collective-permute-start.13) | collective-permute-done | bytes 98336 | tf_op jit(solution)/shard_map/ppermute | solution.py:266
  (47 shorter events, 17.4 us)
Async XLA Ops:
  7.2 39.6 %copy-start = (bf16[32,16,512]{2,1,0:T(8,128)(2,1)S(1)}, bf16[32,16,512]{2,1,0:T(8,128)(2,1)}, u32[]{:S(2)}) copy-start(bf16[32,16,512]{2,1,0:T(8,128)(2,1)} %param.10) | copy-start | bytes 1572868
  7.2 42.2 %copy-start.2 = (bf16[1,384,512]{2,1,0:T(8,128)(2,1)S(1)}, bf16[1,384,512]{2,1,0:T(8,128)(2,1)}, u32[]{:S(2)}) copy-start(bf16[1,384,512]{2,1,0:T(8,128)(2,1)} %param.8) | copy-start | bytes 1179652
  7.2 107.1 %all-gather.3.cloned.1.call-start = ((), (), s32[]{:S(2)}) async-start(), calls=%async_computation.3 | async-start | bytes 4718592 | tf_op jit(solution)/shard_map/all_gather | solution.py:232
  7.2 8.9 %collective-permute-start.4 = (bf16[512,256]{1,0:T(8,128)(2,1)}, bf16[512,256]{1,0:T(8,128)(2,1)S(1)}, u32[]{:S(2)}, u32[]{:S(2)}) collective-permute-start(bf16[512,256]{1,0:T(8,128)(2,1)} %param.9), channel_id=1, source_target_pairs={{0,1},{1,0},{2,3},{3,2},{4,5},{5,4},{6,7},{7,6},{8,9},{9,8},{10,11... | collective-permute-start | bytes 786440 | tf_op jit(solution)/shard_map/ppermute | solution.py:231
  12.3 1.0 copy-start.3
  13.3 0.7 copy-start.5
  14.0 71.6 %copy-start.4 = (s32[1,3]{1,0:T(1,128)S(1)}, s32[1,3]{1,0:T(1,128)}, u32[]{:S(2)}) copy-start(s32[1,3]{1,0:T(1,128)} %ids_ref.1) | copy-start | bytes 40
  18.0 31.4 %all-to-all-start = ((bf16[16,24,512]{2,1,0:T(8,128)(2,1)}), bf16[16,24,512]{2,1,0:T(8,128)(2,1)S(1)}, u32[]{:S(2)}, u32[]{:S(2)}) async-start(bf16[16,24,512]{2,1,0:T(8,128)(2,1)} %get-tuple-element.19), calls=%async_computation | async-start | bytes 786432 | tf_op jit(solution)/shard_map/all_to_all | solution.py:20
  33.7 23.7 %collective-permute-start.2 = (bf16[2,24,2048]{2,1,0:T(8,128)(2,1)S(1)}, bf16[2,24,2048]{2,1,0:T(8,128)(2,1)S(1)}, u32[]{:S(2)}, u32[]{:S(2)}) collective-permute-start(bf16[2,24,2048]{2,1,0:T(8,128)(2,1)S(1)} %get-tuple-element.21), channel_id=1, source_target_pairs={{0,258},{2,256},{256,2},{258,0},{1,259},{3,257},{257,3},{259,1},{4... | collective-permute-start | bytes 589832 | tf_op jit(solution)/shard_map/ppermute | solution.py:235
  40.9 21.8 %collective-permute-start.1 = (bf16[2,24,2048]{2,1,0:T(8,128)(2,1)S(1)}, bf16[2,24,2048]{2,1,0:T(8,128)(2,1)}, u32[]{:S(2)}, u32[]{:S(2)}) collective-permute-start(bf16[2,24,2048]{2,1,0:T(8,128)(2,1)S(1)} %get-tuple-element.21), channel_id=1, source_target_pairs={{0,2},{2,0},{1,3},{3,1},{4,6},{6,4},{5,7},{7,5},{8,10},{10,8},{9,1... | collective-permute-start | bytes 589832 | tf_op jit(solution)/shard_map/ppermute | solution.py:236
  43.1 22.7 %collective-permute-start = (bf16[2,24,2048]{2,1,0:T(8,128)(2,1)S(1)}, bf16[2,24,2048]{2,1,0:T(8,128)(2,1)}, u32[]{:S(2)}, u32[]{:S(2)}) collective-permute-start(bf16[2,24,2048]{2,1,0:T(8,128)(2,1)S(1)} %get-tuple-element.20), channel_id=1, source_target_pairs={{0,256},{256,0},{1,257},{257,1},{2,258},{258,2},{3,259},{259,3},{4... | collective-permute-start | bytes 589832 | tf_op jit(solution)/shard_map/ppermute | solution.py:234
  50.5 16.4 %all-to-all-start.1 = ((f32[8,6,16,128]{3,2,1,0:T(8,128)}), f32[8,6,16,128]{3,2,1,0:T(8,128)S(1)}, u32[]{:S(2)}, u32[]{:S(2)}) async-start(f32[8,6,16,128]{3,2,1,0:T(8,128)} %rank_parts.1), calls=%async_computation.1 | async-start | bytes 786432 | tf_op jit(solution)/shard_map/all_to_all | solution.py:20
  66.9 36.4 %collective-permute-start.6 = (bf16[4,2,24,2048]{3,2,1,0:T(8,128)(2,1)S(1)}, bf16[4,2,24,2048]{3,2,1,0:T(8,128)(2,1)}, u32[]{:S(2)}, u32[]{:S(2)}) collective-permute-start(bf16[4,2,24,2048]{3,2,1,0:T(8,128)(2,1)S(1)} %pad_maximum_fusion.refs_0_), channel_id=1, source_target_pairs={{0,64},{64,128},{128,192},{192,0},{1,65},{65,129},{129,193},{193,1... | collective-permute-start | bytes 2359304 | tf_op jit(solution)/shard_map/ppermute | solution.py:254
  70.0 39.1 %collective-permute-start.8 = (bf16[4,2,24,2048]{3,2,1,0:T(8,128)(2,1)S(1)}, bf16[4,2,24,2048]{3,2,1,0:T(8,128)(2,1)}, u32[]{:S(2)}, u32[]{:S(2)}) collective-permute-start(bf16[4,2,24,2048]{3,2,1,0:T(8,128)(2,1)S(1)} %pad_maximum_fusion.refs_0_), channel_id=1, source_target_pairs={{0,192},{64,0},{128,64},{192,128},{1,193},{65,1},{129,65},{193,129... | collective-permute-start | bytes 2359304 | tf_op jit(solution)/shard_map/ppermute | solution.py:254
  73.4 37.6 %collective-permute-start.11 = (bf16[4,2,24,2048]{3,2,1,0:T(8,128)(2,1)S(1)}, bf16[4,2,24,2048]{3,2,1,0:T(8,128)(2,1)S(1)}, u32[]{:S(2)}, u32[]{:S(2)}) collective-permute-start(bf16[4,2,24,2048]{3,2,1,0:T(8,128)(2,1)S(1)} %pad_maximum_fusion.refs_0_), channel_id=1, source_target_pairs={{0,128},{64,192},{128,0},{192,64},{1,129},{65,193},{129,1},{193,65... | collective-permute-start | bytes 2359304 | tf_op jit(solution)/shard_map/ppermute | solution.py:254
  76.8 8.7 %collective-permute-start.3 = (f32[6,16,128]{2,1,0:T(8,128)S(1)}, f32[6,16,128]{2,1,0:T(8,128)S(1)}, u32[]{:S(2)}, u32[]{:S(2)}) collective-permute-start(f32[6,16,128]{2,1,0:T(8,128)S(1)} %reduce_sum.9.own_ref), channel_id=1, source_target_pairs={{0,256},{256,0},{1,257},{257,1},{2,258},{258,2},{3,259},{259,3},{4... | collective-permute-start | bytes 147464 | tf_op jit(solution)/shard_map/ppermute | solution.py:246
  87.0 16.2 %all-to-all-start.2 = ((f32[8,13,512]{2,1,0:T(8,128)}), f32[8,13,512]{2,1,0:T(8,128)S(1)}, u32[]{:S(2)}, u32[]{:S(2)}) async-start(f32[8,13,512]{2,1,0:T(8,128)} %get-tuple-element.26), calls=%async_computation.2 | async-start | bytes 524288 | tf_op jit(solution)/shard_map/all_to_all | solution.py:20
  93.8 20.4 %collective-permute-start.5 = (bf16[4,2,24,2048]{3,2,1,0:T(8,128)(2,1)S(1)}, bf16[4,2,24,2048]{3,2,1,0:T(8,128)(2,1)}, u32[]{:S(2)}, u32[]{:S(2)}) collective-permute-start(bf16[4,2,24,2048]{3,2,1,0:T(8,128)(2,1)S(1)} %pad_maximum_fusion.refs_0_), channel_id=1, source_target_pairs={{0,32},{32,0},{1,33},{33,1},{2,34},{34,2},{3,35},{35,3},{4,36},{36... | collective-permute-start | bytes 2359304 | tf_op jit(solution)/shard_map/ppermute | solution.py:261
  103.2 11.0 %collective-permute-start.7 = (bf16[4,2,24,2048]{3,2,1,0:T(8,128)(2,1)}, bf16[4,2,24,2048]{3,2,1,0:T(8,128)(2,1)}, u32[]{:S(2)}, u32[]{:S(2)}) collective-permute-start(bf16[4,2,24,2048]{3,2,1,0:T(8,128)(2,1)} %collective-permute-done.6.refs_2_), channel_id=1, source_target_pairs={{0,32},{32,0},{1,33},{33,1},{2,34},{34,2},{3,35},{35,3},{4,36},{36... | collective-permute-start | bytes 2359304 | tf_op jit(solution)/shard_map/ppermute | solution.py:261
  109.1 5.2 %collective-permute-start.9 = (bf16[4,2,24,2048]{3,2,1,0:T(8,128)(2,1)}, bf16[4,2,24,2048]{3,2,1,0:T(8,128)(2,1)}, u32[]{:S(2)}, u32[]{:S(2)}) collective-permute-start(bf16[4,2,24,2048]{3,2,1,0:T(8,128)(2,1)} %collective-permute-done.8.refs_4_), channel_id=1, source_target_pairs={{0,32},{32,0},{1,33},{33,1},{2,34},{34,2},{3,35},{35,3},{4,36},{36... | collective-permute-start | bytes 2359304 | tf_op jit(solution)/shard_map/ppermute | solution.py:261
  111.0 11.3 %collective-permute-start.12 = (bf16[4,2,24,2048]{3,2,1,0:T(8,128)(2,1)S(1)}, bf16[4,2,24,2048]{3,2,1,0:T(8,128)(2,1)S(1)}, u32[]{:S(2)}, u32[]{:S(2)}) collective-permute-start(bf16[4,2,24,2048]{3,2,1,0:T(8,128)(2,1)S(1)} %collective-permute-done.11.refs_0_), channel_id=1, source_target_pairs={{0,32},{32,0},{1,33},{33,1},{2,34},{34,2},{3,35},{35,3},{4,36},{36... | collective-permute-start | bytes 2359304 | tf_op jit(solution)/shard_map/ppermute | solution.py:261
  114.3 8.0 %copy-start.1 = (bf16[16,512,256]{2,1,0:T(8,128)(2,1)S(1)}, bf16[16,512,256]{2,1,0:T(8,128)(2,1)}, u32[]{:S(2)}) copy-start(bf16[16,512,256]{2,1,0:T(8,128)(2,1)} %all-gather.3.cloned.1.call-done) | copy-start | bytes 12582916
  120.4 22.0 %collective-permute-start.10 = (bf16[12,24,512]{2,1,0:T(8,128)(2,1)S(1)}, bf16[12,24,512]{2,1,0:T(8,128)(2,1)S(1)}, u32[]{:S(2)}, u32[]{:S(2)}) collective-permute-start(bf16[12,24,512]{2,1,0:T(8,128)(2,1)S(1)} %get-tuple-element.31), channel_id=1, source_target_pairs={{0,2},{2,0},{1,3},{3,1},{4,6},{6,4},{5,7},{7,5},{8,10},{10,8},{9,1... | collective-permute-start | bytes 884744 | tf_op jit(solution)/shard_map/ppermute | solution.py:266
  123.8 18.5 %collective-permute-start.13 = (bf16[4,24,512]{2,1,0:T(8,128)(2,1)S(1)}, bf16[4,24,512]{2,1,0:T(8,128)(2,1)S(1)}, u32[]{:S(2)}, u32[]{:S(2)}) collective-permute-start(bf16[4,24,512]{2,1,0:T(8,128)(2,1)S(1)} %get-tuple-element.33), channel_id=1, source_target_pairs={{0,2},{2,0},{1,3},{3,1},{4,6},{6,4},{5,7},{7,5},{8,10},{10,8},{9,1... | collective-permute-start | bytes 294920 | tf_op jit(solution)/shard_map/ppermute | solution.py:266
Sparse Core Ops, SparseCore 0:
  18.1 63.9 all-gather.2

commit v3 on v2

--- a/solution.py
+++ b/solution.py
@@ -12,8 +12,8 @@
 TENSOR, TENANT = ("zh", "x", "core"), ("kh", "kl")
 AXES = TENSOR + ("dp",) + TENANT
 F32, BF16 = jnp.float32, jnp.bfloat16
-GROUPS = ((0, 1, 3), (2,))
-VMEM_LIMIT = 48 * 2**20
+OFFSETS = (0, 1, 3, 2)
+VMEM_LIMIT = 12 * 2**20
 
 
 def exchange(blocks, axes):
@@ -70,40 +70,44 @@
     )(at, live_count, dy)
 
 
-def base_kernel(count, w_ref, *refs):
-    pieces, keep_ref, send_ref = refs[:count], refs[count], refs[count + 1]
-    m = pieces[0].shape[2]
-    feats, chunk = w_ref.shape[2:]
-    total = None
+def base_kernel(core_ref, w_ref, *refs):
+    pieces, outs = refs[:-CORE], refs[-CORE:]
+    zs, _, m, depth = pieces[0].shape
+    chunk = w_ref.shape[3]
     for h in range(KL):
-        rows = [piece[:, h].reshape(KH * ZH * m, DP * chunk) for piece in pieces]
-        rows = jnp.concatenate(rows, axis=0)
-        for d in range(DP):
-            term = lax.dot_general(
-                rows[:, d * chunk : (d + 1) * chunk], w_ref[d, h], (((1,), (1,)), ((), ())), preferred_element_type=F32
-            )
-            total = term if total is None else total + term
-    total = total.reshape(count, KH, ZH, m, feats)
-    keep_ref[...] = total[:, 0].reshape(keep_ref.shape)
-    send_ref[...] = total[:, 1].reshape(send_ref.shape).astype(BF16)
-
-
-def base_product(weights, pieces):
-    count, m, feats = len(pieces), pieces[0].shape[2], weights.shape[2]
-    vmem = pl.BlockSpec(memory_space=pltpu.VMEM)
-    rows = count * ZH * KH * m
-    shape = (count * ZH, m, feats)
-    return pl.pallas_call(
-        functools.partial(base_kernel, count),
-        out_shape=[jax.ShapeDtypeStruct(shape, F32), jax.ShapeDtypeStruct(shape, BF16)],
-        in_specs=[vmem] * (1 + count),
-        out_specs=[vmem] * 2,
+        rows = jnp.concatenate([piece[:, h].reshape(zs * m, depth) for piece in pieces], axis=0)
+        if h == 0:
+            first = rows
+    for i, out in enumerate(outs):
+        at = lax.rem(core_ref[0] + i, CORE)
+        total = None
+        for h, rows_h in enumerate((first, rows)):
+            for d in range(DP):
+                term = lax.dot_general(
+                    rows_h[:, d * chunk : (d + 1) * chunk], w_ref[d, at, h], (((1,), (0,)), ((), ())), preferred_element_type=F32
+                )
+                total = term if total is None else total + term
+        out[...] = total.reshape(out.shape).astype(out.dtype)
+
+
+def base_product(core, weights, pieces, dtypes):
+    zs, _, m, _ = pieces[0].shape
+    count, feats = len(pieces) * zs, weights.shape[4]
+    vmem = pl.BlockSpec(memory_space=pltpu.VMEM)
+    smem = pl.BlockSpec(memory_space=pltpu.SMEM)
+    return pl.pallas_call(
+        base_kernel,
+        out_shape=[jax.ShapeDtypeStruct((count, m, feats), dtype) for dtype in dtypes],
+        in_specs=[smem, vmem] + [vmem] * len(pieces),
+        out_specs=[vmem] * CORE,
         cost_estimate=pl.CostEstimate(
-            flops=2 * rows * weights.size, bytes_accessed=2 * (count * pieces[0].size + weights.size + rows * feats), transcendentals=0
+            flops=2 * count * m * weights.size,
+            bytes_accessed=2 * (len(pieces) * pieces[0].size + weights.size + 2 * count * m * feats),
+            transcendentals=0,
         ),
-        compiler_params=pltpu.CompilerParams(vmem_limit_bytes=VMEM_LIMIT),
+        compiler_params=pltpu.CompilerParams(vmem_limit_bytes=2 * VMEM_LIMIT),
         name="base_product",
-    )(weights, *pieces)
+    )(core, weights, *pieces)
 
 
 def parts_kernel(down_ref, up_ref, in_ref, cols_ref, out_ref):
@@ -175,40 +179,30 @@
     )(tenant_index, own, got, inputs, cols)
 
 
-def join_kernel(nblocks, group_sizes, where_ref, proj_ref, down_ref, *refs):
-    adapter_ref, out_ref = refs[-1], refs[-2]
-    m = out_ref.shape[1]
-    terms = [
-        SCALE
-        * lax.dot_general(proj_ref[b], down_ref[b], (((0,), (0,)), ((), ())), preferred_element_type=F32)
-        for b in range(nblocks)
-    ]
+def join_kernel(nblocks, where_ref, proj_ref, down_ref, *refs):
+    *parts, out_ref, adapter_ref = refs
+    dims = (((0,), (0,)), ((), ()))
+    terms = [SCALE * lax.dot_general(proj_ref[b], down_ref[b], dims, preferred_element_type=F32) for b in range(nblocks)]
     adapter_ref[...] = jnp.concatenate(terms, axis=0).reshape(adapter_ref.shape)
-    at, place = 0, 0
-    for size in group_sizes:
-        keep, got = refs[at : at + 2]
-        at += 2
-        for p in range(size):
-            for z in range(ZH):
-                to = where_ref[place]
-                place += 1
-                total = keep[p * ZH + z] + got[p * ZH + z].astype(F32) + adapter_ref[to]
-                out_ref[to] = total.astype(BF16)
-
-
-def join(where, proj_out, sel_down, groups):
-    m, feats = groups[0][0].shape[1:]
-    blocks = ZH * X * CORE
-    vmem = pl.BlockSpec(memory_space=pltpu.VMEM)
-    smem = pl.BlockSpec(memory_space=pltpu.SMEM)
-    parts = [part for group in groups for part in group]
-    return pl.pallas_call(
-        functools.partial(join_kernel, proj_out.shape[0], [group[0].shape[0] // ZH for group in groups]),
-        out_shape=jax.ShapeDtypeStruct((blocks, m, feats), BF16),
+    for c in range(CORE):
+        keep, got = parts[2 * c : 2 * c + 2]
+        for p in range(keep.shape[0]):
+            to = where_ref[c * keep.shape[0] + p]
+            out_ref[to] = (keep[p].astype(F32) + got[p].astype(F32) + adapter_ref[to]).astype(BF16)
+
+
+def join(where, proj_out, sel_down, parts):
+    count, m, feats = parts[0].shape
+    shape = (CORE * count, m, feats)
+    vmem = pl.BlockSpec(memory_space=pltpu.VMEM)
+    smem = pl.BlockSpec(memory_space=pltpu.SMEM)
+    return pl.pallas_call(
+        functools.partial(join_kernel, proj_out.shape[0]),
+        out_shape=jax.ShapeDtypeStruct(shape, BF16),
         in_specs=[smem] + [vmem] * (2 + len(parts)),
         out_specs=vmem,
-        scratch_shapes=[pltpu.VMEM((blocks, m, feats), F32)],
-        cost_estimate=pl.CostEstimate(flops=0, bytes_accessed=10 * blocks * m * feats, transcendentals=0),
+        scratch_shapes=[pltpu.VMEM(shape, F32)],
+        cost_estimate=pl.CostEstimate(flops=0, bytes_accessed=20 * count * m * feats, transcendentals=0),
         compiler_params=pltpu.CompilerParams(vmem_limit_bytes=VMEM_LIMIT),
         name="join_rows",
     )(where, proj_out, sel_down, *parts)
@@ -229,41 +223,44 @@
     same, other, cols = split_rows(dy, at, live_count, nblocks, block)
 
     swapped, _ = lax.optimization_barrier((lax.ppermute(weight, "kl", swap_pairs(KL, 1)), same))
-    weights = lax.all_gather(jnp.stack([weight, swapped]), "dp", axis=0, tiled=False)
+    weights = lax.all_gather(jnp.stack([weight.T, swapped.T]), ("dp", "core"), axis=0, tiled=False)
+    weights = weights.reshape((DP, CORE, KL) + weight.T.shape)
 
     from_zh = lax.ppermute(same, "zh", swap_pairs(ZH, 1))
     from_both = lax.ppermute(other, ("zh", "kh"), swap_pairs(ZH * KH, 3))
     from_kh = lax.ppermute(other, "kh", swap_pairs(KH, 1))
-    mine = jnp.stack([same, from_zh, from_kh, from_both])
+    away, home = jnp.stack([from_kh, from_both]), jnp.stack([same, from_zh])
     hot = tenant_index[0][:, None] == lax.broadcasted_iota(jnp.int32, (nblocks, tenants), 1)
     hot = hot.astype(BF16)
     sel_down = jnp.einsum("bt,trd->brd", hot, down, preferred_element_type=F32).astype(BF16)
     sel_up = jnp.einsum("bt,trd->brd", hot, up, preferred_element_type=F32).astype(BF16)
-    cols = exchange(cols, TENSOR).reshape(nrows, -1)
-    parts = exchange(rank_parts(sel_down, sel_up, inputs, cols), ("x", "core"))
-    parts, mine = lax.optimization_barrier((parts, mine))
+    cols = exchange(cols, TENSOR)
+    cols = cols.reshape(nrows, -1)
+    parts = rank_parts(sel_down, sel_up, inputs, cols)
+    parts = exchange(parts, ("x", "core"))
+    parts, away, home = lax.optimization_barrier((parts, away, home))
     parts = parts.sum(axis=0)
     parts_got = lax.ppermute(parts, "zh", swap_pairs(ZH, 1))
 
     share = rank // DP
     grads, proj_out = block_grads(tenant_index, parts, parts_got, inputs, cols)
+
+    away = [lax.ppermute(away, "x", shift_pairs(X, offset)) if offset else away for offset in OFFSETS]
+    home = [lax.ppermute(home, "x", shift_pairs(X, offset)) if offset else home for offset in OFFSETS]
+    away, grads = lax.optimization_barrier((away, grads))
+    core_at = core[None].astype(jnp.int32)
+    send, send_other = base_product(core_at, weights, away, (BF16, BF16))
+    sums = lax.ppermute(send, "kh", swap_pairs(KH, 1))
+    sums_other = lax.ppermute(send_other, ("core", "kh"), swap_pairs(CORE * KH, 3))
+    grads, send = lax.optimization_barrier((grads, send))
     got = exchange(grads, "dp")
-
-    from_x = {0: mine}
-    for offset in (1, 3, 2):
-        from_x[offset] = lax.ppermute(mine, "x", shift_pairs(X, offset))
-    for offset in (1, 3):
-        from_x[offset], got = lax.optimization_barrier((from_x[offset], got))
-    groups, where, swapped = [], [], []
-    for offsets in GROUPS:
-        pieces = []
-        for offset in offsets:
-            swapped.append(lax.ppermute(from_x[offset], "core", swap_pairs(CORE, 1)))
-            pieces += [from_x[offset], swapped[-1]]
-            for c in (core, 1 - core):
-                where += [((zh + z) % ZH * X + (x + X - offset) % X) * CORE + c for z in range(ZH)]
-        keep, send = base_product(weights, pieces)
-        groups.append([keep, lax.ppermute(send, "kh", swap_pairs(KH, 1))])
+    home, send, got = lax.optimization_barrier((home, send, got))
+    keep, keep_other = base_product(core_at, weights, home, (F32, BF16))
+    keep_other = lax.ppermute(keep_other, "core", swap_pairs(CORE, 1))
+    where = [
+        ((zh + z) % ZH * X + (x + X - offset) % X) * CORE + c
+        for c in (core, 1 - core) for offset in OFFSETS for z in range(ZH)
+    ]
     where = jnp.stack(where).astype(jnp.int32)
 
     ids = got[:, -1, :nblocks].astype(jnp.int32)
@@ -271,7 +268,7 @@
     place = (ids[None] == lax.broadcasted_iota(jnp.int32, (tenants, DP, nblocks), 0)).astype(F32)
     out = jnp.einsum("tgb,gabsd->atsd", place, got, precision=lax.Precision.HIGHEST, preferred_element_type=F32)
 
-    input_gradient = join(where, proj_out, sel_down, groups).reshape(1, nrows, in_width)
+    input_gradient = join(where, proj_out, sel_down, (keep, sums, keep_other, sums_other)).reshape(1, nrows, in_width)
     return input_gradient, out[0], out[1]
 
 

time: 152 us -> 139 us (0.914)
  waiting for transfers between devices: 30.6 us -> 12.1 us
  local copies, waits for them, and re-layouts: 3.53 us -> 13.1 us
  Pallas kernels: 13.1 us -> 10.9 us
  other arithmetic: 3.07 us -> 1.09 us
    ppermute x9, waiting for transfers between devices: 12.7 us -> 1.23 us  [the longest x1 1.21 us: per_device(): lax.ppermute(send_other, ('core', 'kh'), swap_pairs(CORE * KH, 3))]
    unnamed x14 -> x21, local copies, waits for them, and re-layouts: 3.19 us -> 12.8 us
    ppermute x1, starting transfers between devices: 7.21 us -> 1.92 us  [per_device(): from_both = lax.ppermute(other, ('zh', 'kh'), swap_pairs(ZH * KH, 3))]
    all_to_all x3, waiting for transfers between devices: 4.67 us -> 0.33 us  [exchange(): return lax.all_to_all(blocks, axes, split_axis=0, concat_axis=0, tiled=True)]
    ppermute x1, starting transfers between devices: 3.74 us -> 7.19 us  [per_device(): from_zh = lax.ppermute(same, 'zh', swap_pairs(ZH, 1))]
    ppermute x1, waiting for transfers between devices: 3.05 us -> 0.01 us  [per_device(): from_zh = lax.ppermute(same, 'zh', swap_pairs(ZH, 1))]
    ppermute x1, waiting for transfers between devices: 5.36 us -> 7.66 us  [per_device(): from_kh = lax.ppermute(other, 'kh', swap_pairs(KH, 1))]
    pallas_call x3, Pallas kernels: 9.22 us -> 7 us  [the longest x2 5.35 us: base_product(): pl.pallas_call(base_kernel, out_shape=[jax.ShapeDtypeStruct((count, m, fe...]
  transfers between devices with their start and end apart: 18 -> 18, of which waited for: 7 -> 5; matrix products, arithmetic and copies ran while one was open for 4% -> 4% of each run, Pallas kernels for 8% -> 7%
where the time goes in v3:
time: 139 us; the launch traced here: 138 us
  starting transfers between devices  83 us (60%)
  between operations  14.4 us (10%)
  local copies, waits for them, and re-layouts  13.1 us (9%)
  waiting for transfers between devices  12.1 us (9%)
  Pallas kernels  10.9 us (8%)
  matrix products  2.89 us (2%)
    all_to_all x3, starting transfers between devices, exchange(): return lax.all_to_all(blocks, axes, split_axis=0, concat_axis=0, tiled=True)  27.6 us
    unnamed x21, local copies, waits for them, and re-layouts  12.8 us
    ppermute x3, starting transfers between devices, per_device(): lax.ppermute(away, 'x', shift_pairs(X, offset))  10.7 us
    ppermute x1, waiting for transfers between devices, per_device(): from_kh = lax.ppermute(other, 'kh', swap_pairs(KH, 1))  7.66 us
    ppermute x1, starting transfers between devices, per_device(): from_zh = lax.ppermute(same, 'zh', swap_pairs(ZH, 1))  7.19 us
    ppermute x3, starting transfers between devices, per_device(): lax.ppermute(home, 'x', shift_pairs(X, offset))  6.58 us
    ppermute x1, starting transfers between devices, per_device(): sums = lax.ppermute(send, 'kh', swap_pairs(KH, 1))  6.2 us
    pallas_call x2, Pallas kernels, base_product(): pl.pallas_call(base_kernel, out_shape=[jax.ShapeDtypeStruct((count, m, fe...  5.35 us
  transfers between devices with their start and end apart: 18, of which 5 were waited for; matrix products, arithmetic and copies ran while one was open for 4% of the time, Pallas kernels for 7%

profile of v3, /device:TPU:1, one launch (start us, length us, event | category | flops | bytes accessed | tf_op | source)
XLA Modules:
  0.0 137.5 jit_solution(6755937788478034577)
XLA Ops:
  8.4 4.8 %collective-permute-start.4 = (bf16[512,256]{0,1:T(8,128)(2,1)S(1)}, bf16[512,256]{0,1:T(8,128)(2,1)S(1)}, u32[]{:S(2)}, u32[]{:S(2)}) collective-permute-start(bf16[512,256]{0,1:T(8,128)(2,1)S(1)} %copy.44), channel_id=1, source_target_pairs={{0,1},{1,0},{2,3},{3,2},{4,5},{5,4},{6,7},{7,6},{8,9},{9,8},{10,11... | collective-permute-start | bytes 786440 | tf_op jit(solution)/shard_map/ppermute | solution.py:225
  17.9 15.6 %all-to-all-start = ((bf16[16,24,512]{2,1,0:T(8,128)(2,1)}), bf16[16,24,512]{2,1,0:T(8,128)(2,1)S(1)}, u32[]{:S(2)}, u32[]{:S(2)}) async-start(bf16[16,24,512]{2,1,0:T(8,128)(2,1)} %get-tuple-element.27), calls=%async_computation | async-start | bytes 786432 | tf_op jit(solution)/shard_map/all_to_all | solution.py:20
  33.5 7.2 %collective-permute-start.2 = (bf16[2,24,2048]{2,1,0:T(8,128)(2,1)S(1)}, bf16[2,24,2048]{2,1,0:T(8,128)(2,1)S(1)}, u32[]{:S(2)}, u32[]{:S(2)}) collective-permute-start(bf16[2,24,2048]{2,1,0:T(8,128)(2,1)S(1)} %get-tuple-element.29), channel_id=1, source_target_pairs={{0,256},{256,0},{1,257},{257,1},{2,258},{258,2},{3,259},{259,3},{4... | collective-permute-start | bytes 589832 | tf_op jit(solution)/shard_map/ppermute | solution.py:229
  40.7 4.0 %collective-permute-start = (bf16[2,24,2048]{2,1,0:T(8,128)(2,1)S(1)}, bf16[2,24,2048]{2,1,0:T(8,128)(2,1)S(1)}, u32[]{:S(2)}, u32[]{:S(2)}) collective-permute-start(bf16[2,24,2048]{2,1,0:T(8,128)(2,1)S(1)} %get-tuple-element.28), channel_id=1, source_target_pairs={{0,2},{2,0},{1,3},{3,1},{4,6},{6,4},{5,7},{7,5},{8,10},{10,8},{9,1... | collective-permute-start | bytes 589832 | tf_op jit(solution)/shard_map/ppermute | solution.py:231
  44.8 1.9 %collective-permute-start.1 = (bf16[2,24,2048]{2,1,0:T(8,128)(2,1)S(1)}, bf16[2,24,2048]{2,1,0:T(8,128)(2,1)S(1)}, u32[]{:S(2)}, u32[]{:S(2)}) collective-permute-start(bf16[2,24,2048]{2,1,0:T(8,128)(2,1)S(1)} %get-tuple-element.28), channel_id=1, source_target_pairs={{0,258},{2,256},{256,2},{258,0},{1,259},{3,257},{257,3},{259,1},{4... | collective-permute-start | bytes 589832 | tf_op jit(solution)/shard_map/ppermute | solution.py:230
  51.3 5.2 %all-to-all-start.1 = ((f32[8,6,16,128]{3,2,1,0:T(8,128)}), f32[8,6,16,128]{3,2,1,0:T(8,128)S(1)}, u32[]{:S(2)}, u32[]{:S(2)}) async-start(f32[8,6,16,128]{3,2,1,0:T(8,128)} %rank_parts.1), calls=%async_computation.1 | async-start | bytes 786432 | tf_op jit(solution)/shard_map/all_to_all | solution.py:20
  56.6 7.7 %collective-permute-done = bf16[2,24,2048]{2,1,0:T(8,128)(2,1)S(1)} collective-permute-done((bf16[2,24,2048]{2,1,0:T(8,128)(2,1)S(1)}, bf16[2,24,2048]{2,1,0:T(8,128)(2,1)S(1)}, u32[]{:S(2)}, u32[]{:S(2)}) %collective-permute-start) | collective-permute-done | bytes 196640 | tf_op jit(solution)/shard_map/ppermute | solution.py:231
  64.6 4.2 %collective-permute-start.10 = (bf16[2,2,24,2048]{3,2,1,0:T(8,128)(2,1)S(1)}, bf16[2,2,24,2048]{3,2,1,0:T(8,128)(2,1)S(1)}, u32[]{:S(2)}, u32[]{:S(2)}) collective-permute-start(bf16[2,2,24,2048]{3,2,1,0:T(8,128)(2,1)S(1)} %pad_maximum_fusion.1.refs_0_), channel_id=1, source_target_pairs={{0,128},{64,192},{128,0},{192,64},{1,129},{65,193},{129,1},{193,65... | collective-permute-start | bytes 1179656 | tf_op jit(solution)/shard_map/ppermute | solution.py:248
  68.8 2.2 %collective-permute-start.8 = (bf16[2,2,24,2048]{3,2,1,0:T(8,128)(2,1)S(1)}, bf16[2,2,24,2048]{3,2,1,0:T(8,128)(2,1)}, u32[]{:S(2)}, u32[]{:S(2)}) collective-permute-start(bf16[2,2,24,2048]{3,2,1,0:T(8,128)(2,1)S(1)} %pad_maximum_fusion.1.refs_0_), channel_id=1, source_target_pairs={{0,64},{64,128},{128,192},{192,0},{1,65},{65,129},{129,193},{193,1... | collective-permute-start | bytes 1179656 | tf_op jit(solution)/shard_map/ppermute | solution.py:248
  71.0 4.3 %collective-permute-start.9 = (bf16[2,2,24,2048]{3,2,1,0:T(8,128)(2,1)S(1)}, bf16[2,2,24,2048]{3,2,1,0:T(8,128)(2,1)}, u32[]{:S(2)}, u32[]{:S(2)}) collective-permute-start(bf16[2,2,24,2048]{3,2,1,0:T(8,128)(2,1)S(1)} %pad_maximum_fusion.1.refs_0_), channel_id=1, source_target_pairs={{0,192},{64,0},{128,64},{192,128},{1,193},{65,1},{129,65},{193,129... | collective-permute-start | bytes 1179656 | tf_op jit(solution)/shard_map/ppermute | solution.py:248
  75.4 4.6 %collective-permute-start.3 = (f32[6,16,128]{2,1,0:T(8,128)S(1)}, f32[6,16,128]{2,1,0:T(8,128)S(1)}, u32[]{:S(2)}, u32[]{:S(2)}) collective-permute-start(f32[6,16,128]{2,1,0:T(8,128)S(1)} %reduce_sum.9.own_ref), channel_id=1, source_target_pairs={{0,256},{256,0},{1,257},{257,1},{2,258},{258,2},{3,259},{259,3},{4... | collective-permute-start | bytes 147464 | tf_op jit(solution)/shard_map/ppermute | solution.py:243
  80.0 1.9 %collective-permute-start.5 = (bf16[2,2,24,2048]{3,2,1,0:T(8,128)(2,1)S(1)}, bf16[2,2,24,2048]{3,2,1,0:T(8,128)(2,1)S(1)}, u32[]{:S(2)}, u32[]{:S(2)}) collective-permute-start(bf16[2,2,24,2048]{3,2,1,0:T(8,128)(2,1)S(1)} %pad_maximum_fusion.2.refs_0_), channel_id=1, source_target_pairs={{0,64},{64,128},{128,192},{192,0},{1,65},{65,129},{129,193},{193,1... | collective-permute-start | bytes 1179656 | tf_op jit(solution)/shard_map/ppermute | solution.py:249
  81.9 2.2 %collective-permute-done.3.got_ref = f32[6,16,128]{2,1,0:T(8,128)S(1)} collective-permute-done((f32[6,16,128]{2,1,0:T(8,128)S(1)}, f32[6,16,128]{2,1,0:T(8,128)S(1)}, u32[]{:S(2)}, u32[]{:S(2)}) %collective-permute-start.3) | collective-permute-done | bytes 49184 | tf_op jit(solution)/shard_map/ppermute | solution.py:243
  84.1 2.4 %collective-permute-start.6 = (bf16[2,2,24,2048]{3,2,1,0:T(8,128)(2,1)S(1)}, bf16[2,2,24,2048]{3,2,1,0:T(8,128)(2,1)S(1)}, u32[]{:S(2)}, u32[]{:S(2)}) collective-permute-start(bf16[2,2,24,2048]{3,2,1,0:T(8,128)(2,1)S(1)} %pad_maximum_fusion.2.refs_0_), channel_id=1, source_target_pairs={{0,192},{64,0},{128,64},{192,128},{1,193},{65,1},{129,65},{193,129... | collective-permute-start | bytes 1179656 | tf_op jit(solution)/shard_map/ppermute | solution.py:249
  88.0 2.3 %collective-permute-start.7 = (bf16[2,2,24,2048]{3,2,1,0:T(8,128)(2,1)S(1)}, bf16[2,2,24,2048]{3,2,1,0:T(8,128)(2,1)S(1)}, u32[]{:S(2)}, u32[]{:S(2)}) collective-permute-start(bf16[2,2,24,2048]{3,2,1,0:T(8,128)(2,1)S(1)} %pad_maximum_fusion.2.refs_0_), channel_id=1, source_target_pairs={{0,128},{64,192},{128,0},{192,64},{1,129},{65,193},{129,1},{193,65... | collective-permute-start | bytes 1179656 | tf_op jit(solution)/shard_map/ppermute | solution.py:249
  90.4 3.4 %copy-done.1 = bf16[32,256,512]{2,1,0:T(8,128)(2,1)S(1)} copy-done((bf16[32,256,512]{2,1,0:T(8,128)(2,1)S(1)}, bf16[32,256,512]{2,1,0:T(8,128)(2,1)}, u32[]{:S(2)}) %copy-start.1) | copy-done | bytes 8388632
  93.7 3.5 %base_product.2 = (bf16[8,24,512]{2,1,0:T(8,128)(2,1)}, bf16[8,24,512]{2,1,0:T(8,128)(2,1)S(1)}) custom-call(s32[1]{0:T(128)} %bitcast.28.core_ref, bf16[8,2,2,256,512]{4,3,2,1,0:T(8,128)(2,1)S(1)} %bitcast.62, bf16[2,2,24,2048]{3,2,1,0:T(8,128)(2,1)S(1)} %pad_maximum_fusion.1.refs_0_, bf16[2,2,24,2048]{3,2,1,0:T(8,128)(2,1)} %collective-permute-done.8.refs_1_, ...), custom_call_target="tpu_custom_call" | custom-call | flops 1610612736 | bytes 10354688 | tf_op jit(solution)/shard_map/base_product/pallas_call | solution.py:98
  97.9 6.8 %all-to-all-start.2 = ((f32[8,13,512]{2,1,0:T(8,128)}), f32[8,13,512]{2,1,0:T(8,128)S(1)}, u32[]{:S(2)}, u32[]{:S(2)}) async-start(f32[8,13,512]{2,1,0:T(8,128)} %get-tuple-element.42), calls=%async_computation.2 | async-start | bytes 524288 | tf_op jit(solution)/shard_map/all_to_all | solution.py:20
  104.8 6.2 %collective-permute-start.11 = (bf16[8,24,512]{2,1,0:T(8,128)(2,1)}, bf16[8,24,512]{2,1,0:T(8,128)(2,1)S(1)}, u32[]{:S(2)}, u32[]{:S(2)}) collective-permute-start(bf16[8,24,512]{2,1,0:T(8,128)(2,1)} %get-tuple-element.41), channel_id=1, source_target_pairs={{0,2},{2,0},{1,3},{3,1},{4,6},{6,4},{5,7},{7,5},{8,10},{10,8},{9,1... | collective-permute-start | bytes 589832 | tf_op jit(solution)/shard_map/ppermute | solution.py:253
  111.0 5.1 %collective-permute-start.13 = (bf16[8,24,512]{2,1,0:T(8,128)(2,1)}, bf16[8,24,512]{2,1,0:T(8,128)(2,1)S(1)}, u32[]{:S(2)}, u32[]{:S(2)}) collective-permute-start(bf16[8,24,512]{2,1,0:T(8,128)(2,1)} %copy-done.8), channel_id=1, source_target_pairs={{0,34},{2,32},{32,2},{34,0},{1,35},{3,33},{33,3},{35,1},{4,38},{6,... | collective-permute-start | bytes 589832 | tf_op jit(solution)/shard_map/ppermute | solution.py:254
  116.4 3.4 %copy-done.2 = bf16[32,256,512]{2,1,0:T(8,128)(2,1)S(1)} copy-done((bf16[32,256,512]{2,1,0:T(8,128)(2,1)S(1)}, bf16[32,256,512]{2,1,0:T(8,128)(2,1)}, u32[]{:S(2)}) %copy-start.2) | copy-done | bytes 8388632
  119.7 1.9 %base_product.3 = (f32[8,24,512]{2,1,0:T(8,128)S(1)}, bf16[8,24,512]{2,1,0:T(8,128)(2,1)S(1)}) custom-call(s32[1]{0:T(128)} %bitcast.28.core_ref, bf16[8,2,2,256,512]{4,3,2,1,0:T(8,128)(2,1)S(1)} %bitcast.63, bf16[2,2,24,2048]{3,2,1,0:T(8,128)(2,1)S(1)} %pad_maximum_fusion.2.refs_0_, bf16[2,2,24,2048]{3,2,1,0:T(8,128)(2,1)S(1)} %collective-permute-done.5.refs_1_, ...), custom_call_target="tpu_custom_call" | custom-call | flops 1610612736 | bytes 10354688 | tf_op jit(solution)/shard_map/base_product/pallas_call | solution.py:98
  121.6 4.2 %collective-permute-start.12 = (bf16[8,24,512]{2,1,0:T(8,128)(2,1)S(1)}, bf16[8,24,512]{2,1,0:T(8,128)(2,1)S(1)}, u32[]{:S(2)}, u32[]{:S(2)}) collective-permute-start(bf16[8,24,512]{2,1,0:T(8,128)(2,1)S(1)} %get-tuple-element.48), channel_id=1, source_target_pairs={{0,32},{32,0},{1,33},{33,1},{2,34},{34,2},{3,35},{35,3},{4,36},{36... | collective-permute-start | bytes 589832 | tf_op jit(solution)/shard_map/ppermute | solution.py:259
  129.0 1.7 %join_rows.1 = bf16[16,24,512]{2,1,0:T(8,128)(2,1)} custom-call(s32[16]{0:T(128)S(1)} %stack.106.where_ref, bf16[3,16,128]{2,1,0:T(8,128)(2,1)S(1)} %get-tuple-element.31.proj_ref, bf16[3,16,512]{2,1,0:T(8,128)(2,1)S(1)} %copy.60.down_ref, f32[8,24,512]{2,1,0:T(8,128)S(1)} %get-tuple-element.47.refs_0_, ...), custom_call_target="tpu_custom_call" | custom-call | bytes 1966080 | tf_op jit(solution)/shard_map/join_rows/pallas_call | solution.py:199
  (55 shorter events, 16.5 us)
Async XLA Ops:
  7.2 39.5 %copy-start = (bf16[32,16,512]{2,1,0:T(8,128)(2,1)S(1)}, bf16[32,16,512]{2,1,0:T(8,128)(2,1)}, u32[]{:S(2)}) copy-start(bf16[32,16,512]{2,1,0:T(8,128)(2,1)} %param.10) | copy-start | bytes 1572868
  7.2 79.3 %copy-start.6 = (s32[1,3]{1,0:T(1,128)S(1)}, s32[1,3]{1,0:T(1,128)}, u32[]{:S(2)}) copy-start(s32[1,3]{1,0:T(1,128)} %ids_ref.1) | copy-start | bytes 40
  7.2 79.3 %copy-start.4 = (bf16[1,384,512]{2,1,0:T(8,128)(2,1)S(1)}, bf16[1,384,512]{2,1,0:T(8,128)(2,1)}, u32[]{:S(2)}) copy-start(bf16[1,384,512]{2,1,0:T(8,128)(2,1)} %param.8) | copy-start | bytes 1179652
  7.2 83.1 %all-gather.3.cloned.1.call-start = ((), (), s32[]{:S(2)}) async-start(), calls=%async_computation.3 | async-start | bytes 8912896 | tf_op jit(solution)/shard_map/all_gather | solution.py:226
  8.4 8.6 %collective-permute-start.4 = (bf16[512,256]{0,1:T(8,128)(2,1)S(1)}, bf16[512,256]{0,1:T(8,128)(2,1)S(1)}, u32[]{:S(2)}, u32[]{:S(2)}) collective-permute-start(bf16[512,256]{0,1:T(8,128)(2,1)S(1)} %copy.44), channel_id=1, source_target_pairs={{0,1},{1,0},{2,3},{3,2},{4,5},{5,4},{6,7},{7,6},{8,9},{9,8},{10,11... | collective-permute-start | bytes 786440 | tf_op jit(solution)/shard_map/ppermute | solution.py:225
  17.9 31.4 %all-to-all-start = ((bf16[16,24,512]{2,1,0:T(8,128)(2,1)}), bf16[16,24,512]{2,1,0:T(8,128)(2,1)S(1)}, u32[]{:S(2)}, u32[]{:S(2)}) async-start(bf16[16,24,512]{2,1,0:T(8,128)(2,1)} %get-tuple-element.27), calls=%async_computation | async-start | bytes 786432 | tf_op jit(solution)/shard_map/all_to_all | solution.py:20
  33.5 23.0 %collective-permute-start.2 = (bf16[2,24,2048]{2,1,0:T(8,128)(2,1)S(1)}, bf16[2,24,2048]{2,1,0:T(8,128)(2,1)S(1)}, u32[]{:S(2)}, u32[]{:S(2)}) collective-permute-start(bf16[2,24,2048]{2,1,0:T(8,128)(2,1)S(1)} %get-tuple-element.29), channel_id=1, source_target_pairs={{0,256},{256,0},{1,257},{257,1},{2,258},{258,2},{3,259},{259,3},{4... | collective-permute-start | bytes 589832 | tf_op jit(solution)/shard_map/ppermute | solution.py:229
  40.7 23.5 %collective-permute-start = (bf16[2,24,2048]{2,1,0:T(8,128)(2,1)S(1)}, bf16[2,24,2048]{2,1,0:T(8,128)(2,1)S(1)}, u32[]{:S(2)}, u32[]{:S(2)}) collective-permute-start(bf16[2,24,2048]{2,1,0:T(8,128)(2,1)S(1)} %get-tuple-element.28), channel_id=1, source_target_pairs={{0,2},{2,0},{1,3},{3,1},{4,6},{6,4},{5,7},{7,5},{8,10},{10,8},{9,1... | collective-permute-start | bytes 589832 | tf_op jit(solution)/shard_map/ppermute | solution.py:231
  44.8 19.5 %collective-permute-start.1 = (bf16[2,24,2048]{2,1,0:T(8,128)(2,1)S(1)}, bf16[2,24,2048]{2,1,0:T(8,128)(2,1)S(1)}, u32[]{:S(2)}, u32[]{:S(2)}) collective-permute-start(bf16[2,24,2048]{2,1,0:T(8,128)(2,1)S(1)} %get-tuple-element.28), channel_id=1, source_target_pairs={{0,258},{2,256},{256,2},{258,0},{1,259},{3,257},{257,3},{259,1},{4... | collective-permute-start | bytes 589832 | tf_op jit(solution)/shard_map/ppermute | solution.py:230
  49.3 1.0 copy-start.3
  51.3 13.2 %all-to-all-start.1 = ((f32[8,6,16,128]{3,2,1,0:T(8,128)}), f32[8,6,16,128]{3,2,1,0:T(8,128)S(1)}, u32[]{:S(2)}, u32[]{:S(2)}) async-start(f32[8,6,16,128]{3,2,1,0:T(8,128)} %rank_parts.1), calls=%async_computation.1 | async-start | bytes 786432 | tf_op jit(solution)/shard_map/all_to_all | solution.py:20
  64.6 23.4 %collective-permute-start.10 = (bf16[2,2,24,2048]{3,2,1,0:T(8,128)(2,1)S(1)}, bf16[2,2,24,2048]{3,2,1,0:T(8,128)(2,1)S(1)}, u32[]{:S(2)}, u32[]{:S(2)}) collective-permute-start(bf16[2,2,24,2048]{3,2,1,0:T(8,128)(2,1)S(1)} %pad_maximum_fusion.1.refs_0_), channel_id=1, source_target_pairs={{0,128},{64,192},{128,0},{192,64},{1,129},{65,193},{129,1},{193,65... | collective-permute-start | bytes 1179656 | tf_op jit(solution)/shard_map/ppermute | solution.py:248
  68.8 21.5 %collective-permute-start.8 = (bf16[2,2,24,2048]{3,2,1,0:T(8,128)(2,1)S(1)}, bf16[2,2,24,2048]{3,2,1,0:T(8,128)(2,1)}, u32[]{:S(2)}, u32[]{:S(2)}) collective-permute-start(bf16[2,2,24,2048]{3,2,1,0:T(8,128)(2,1)S(1)} %pad_maximum_fusion.1.refs_0_), channel_id=1, source_target_pairs={{0,64},{64,128},{128,192},{192,0},{1,65},{65,129},{129,193},{193,1... | collective-permute-start | bytes 1179656 | tf_op jit(solution)/shard_map/ppermute | solution.py:248
  71.0 19.3 %collective-permute-start.9 = (bf16[2,2,24,2048]{3,2,1,0:T(8,128)(2,1)S(1)}, bf16[2,2,24,2048]{3,2,1,0:T(8,128)(2,1)}, u32[]{:S(2)}, u32[]{:S(2)}) collective-permute-start(bf16[2,2,24,2048]{3,2,1,0:T(8,128)(2,1)S(1)} %pad_maximum_fusion.1.refs_0_), channel_id=1, source_target_pairs={{0,192},{64,0},{128,64},{192,128},{1,193},{65,1},{129,65},{193,129... | collective-permute-start | bytes 1179656 | tf_op jit(solution)/shard_map/ppermute | solution.py:248
  75.4 8.7 %collective-permute-start.3 = (f32[6,16,128]{2,1,0:T(8,128)S(1)}, f32[6,16,128]{2,1,0:T(8,128)S(1)}, u32[]{:S(2)}, u32[]{:S(2)}) collective-permute-start(f32[6,16,128]{2,1,0:T(8,128)S(1)} %reduce_sum.9.own_ref), channel_id=1, source_target_pairs={{0,256},{256,0},{1,257},{257,1},{2,258},{258,2},{3,259},{259,3},{4... | collective-permute-start | bytes 147464 | tf_op jit(solution)/shard_map/ppermute | solution.py:243
  80.0 36.1 %collective-permute-start.5 = (bf16[2,2,24,2048]{3,2,1,0:T(8,128)(2,1)S(1)}, bf16[2,2,24,2048]{3,2,1,0:T(8,128)(2,1)S(1)}, u32[]{:S(2)}, u32[]{:S(2)}) collective-permute-start(bf16[2,2,24,2048]{3,2,1,0:T(8,128)(2,1)S(1)} %pad_maximum_fusion.2.refs_0_), channel_id=1, source_target_pairs={{0,64},{64,128},{128,192},{192,0},{1,65},{65,129},{129,193},{193,1... | collective-permute-start | bytes 1179656 | tf_op jit(solution)/shard_map/ppermute | solution.py:249
  84.1 32.0 %collective-permute-start.6 = (bf16[2,2,24,2048]{3,2,1,0:T(8,128)(2,1)S(1)}, bf16[2,2,24,2048]{3,2,1,0:T(8,128)(2,1)S(1)}, u32[]{:S(2)}, u32[]{:S(2)}) collective-permute-start(bf16[2,2,24,2048]{3,2,1,0:T(8,128)(2,1)S(1)} %pad_maximum_fusion.2.refs_0_), channel_id=1, source_target_pairs={{0,192},{64,0},{128,64},{192,128},{1,193},{65,1},{129,65},{193,129... | collective-permute-start | bytes 1179656 | tf_op jit(solution)/shard_map/ppermute | solution.py:249
  88.0 28.1 %collective-permute-start.7 = (bf16[2,2,24,2048]{3,2,1,0:T(8,128)(2,1)S(1)}, bf16[2,2,24,2048]{3,2,1,0:T(8,128)(2,1)S(1)}, u32[]{:S(2)}, u32[]{:S(2)}) collective-permute-start(bf16[2,2,24,2048]{3,2,1,0:T(8,128)(2,1)S(1)} %pad_maximum_fusion.2.refs_0_), channel_id=1, source_target_pairs={{0,128},{64,192},{128,0},{192,64},{1,129},{65,193},{129,1},{193,65... | collective-permute-start | bytes 1179656 | tf_op jit(solution)/shard_map/ppermute | solution.py:249
  90.3 3.4 %copy-start.1 = (bf16[32,256,512]{2,1,0:T(8,128)(2,1)S(1)}, bf16[32,256,512]{2,1,0:T(8,128)(2,1)}, u32[]{:S(2)}) copy-start(bf16[32,256,512]{2,1,0:T(8,128)(2,1)} %all-gather.3.cloned.1.call-done) | copy-start | bytes 25165828
  97.9 18.3 %all-to-all-start.2 = ((f32[8,13,512]{2,1,0:T(8,128)}), f32[8,13,512]{2,1,0:T(8,128)S(1)}, u32[]{:S(2)}, u32[]{:S(2)}) async-start(f32[8,13,512]{2,1,0:T(8,128)} %get-tuple-element.42), calls=%async_computation.2 | async-start | bytes 524288 | tf_op jit(solution)/shard_map/all_to_all | solution.py:20
  104.8 23.0 %collective-permute-start.11 = (bf16[8,24,512]{2,1,0:T(8,128)(2,1)}, bf16[8,24,512]{2,1,0:T(8,128)(2,1)S(1)}, u32[]{:S(2)}, u32[]{:S(2)}) collective-permute-start(bf16[8,24,512]{2,1,0:T(8,128)(2,1)} %get-tuple-element.41), channel_id=1, source_target_pairs={{0,2},{2,0},{1,3},{3,1},{4,6},{6,4},{5,7},{7,5},{8,10},{10,8},{9,1... | collective-permute-start | bytes 589832 | tf_op jit(solution)/shard_map/ppermute | solution.py:253
  111.0 18.0 %collective-permute-start.13 = (bf16[8,24,512]{2,1,0:T(8,128)(2,1)}, bf16[8,24,512]{2,1,0:T(8,128)(2,1)S(1)}, u32[]{:S(2)}, u32[]{:S(2)}) collective-permute-start(bf16[8,24,512]{2,1,0:T(8,128)(2,1)} %copy-done.8), channel_id=1, source_target_pairs={{0,34},{2,32},{32,2},{34,0},{1,35},{3,33},{33,3},{35,1},{4,38},{6,... | collective-permute-start | bytes 589832 | tf_op jit(solution)/shard_map/ppermute | solution.py:254
  116.4 3.4 %copy-start.2 = (bf16[32,256,512]{2,1,0:T(8,128)(2,1)S(1)}, bf16[32,256,512]{2,1,0:T(8,128)(2,1)}, u32[]{:S(2)}) copy-start(bf16[32,256,512]{2,1,0:T(8,128)(2,1)} %all-gather.3.cloned.1.call-done) | copy-start | bytes 25165828
  121.6 7.4 %collective-permute-start.12 = (bf16[8,24,512]{2,1,0:T(8,128)(2,1)S(1)}, bf16[8,24,512]{2,1,0:T(8,128)(2,1)S(1)}, u32[]{:S(2)}, u32[]{:S(2)}) collective-permute-start(bf16[8,24,512]{2,1,0:T(8,128)(2,1)S(1)} %get-tuple-element.48), channel_id=1, source_target_pairs={{0,32},{32,0},{1,33},{33,1},{2,34},{34,2},{3,35},{35,3},{4,36},{36... | collective-permute-start | bytes 589832 | tf_op jit(solution)/shard_map/ppermute | solution.py:259
  (3 other events, 2.3 us)
Sparse Core Ops, SparseCore 0:
  18.0 65.4 all-gather.2

commit v4 on v3

--- a/solution.py
+++ b/solution.py
@@ -70,42 +70,65 @@
     )(at, live_count, dy)
 
 
+def turn_kernel(own_ref, got_ref, out_ref):
+    out_ref[0] = own_ref[...].T
+    out_ref[1] = got_ref[...].T
+
+
+def turned(own, got):
+    vmem = pl.BlockSpec(memory_space=pltpu.VMEM)
+    return pl.pallas_call(
+        turn_kernel,
+        out_shape=jax.ShapeDtypeStruct((KL,) + own.shape[::-1], own.dtype),
+        in_specs=[vmem, vmem],
+        out_specs=vmem,
+        cost_estimate=pl.CostEstimate(flops=0, bytes_accessed=8 * own.size, transcendentals=0),
+        compiler_params=pltpu.CompilerParams(vmem_limit_bytes=VMEM_LIMIT),
+        name="turned",
+    )(own, got)
+
+
 def base_kernel(core_ref, w_ref, *refs):
-    pieces, outs = refs[:-CORE], refs[-CORE:]
+    pieces, outs, held_ref, sems = refs[: -CORE - 2], refs[-CORE - 2 : -2], refs[-2], refs[-1]
+    copies = [pltpu.make_async_copy(w_ref.at[d], held_ref.at[d], sems.at[d]) for d in range(DP)]
+    for copy in copies:
+        copy.start()
+    if len(pieces[0].shape) > 4:
+        pieces = [pieces[0][i] for i in range(pieces[0].shape[0])]
     zs, _, m, depth = pieces[0].shape
     chunk = w_ref.shape[3]
-    for h in range(KL):
-        rows = jnp.concatenate([piece[:, h].reshape(zs * m, depth) for piece in pieces], axis=0)
-        if h == 0:
-            first = rows
-    for i, out in enumerate(outs):
-        at = lax.rem(core_ref[0] + i, CORE)
-        total = None
-        for h, rows_h in enumerate((first, rows)):
-            for d in range(DP):
+    rows = [jnp.concatenate([piece[:, h].reshape(zs * m, depth) for piece in pieces], axis=0) for h in range(KL)]
+    totals = [None] * CORE
+    for d, copy in enumerate(copies):
+        copy.wait()
+        for i in range(CORE):
+            at = lax.rem(core_ref[0] + i, CORE)
+            for h in range(KL):
                 term = lax.dot_general(
-                    rows_h[:, d * chunk : (d + 1) * chunk], w_ref[d, at, h], (((1,), (0,)), ((), ())), preferred_element_type=F32
+                    rows[h][:, d * chunk : (d + 1) * chunk], held_ref[d, at, h], (((1,), (0,)), ((), ())), preferred_element_type=F32
                 )
-                total = term if total is None else total + term
+                totals[i] = term if totals[i] is None else totals[i] + term
+    for out, total in zip(outs, totals):
         out[...] = total.reshape(out.shape).astype(out.dtype)
 
 
 def base_product(core, weights, pieces, dtypes):
-    zs, _, m, _ = pieces[0].shape
-    count, feats = len(pieces) * zs, weights.shape[4]
+    zs, _, m, _ = pieces[0].shape[-4:]
+    count, feats = X * zs, weights.shape[4]
     vmem = pl.BlockSpec(memory_space=pltpu.VMEM)
     smem = pl.BlockSpec(memory_space=pltpu.SMEM)
     return pl.pallas_call(
         base_kernel,
         out_shape=[jax.ShapeDtypeStruct((count, m, feats), dtype) for dtype in dtypes],
-        in_specs=[smem, vmem] + [vmem] * len(pieces),
+        in_specs=[smem, pl.BlockSpec(memory_space=pl.ANY)] + [vmem] * len(pieces),
         out_specs=[vmem] * CORE,
+        scratch_shapes=[pltpu.VMEM(weights.shape, weights.dtype), pltpu.SemaphoreType.DMA((DP,))],
         cost_estimate=pl.CostEstimate(
             flops=2 * count * m * weights.size,
-            bytes_accessed=2 * (len(pieces) * pieces[0].size + weights.size + 2 * count * m * feats),
+            bytes_accessed=2 * (sum(p.size for p in pieces) + weights.size + 2 * count * m * feats),
             transcendentals=0,
         ),
-        compiler_params=pltpu.CompilerParams(vmem_limit_bytes=2 * VMEM_LIMIT),
+        compiler_params=pltpu.CompilerParams(vmem_limit_bytes=4 * VMEM_LIMIT),
         name="base_product",
     )(core, weights, *pieces)
 
@@ -184,11 +207,16 @@
     dims = (((0,), (0,)), ((), ()))
     terms = [SCALE * lax.dot_general(proj_ref[b], down_ref[b], dims, preferred_element_type=F32) for b in range(nblocks)]
     adapter_ref[...] = jnp.concatenate(terms, axis=0).reshape(adapter_ref.shape)
+    count = parts[0].shape[0]
     for c in range(CORE):
-        keep, got = parts[2 * c : 2 * c + 2]
-        for p in range(keep.shape[0]):
-            to = where_ref[c * keep.shape[0] + p]
-            out_ref[to] = (keep[p].astype(F32) + got[p].astype(F32) + adapter_ref[to]).astype(BF16)
+        got = parts[2 * c + 1]
+        for p in range(count):
+            adapter_ref[where_ref[1, c * count + p]] += got[p].astype(F32)
+    for c in range(CORE):
+        keep = parts[2 * c]
+        for p in range(count):
+            to = where_ref[0, c * count + p]
+            out_ref[to] = (keep[p].astype(F32) + adapter_ref[to]).astype(BF16)
 
 
 def join(where, proj_out, sel_down, parts):
@@ -223,8 +251,8 @@
     same, other, cols = split_rows(dy, at, live_count, nblocks, block)
 
     swapped, _ = lax.optimization_barrier((lax.ppermute(weight, "kl", swap_pairs(KL, 1)), same))
-    weights = lax.all_gather(jnp.stack([weight.T, swapped.T]), ("dp", "core"), axis=0, tiled=False)
-    weights = weights.reshape((DP, CORE, KL) + weight.T.shape)
+    weights = lax.all_gather(turned(weight, swapped), ("dp", "core"), axis=0, tiled=False)
+    weights = weights.reshape((DP, CORE, KL) + weight.shape[::-1])
 
     from_zh = lax.ppermute(same, "zh", swap_pairs(ZH, 1))
     from_both = lax.ppermute(other, ("zh", "kh"), swap_pairs(ZH * KH, 3))
@@ -238,30 +266,32 @@
     cols = cols.reshape(nrows, -1)
     parts = rank_parts(sel_down, sel_up, inputs, cols)
     parts = exchange(parts, ("x", "core"))
+    away = jnp.broadcast_to(away[None], (X,) + away.shape)
     parts, away, home = lax.optimization_barrier((parts, away, home))
     parts = parts.sum(axis=0)
     parts_got = lax.ppermute(parts, "zh", swap_pairs(ZH, 1))
 
+    parts_got, weights = lax.optimization_barrier((parts_got, weights))
+
     share = rank // DP
     grads, proj_out = block_grads(tenant_index, parts, parts_got, inputs, cols)
 
-    away = [lax.ppermute(away, "x", shift_pairs(X, offset)) if offset else away for offset in OFFSETS]
+    away = exchange(away, "x")
     home = [lax.ppermute(home, "x", shift_pairs(X, offset)) if offset else home for offset in OFFSETS]
     away, grads = lax.optimization_barrier((away, grads))
     core_at = core[None].astype(jnp.int32)
-    send, send_other = base_product(core_at, weights, away, (BF16, BF16))
+    send, send_other = base_product(core_at, weights, [away], (BF16, BF16))
     sums = lax.ppermute(send, "kh", swap_pairs(KH, 1))
     sums_other = lax.ppermute(send_other, ("core", "kh"), swap_pairs(CORE * KH, 3))
-    grads, send = lax.optimization_barrier((grads, send))
     got = exchange(grads, "dp")
     home, send, got = lax.optimization_barrier((home, send, got))
     keep, keep_other = base_product(core_at, weights, home, (F32, BF16))
     keep_other = lax.ppermute(keep_other, "core", swap_pairs(CORE, 1))
     where = [
-        ((zh + z) % ZH * X + (x + X - offset) % X) * CORE + c
-        for c in (core, 1 - core) for offset in OFFSETS for z in range(ZH)
+        [((zh + z) % ZH * X + at) * CORE + c for c in (core, 1 - core) for at in order for z in range(ZH)]
+        for order in ([(x + X - offset) % X for offset in OFFSETS], range(X))
     ]
-    where = jnp.stack(where).astype(jnp.int32)
+    where = jnp.stack([jnp.stack(row) for row in where]).astype(jnp.int32)
 
     ids = got[:, -1, :nblocks].astype(jnp.int32)
     got = got[:, :-1].reshape(DP, 2, nblocks, share, in_width)

time: 139 us -> 136 us (0.978)
  local copies, waits for them, and re-layouts: 13.1 us -> 6.66 us
  waiting for transfers between devices: 12.1 us -> 17.6 us
  starting transfers between devices: 83 us -> 77.7 us
  Pallas kernels: 10.9 us -> 14.9 us
    ppermute x3 -> x0, starting transfers between devices: 10.7 us -> none  [per_device(): lax.ppermute(away, 'x', shift_pairs(X, offset))]
    unnamed x21 -> x18, local copies, waits for them, and re-layouts: 12.8 us -> 4.84 us
    ppermute x1, starting transfers between devices: 6.2 us -> 1.92 us  [per_device(): sums = lax.ppermute(send, 'kh', swap_pairs(KH, 1))]
    ppermute x1, waiting for transfers between devices: 0.01 us -> 4.21 us  [per_device(): sums = lax.ppermute(send, 'kh', swap_pairs(KH, 1))]
    all_to_all x3 -> x4, starting transfers between devices: 27.6 us -> 31.7 us  [exchange(): return lax.all_to_all(blocks, axes, split_axis=0, concat_axis=0, tiled=True)]
    ppermute x1, starting transfers between devices: 5.09 us -> 8.97 us  [per_device(): lax.ppermute(send_other, ('core', 'kh'), swap_pairs(CORE * KH, 3))]
    pallas_call x2, Pallas kernels: 5.35 us -> 8.94 us  [base_product(): pl.pallas_call(base_kernel, out_shape=[jax.ShapeDtypeStruct((count, m, fe...]
    ppermute x3, starting transfers between devices: 6.58 us -> 10.2 us  [per_device(): lax.ppermute(home, 'x', shift_pairs(X, offset))]
  transfers between devices with their start and end apart: 18 -> 16, of which waited for: 5 -> 5; matrix products, arithmetic and copies ran while one was open for 4% -> 5% of each run, Pallas kernels for 7% -> 9%
where the time goes in v4:
time: 136 us; the launch traced here: 135 us
  starting transfers between devices  77.7 us (57%)
  waiting for transfers between devices  17.6 us (13%)
  Pallas kernels  14.9 us (11%)
  between operations  14.4 us (11%)
  local copies, waits for them, and re-layouts  6.66 us (5%)
  matrix products  2.23 us (2%)
    all_to_all x4, starting transfers between devices, exchange(): return lax.all_to_all(blocks, axes, split_axis=0, concat_axis=0, tiled=True)  31.7 us
    ppermute x3, starting transfers between devices, per_device(): lax.ppermute(home, 'x', shift_pairs(X, offset))  10.2 us
    ppermute x1, waiting for transfers between devices, per_device(): from_kh = lax.ppermute(other, 'kh', swap_pairs(KH, 1))  9.3 us
    ppermute x1, starting transfers between devices, per_device(): lax.ppermute(send_other, ('core', 'kh'), swap_pairs(CORE * KH, 3))  8.97 us
    pallas_call x2, Pallas kernels, base_product(): pl.pallas_call(base_kernel, out_shape=[jax.ShapeDtypeStruct((count, m, fe...  8.94 us
    ppermute x1, starting transfers between devices, per_device(): from_zh = lax.ppermute(same, 'zh', swap_pairs(ZH, 1))  7.19 us
    ppermute x1, starting transfers between devices, per_device(): lax.ppermute(weight, 'kl', swap_pairs(KL, 1))  4.96 us
    unnamed x18, local copies, waits for them, and re-layouts  4.84 us
  transfers between devices with their start and end apart: 16, of which 5 were waited for; matrix products, arithmetic and copies ran while one was open for 5% of the time, Pallas kernels for 9%

profile of v4, /device:TPU:1, one launch (start us, length us, event | category | flops | bytes accessed | tf_op | source)
XLA Modules:
  0.0 134.7 jit_solution(11531129964771618504)
XLA Ops:
  7.2 5.0 %collective-permute-start.4 = (bf16[512,256]{1,0:T(8,128)(2,1)}, bf16[512,256]{1,0:T(8,128)(2,1)S(1)}, u32[]{:S(2)}, u32[]{:S(2)}) collective-permute-start(bf16[512,256]{1,0:T(8,128)(2,1)} %own_ref.1), channel_id=1, source_target_pairs={{0,1},{1,0},{2,3},{3,2},{4,5},{5,4},{6,7},{7,6},{8,9},{9,8},{10,11... | collective-permute-start | bytes 786440 | tf_op jit(solution)/shard_map/ppermute | solution.py:253
  14.0 1.4 %split_rows.1 = (bf16[2,24,2048]{2,1,0:T(8,128)(2,1)S(1)}, bf16[2,24,2048]{2,1,0:T(8,128)(2,1)S(1)}, bf16[16,24,512]{2,1,0:T(8,128)(2,1)}) custom-call(s32[3]{0:T(128)S(1)} %pad_add_fusion.1.at_ref, s32[1,3]{1,0:T(1,128)S(1)} %copy-done.6, bf16[24,8192]{1,0:T(8,128)(2,1)S(1)} %bitcast.78), custom_call_target="tpu_custom_call" | custom-call | bytes 1179648 | tf_op jit(solution)/shard_map/split_rows/pallas_call | solution.py:62
  18.2 15.8 %all-to-all-start = ((bf16[16,24,512]{2,1,0:T(8,128)(2,1)}), bf16[16,24,512]{2,1,0:T(8,128)(2,1)S(1)}, u32[]{:S(2)}, u32[]{:S(2)}) async-start(bf16[16,24,512]{2,1,0:T(8,128)(2,1)} %get-tuple-element.25), calls=%async_computation | async-start | bytes 786432 | tf_op jit(solution)/shard_map/all_to_all | solution.py:20
  33.9 7.2 %collective-permute-start.2 = (bf16[2,24,2048]{2,1,0:T(8,128)(2,1)S(1)}, bf16[2,24,2048]{2,1,0:T(8,128)(2,1)S(1)}, u32[]{:S(2)}, u32[]{:S(2)}) collective-permute-start(bf16[2,24,2048]{2,1,0:T(8,128)(2,1)S(1)} %get-tuple-element.27), channel_id=1, source_target_pairs={{0,256},{256,0},{1,257},{257,1},{2,258},{258,2},{3,259},{259,3},{4... | collective-permute-start | bytes 589832 | tf_op jit(solution)/shard_map/ppermute | solution.py:257
  41.1 4.0 %collective-permute-start = (bf16[2,24,2048]{2,1,0:T(8,128)(2,1)S(1)}, bf16[2,24,2048]{2,1,0:T(8,128)(2,1)S(1)}, u32[]{:S(2)}, u32[]{:S(2)}) collective-permute-start(bf16[2,24,2048]{2,1,0:T(8,128)(2,1)S(1)} %get-tuple-element.26), channel_id=1, source_target_pairs={{0,2},{2,0},{1,3},{3,1},{4,6},{6,4},{5,7},{7,5},{8,10},{10,8},{9,1... | collective-permute-start | bytes 589832 | tf_op jit(solution)/shard_map/ppermute | solution.py:259
  45.1 1.9 %collective-permute-start.1 = (bf16[2,24,2048]{2,1,0:T(8,128)(2,1)S(1)}, bf16[2,24,2048]{2,1,0:T(8,128)(2,1)S(1)}, u32[]{:S(2)}, u32[]{:S(2)}) collective-permute-start(bf16[2,24,2048]{2,1,0:T(8,128)(2,1)S(1)} %get-tuple-element.26), channel_id=1, source_target_pairs={{0,258},{2,256},{256,2},{258,0},{1,259},{3,257},{257,3},{259,1},{4... | collective-permute-start | bytes 589832 | tf_op jit(solution)/shard_map/ppermute | solution.py:258
  47.5 1.5 %fusion = bf16[3,16,512]{2,0,1:T(4,128)(2,1)S(1)} fusion(bf16[32,16,512]{2,1,0:T(8,128)(2,1)} %param.11, s32[3]{0:T(128)S(1)} %bitcast.81), kind=kOutput, calls=%fused_computation.1 | convolution fusion | flops 1572960 | bytes 573452 | tf_op jit(solution)/shard_map/bt,trd->brd/dot_general | solution.py:264
  50.1 5.2 %all-to-all-start.1 = ((f32[8,6,16,128]{3,2,1,0:T(8,128)}), f32[8,6,16,128]{3,2,1,0:T(8,128)S(1)}, u32[]{:S(2)}, u32[]{:S(2)}) async-start(f32[8,6,16,128]{3,2,1,0:T(8,128)} %rank_parts.1), calls=%async_computation.1 | async-start | bytes 786432 | tf_op jit(solution)/shard_map/all_to_all | solution.py:20
  55.3 9.3 %collective-permute-done = bf16[2,24,2048]{2,1,0:T(8,128)(2,1)S(1)} collective-permute-done((bf16[2,24,2048]{2,1,0:T(8,128)(2,1)S(1)}, bf16[2,24,2048]{2,1,0:T(8,128)(2,1)S(1)}, u32[]{:S(2)}, u32[]{:S(2)}) %collective-permute-start) | collective-permute-done | bytes 196640 | tf_op jit(solution)/shard_map/ppermute | solution.py:259
  64.7 1.4 %broadcast_in_dim.4 = bf16[4,2,2,24,2048]{4,3,2,1,0:T(8,128)(2,1)} broadcast(bf16[2,2,24,2048]{3,2,1,0:T(8,128)(2,1)S(1)} %pad_maximum_fusion), dimensions={1,2,3,4} | broadcast | bytes 1966080 | tf_op jit(solution)/shard_map/broadcast_in_dim | solution.py:269
  66.0 3.9 %all-to-all-start.2 = ((bf16[4,2,2,24,2048]{4,3,2,1,0:T(8,128)(2,1)}), bf16[4,2,2,24,2048]{4,3,2,1,0:T(8,128)(2,1)S(1)}, u32[]{:S(2)}, u32[]{:S(2)}) async-start(bf16[4,2,2,24,2048]{4,3,2,1,0:T(8,128)(2,1)} %broadcast_in_dim.4), calls=%async_computation.2 | async-start | bytes 3145728 | tf_op jit(solution)/shard_map/all_to_all | solution.py:20
  71.0 4.6 %collective-permute-start.3 = (f32[6,16,128]{2,1,0:T(8,128)S(1)}, f32[6,16,128]{2,1,0:T(8,128)S(1)}, u32[]{:S(2)}, u32[]{:S(2)}) collective-permute-start(f32[6,16,128]{2,1,0:T(8,128)S(1)} %reduce_sum.9.own_ref), channel_id=1, source_target_pairs={{0,256},{256,0},{1,257},{257,1},{2,258},{258,2},{3,259},{259,3},{4... | collective-permute-start | bytes 147464 | tf_op jit(solution)/shard_map/ppermute | solution.py:272
  75.6 3.4 %collective-permute-start.5 = (bf16[2,2,24,2048]{3,2,1,0:T(8,128)(2,1)S(1)}, bf16[2,2,24,2048]{3,2,1,0:T(8,128)(2,1)}, u32[]{:S(2)}, u32[]{:S(2)}) collective-permute-start(bf16[2,2,24,2048]{3,2,1,0:T(8,128)(2,1)S(1)} %pad_maximum_fusion.1.refs_0_), channel_id=1, source_target_pairs={{0,64},{64,128},{128,192},{192,0},{1,65},{65,129},{129,193},{193,1... | collective-permute-start | bytes 1179656 | tf_op jit(solution)/shard_map/ppermute | solution.py:280
  79.0 3.1 %collective-permute-start.6 = (bf16[2,2,24,2048]{3,2,1,0:T(8,128)(2,1)S(1)}, bf16[2,2,24,2048]{3,2,1,0:T(8,128)(2,1)}, u32[]{:S(2)}, u32[]{:S(2)}) collective-permute-start(bf16[2,2,24,2048]{3,2,1,0:T(8,128)(2,1)S(1)} %pad_maximum_fusion.1.refs_0_), channel_id=1, source_target_pairs={{0,192},{64,0},{128,64},{192,128},{1,193},{65,1},{129,65},{193,129... | collective-permute-start | bytes 1179656 | tf_op jit(solution)/shard_map/ppermute | solution.py:280
  82.1 3.7 %collective-permute-start.7 = (bf16[2,2,24,2048]{3,2,1,0:T(8,128)(2,1)S(1)}, bf16[2,2,24,2048]{3,2,1,0:T(8,128)(2,1)}, u32[]{:S(2)}, u32[]{:S(2)}) collective-permute-start(bf16[2,2,24,2048]{3,2,1,0:T(8,128)(2,1)S(1)} %pad_maximum_fusion.1.refs_0_), channel_id=1, source_target_pairs={{0,128},{64,192},{128,0},{192,64},{1,129},{65,193},{129,1},{193,65... | collective-permute-start | bytes 1179656 | tf_op jit(solution)/shard_map/ppermute | solution.py:280
  87.3 2.8 %all-to-all-done.2.refs_0_ = bf16[4,2,2,24,2048]{4,3,2,1,0:T(8,128)(2,1)S(1)} async-done(((bf16[4,2,2,24,2048]{4,3,2,1,0:T(8,128)(2,1)}), bf16[4,2,2,24,2048]{4,3,2,1,0:T(8,128)(2,1)S(1)}, u32[]{:S(2)}, u32[]{:S(2)}) %all-to-all-start.2) | async-done | bytes 1572896 | tf_op jit(solution)/shard_map/all_to_all | solution.py:20
  90.1 6.8 %all-to-all-start.3 = ((f32[8,13,512]{2,1,0:T(8,128)}), f32[8,13,512]{2,1,0:T(8,128)S(1)}, u32[]{:S(2)}, u32[]{:S(2)}) async-start(f32[8,13,512]{2,1,0:T(8,128)} %copy-done.3), calls=%async_computation.3 | async-start | bytes 524288 | tf_op jit(solution)/shard_map/all_to_all | solution.py:20
  97.2 3.9 %base_product.2 = (bf16[8,24,512]{2,1,0:T(8,128)(2,1)S(1)}, bf16[8,24,512]{2,1,0:T(8,128)(2,1)S(1)}) custom-call(s32[1]{0:T(128)} %bitcast.47.core_ref, bf16[8,2,2,256,512]{4,3,2,1,0:T(8,128)(2,1)} %bitcast.82, bf16[4,2,2,24,2048]{4,3,2,1,0:T(8,128)(2,1)S(1)} %all-to-all-done.2.refs_0_), custom_call_target="tpu_custom_call" | custom-call | flops 1610612736 | bytes 10354688 | tf_op jit(solution)/shard_map/base_product/pallas_call | solution.py:120
  101.0 9.0 %collective-permute-start.10 = (bf16[8,24,512]{2,1,0:T(8,128)(2,1)S(1)}, bf16[8,24,512]{2,1,0:T(8,128)(2,1)S(1)}, u32[]{:S(2)}, u32[]{:S(2)}) collective-permute-start(bf16[8,24,512]{2,1,0:T(8,128)(2,1)S(1)} %get-tuple-element.45), channel_id=1, source_target_pairs={{0,34},{2,32},{32,2},{34,0},{1,35},{3,33},{33,3},{35,1},{4,38},{6,... | collective-permute-start | bytes 589832 | tf_op jit(solution)/shard_map/ppermute | solution.py:285
  110.0 1.9 %collective-permute-start.8 = (bf16[8,24,512]{2,1,0:T(8,128)(2,1)S(1)}, bf16[8,24,512]{2,1,0:T(8,128)(2,1)S(1)}, u32[]{:S(2)}, u32[]{:S(2)}) collective-permute-start(bf16[8,24,512]{2,1,0:T(8,128)(2,1)S(1)} %get-tuple-element.37), channel_id=1, source_target_pairs={{0,2},{2,0},{1,3},{3,1},{4,6},{6,4},{5,7},{7,5},{8,10},{10,8},{9,1... | collective-permute-start | bytes 589832 | tf_op jit(solution)/shard_map/ppermute | solution.py:284
  112.2 5.1 %base_product.3 = (f32[8,24,512]{2,1,0:T(8,128)S(1)}, bf16[8,24,512]{2,1,0:T(8,128)(2,1)S(1)}) custom-call(s32[1]{0:T(128)} %bitcast.47.core_ref, bf16[8,2,2,256,512]{4,3,2,1,0:T(8,128)(2,1)} %bitcast.83, bf16[2,2,24,2048]{3,2,1,0:T(8,128)(2,1)S(1)} %pad_maximum_fusion.1.refs_0_, bf16[2,2,24,2048]{3,2,1,0:T(8,128)(2,1)} %collective-permute-done.5.refs_1_, ...), custom_call_target="tpu_custom_call" | custom-call | flops 1610612736 | bytes 10354688 | tf_op jit(solution)/shard_map/base_product/pallas_call | solution.py:120
  117.3 2.3 %collective-permute-start.9 = (bf16[8,24,512]{2,1,0:T(8,128)(2,1)S(1)}, bf16[8,24,512]{2,1,0:T(8,128)(2,1)S(1)}, u32[]{:S(2)}, u32[]{:S(2)}) collective-permute-start(bf16[8,24,512]{2,1,0:T(8,128)(2,1)S(1)} %get-tuple-element.44), channel_id=1, source_target_pairs={{0,32},{32,0},{1,33},{33,1},{2,34},{34,2},{3,35},{35,3},{4,36},{36... | collective-permute-start | bytes 589832 | tf_op jit(solution)/shard_map/ppermute | solution.py:289
  121.9 4.2 %collective-permute-done.8.refs_1_ = bf16[8,24,512]{2,1,0:T(8,128)(2,1)S(1)} collective-permute-done((bf16[8,24,512]{2,1,0:T(8,128)(2,1)S(1)}, bf16[8,24,512]{2,1,0:T(8,128)(2,1)S(1)}, u32[]{:S(2)}, u32[]{:S(2)}) %collective-permute-start.8) | collective-permute-done | bytes 196640 | tf_op jit(solution)/shard_map/ppermute | solution.py:284
  126.1 1.7 %join_rows.1 = bf16[16,24,512]{2,1,0:T(8,128)(2,1)} custom-call(s32[2,16]{1,0:T(2,128)S(1)} %pad_add_fusion.where_ref, bf16[3,16,128]{2,1,0:T(8,128)(2,1)S(1)} %get-tuple-element.31.proj_ref, bf16[3,16,512]{2,1,0:T(8,128)(2,1)S(1)} %copy.54.down_ref, f32[8,24,512]{2,1,0:T(8,128)S(1)} %get-tuple-element.43.refs_0_, ...), custom_call_target="tpu_custom_call" | custom-call | bytes 1966080 | tf_op jit(solution)/shard_map/join_rows/pallas_call | solution.py:227
  (51 shorter events, 11.4 us)
Async XLA Ops:
  7.2 39.9 %copy-start = (bf16[32,16,512]{2,1,0:T(8,128)(2,1)S(1)}, bf16[32,16,512]{2,1,0:T(8,128)(2,1)}, u32[]{:S(2)}) copy-start(bf16[32,16,512]{2,1,0:T(8,128)(2,1)} %param.10) | copy-start | bytes 1572868
  7.2 39.9 %copy-start.5 = (s32[1,3]{1,0:T(1,128)S(1)}, s32[1,3]{1,0:T(1,128)}, u32[]{:S(2)}) copy-start(s32[1,3]{1,0:T(1,128)} %ids_ref.1) | copy-start | bytes 40
  7.2 78.6 %all-gather.3.cloned.1.call-start = ((), (), s32[]{:S(2)}) async-start(), calls=%async_computation.4 | async-start | bytes 8912896 | tf_op jit(solution)/shard_map/all_gather | solution.py:254
  7.2 8.9 %collective-permute-start.4 = (bf16[512,256]{1,0:T(8,128)(2,1)}, bf16[512,256]{1,0:T(8,128)(2,1)S(1)}, u32[]{:S(2)}, u32[]{:S(2)}) collective-permute-start(bf16[512,256]{1,0:T(8,128)(2,1)} %own_ref.1), channel_id=1, source_target_pairs={{0,1},{1,0},{2,3},{3,2},{4,5},{5,4},{6,7},{7,6},{8,9},{9,8},{10,11... | collective-permute-start | bytes 786440 | tf_op jit(solution)/shard_map/ppermute | solution.py:253
  12.3 1.0 copy-start.2
  13.3 0.7 copy-start.6
  16.2 1.0 copy-start.4
  18.1 30.9 %copy-start.1 = (bf16[1,384,512]{2,1,0:T(8,128)(2,1)S(1)}, bf16[1,384,512]{2,1,0:T(8,128)(2,1)}, u32[]{:S(2)}) copy-start(bf16[1,384,512]{2,1,0:T(8,128)(2,1)} %param.8) | copy-start | bytes 1179652
  18.2 30.8 %all-to-all-start = ((bf16[16,24,512]{2,1,0:T(8,128)(2,1)}), bf16[16,24,512]{2,1,0:T(8,128)(2,1)S(1)}, u32[]{:S(2)}, u32[]{:S(2)}) async-start(bf16[16,24,512]{2,1,0:T(8,128)(2,1)} %get-tuple-element.25), calls=%async_computation | async-start | bytes 786432 | tf_op jit(solution)/shard_map/all_to_all | solution.py:20
  33.9 21.3 %collective-permute-start.2 = (bf16[2,24,2048]{2,1,0:T(8,128)(2,1)S(1)}, bf16[2,24,2048]{2,1,0:T(8,128)(2,1)S(1)}, u32[]{:S(2)}, u32[]{:S(2)}) collective-permute-start(bf16[2,24,2048]{2,1,0:T(8,128)(2,1)S(1)} %get-tuple-element.27), channel_id=1, source_target_pairs={{0,256},{256,0},{1,257},{257,1},{2,258},{258,2},{3,259},{259,3},{4... | collective-permute-start | bytes 589832 | tf_op jit(solution)/shard_map/ppermute | solution.py:257
  41.1 23.5 %collective-permute-start = (bf16[2,24,2048]{2,1,0:T(8,128)(2,1)S(1)}, bf16[2,24,2048]{2,1,0:T(8,128)(2,1)S(1)}, u32[]{:S(2)}, u32[]{:S(2)}) collective-permute-start(bf16[2,24,2048]{2,1,0:T(8,128)(2,1)S(1)} %get-tuple-element.26), channel_id=1, source_target_pairs={{0,2},{2,0},{1,3},{3,1},{4,6},{6,4},{5,7},{7,5},{8,10},{10,8},{9,1... | collective-permute-start | bytes 589832 | tf_op jit(solution)/shard_map/ppermute | solution.py:259
  45.1 19.5 %collective-permute-start.1 = (bf16[2,24,2048]{2,1,0:T(8,128)(2,1)S(1)}, bf16[2,24,2048]{2,1,0:T(8,128)(2,1)S(1)}, u32[]{:S(2)}, u32[]{:S(2)}) collective-permute-start(bf16[2,24,2048]{2,1,0:T(8,128)(2,1)S(1)} %get-tuple-element.26), channel_id=1, source_target_pairs={{0,258},{2,256},{256,2},{258,0},{1,259},{3,257},{257,3},{259,1},{4... | collective-permute-start | bytes 589832 | tf_op jit(solution)/shard_map/ppermute | solution.py:258
  50.1 14.6 %all-to-all-start.1 = ((f32[8,6,16,128]{3,2,1,0:T(8,128)}), f32[8,6,16,128]{3,2,1,0:T(8,128)S(1)}, u32[]{:S(2)}, u32[]{:S(2)}) async-start(f32[8,6,16,128]{3,2,1,0:T(8,128)} %rank_parts.1), calls=%async_computation.1 | async-start | bytes 786432 | tf_op jit(solution)/shard_map/all_to_all | solution.py:20
  64.6 1.4 %copy-start.7 = (f32[8,6,16,128]{3,2,1,0:T(8,128)}, f32[8,6,16,128]{3,2,1,0:T(8,128)S(1)}, u32[]{:S(2)}) copy-start(f32[8,6,16,128]{3,2,1,0:T(8,128)S(1)} %all-to-all-done.1) | copy-start | bytes 1179652
  66.0 24.1 %all-to-all-start.2 = ((bf16[4,2,2,24,2048]{4,3,2,1,0:T(8,128)(2,1)}), bf16[4,2,2,24,2048]{4,3,2,1,0:T(8,128)(2,1)S(1)}, u32[]{:S(2)}, u32[]{:S(2)}) async-start(bf16[4,2,2,24,2048]{4,3,2,1,0:T(8,128)(2,1)} %broadcast_in_dim.4), calls=%async_computation.2 | async-start | bytes 3145728 | tf_op jit(solution)/shard_map/all_to_all | solution.py:20
  71.0 14.8 %collective-permute-start.3 = (f32[6,16,128]{2,1,0:T(8,128)S(1)}, f32[6,16,128]{2,1,0:T(8,128)S(1)}, u32[]{:S(2)}, u32[]{:S(2)}) collective-permute-start(f32[6,16,128]{2,1,0:T(8,128)S(1)} %reduce_sum.9.own_ref), channel_id=1, source_target_pairs={{0,256},{256,0},{1,257},{257,1},{2,258},{258,2},{3,259},{259,3},{4... | collective-permute-start | bytes 147464 | tf_op jit(solution)/shard_map/ppermute | solution.py:272
  75.6 36.4 %collective-permute-start.5 = (bf16[2,2,24,2048]{3,2,1,0:T(8,128)(2,1)S(1)}, bf16[2,2,24,2048]{3,2,1,0:T(8,128)(2,1)}, u32[]{:S(2)}, u32[]{:S(2)}) collective-permute-start(bf16[2,2,24,2048]{3,2,1,0:T(8,128)(2,1)S(1)} %pad_maximum_fusion.1.refs_0_), channel_id=1, source_target_pairs={{0,64},{64,128},{128,192},{192,0},{1,65},{65,129},{129,193},{193,1... | collective-permute-start | bytes 1179656 | tf_op jit(solution)/shard_map/ppermute | solution.py:280
  79.0 33.0 %collective-permute-start.6 = (bf16[2,2,24,2048]{3,2,1,0:T(8,128)(2,1)S(1)}, bf16[2,2,24,2048]{3,2,1,0:T(8,128)(2,1)}, u32[]{:S(2)}, u32[]{:S(2)}) collective-permute-start(bf16[2,2,24,2048]{3,2,1,0:T(8,128)(2,1)S(1)} %pad_maximum_fusion.1.refs_0_), channel_id=1, source_target_pairs={{0,192},{64,0},{128,64},{192,128},{1,193},{65,1},{129,65},{193,129... | collective-permute-start | bytes 1179656 | tf_op jit(solution)/shard_map/ppermute | solution.py:280
  82.1 29.9 %collective-permute-start.7 = (bf16[2,2,24,2048]{3,2,1,0:T(8,128)(2,1)S(1)}, bf16[2,2,24,2048]{3,2,1,0:T(8,128)(2,1)}, u32[]{:S(2)}, u32[]{:S(2)}) collective-permute-start(bf16[2,2,24,2048]{3,2,1,0:T(8,128)(2,1)S(1)} %pad_maximum_fusion.1.refs_0_), channel_id=1, source_target_pairs={{0,128},{64,192},{128,0},{192,64},{1,129},{65,193},{129,1},{193,65... | collective-permute-start | bytes 1179656 | tf_op jit(solution)/shard_map/ppermute | solution.py:280
  86.6 0.7 copy-start.3
  90.1 21.8 %all-to-all-start.3 = ((f32[8,13,512]{2,1,0:T(8,128)}), f32[8,13,512]{2,1,0:T(8,128)S(1)}, u32[]{:S(2)}, u32[]{:S(2)}) async-start(f32[8,13,512]{2,1,0:T(8,128)} %copy-done.3), calls=%async_computation.3 | async-start | bytes 524288 | tf_op jit(solution)/shard_map/all_to_all | solution.py:20
  101.0 20.9 %collective-permute-start.10 = (bf16[8,24,512]{2,1,0:T(8,128)(2,1)S(1)}, bf16[8,24,512]{2,1,0:T(8,128)(2,1)S(1)}, u32[]{:S(2)}, u32[]{:S(2)}) collective-permute-start(bf16[8,24,512]{2,1,0:T(8,128)(2,1)S(1)} %get-tuple-element.45), channel_id=1, source_target_pairs={{0,34},{2,32},{32,2},{34,0},{1,35},{3,33},{33,3},{35,1},{4,38},{6,... | collective-permute-start | bytes 589832 | tf_op jit(solution)/shard_map/ppermute | solution.py:285
  110.0 16.1 %collective-permute-start.8 = (bf16[8,24,512]{2,1,0:T(8,128)(2,1)S(1)}, bf16[8,24,512]{2,1,0:T(8,128)(2,1)S(1)}, u32[]{:S(2)}, u32[]{:S(2)}) collective-permute-start(bf16[8,24,512]{2,1,0:T(8,128)(2,1)S(1)} %get-tuple-element.37), channel_id=1, source_target_pairs={{0,2},{2,0},{1,3},{3,1},{4,6},{6,4},{5,7},{7,5},{8,10},{10,8},{9,1... | collective-permute-start | bytes 589832 | tf_op jit(solution)/shard_map/ppermute | solution.py:284
  117.3 8.8 %collective-permute-start.9 = (bf16[8,24,512]{2,1,0:T(8,128)(2,1)S(1)}, bf16[8,24,512]{2,1,0:T(8,128)(2,1)S(1)}, u32[]{:S(2)}, u32[]{:S(2)}) collective-permute-start(bf16[8,24,512]{2,1,0:T(8,128)(2,1)S(1)} %get-tuple-element.44), channel_id=1, source_target_pairs={{0,32},{32,0},{1,33},{33,1},{2,34},{34,2},{3,35},{35,3},{4,36},{36... | collective-permute-start | bytes 589832 | tf_op jit(solution)/shard_map/ppermute | solution.py:289
Sparse Core Ops, SparseCore 0:
  18.3 65.4 all-gather.2

commit v5 on v4

--- a/solution.py
+++ b/solution.py
@@ -70,22 +70,26 @@
     )(at, live_count, dy)
 
 
-def turn_kernel(own_ref, got_ref, out_ref):
-    out_ref[0] = own_ref[...].T
+def turn_kernel(from_ref, to_ref):
+    to_ref[...] = from_ref[...].T
+
+
+def pair_kernel(own_ref, got_ref, out_ref):
+    out_ref[0] = own_ref[...]
     out_ref[1] = got_ref[...].T
 
 
-def turned(own, got):
-    vmem = pl.BlockSpec(memory_space=pltpu.VMEM)
-    return pl.pallas_call(
-        turn_kernel,
-        out_shape=jax.ShapeDtypeStruct((KL,) + own.shape[::-1], own.dtype),
-        in_specs=[vmem, vmem],
+def on_chip(kernel, name, shape, *operands):
+    vmem = pl.BlockSpec(memory_space=pltpu.VMEM)
+    return pl.pallas_call(
+        kernel,
+        out_shape=jax.ShapeDtypeStruct(shape, operands[0].dtype),
+        in_specs=[vmem] * len(operands),
         out_specs=vmem,
-        cost_estimate=pl.CostEstimate(flops=0, bytes_accessed=8 * own.size, transcendentals=0),
-        compiler_params=pltpu.CompilerParams(vmem_limit_bytes=VMEM_LIMIT),
-        name="turned",
-    )(own, got)
+        cost_estimate=pl.CostEstimate(flops=0, bytes_accessed=4 * sum(o.size for o in operands), transcendentals=0),
+        compiler_params=pltpu.CompilerParams(vmem_limit_bytes=VMEM_LIMIT),
+        name=name,
+    )(*operands)
 
 
 def base_kernel(core_ref, w_ref, *refs):
@@ -251,7 +255,9 @@
     same, other, cols = split_rows(dy, at, live_count, nblocks, block)
 
     swapped, _ = lax.optimization_barrier((lax.ppermute(weight, "kl", swap_pairs(KL, 1)), same))
-    weights = lax.all_gather(turned(weight, swapped), ("dp", "core"), axis=0, tiled=False)
+    turned = on_chip(turn_kernel, "turned", weight.shape[::-1], weight)
+    weights = on_chip(pair_kernel, "paired", (KL,) + turned.shape, turned, swapped)
+    weights = lax.all_gather(weights, ("dp", "core"), axis=0, tiled=False)
     weights = weights.reshape((DP, CORE, KL) + weight.shape[::-1])
 
     from_zh = lax.ppermute(same, "zh", swap_pairs(ZH, 1))

time: 136 us -> 135 us (level)
  transfers between devices with their start and end apart: 16 -> 16, of which waited for: 5 -> 4; matrix products, arithmetic and copies ran while one was open for 5% -> 5% of each run, Pallas kernels for 9% -> 9%
where the time goes in v5:
time: 135 us; the launch traced here: 134 us
  starting transfers between devices  77.5 us (57%)
  waiting for transfers between devices  16.8 us (12%)
  Pallas kernels  15 us (11%)
  between operations  14.4 us (11%)
  local copies, waits for them, and re-layouts  6.66 us (5%)
  matrix products  2.23 us (2%)
    all_to_all x4, starting transfers between devices, exchange(): return lax.all_to_all(blocks, axes, split_axis=0, concat_axis=0, tiled=True)  31.4 us
    ppermute x3, starting transfers between devices, per_device(): lax.ppermute(home, 'x', shift_pairs(X, offset))  10.2 us
    ppermute x1, waiting for transfers between devices, per_device(): from_kh = lax.ppermute(other, 'kh', swap_pairs(KH, 1))  9.3 us
    ppermute x1, starting transfers between devices, per_device(): lax.ppermute(send_other, ('core', 'kh'), swap_pairs(CORE * KH, 3))  8.97 us
    pallas_call x2, Pallas kernels, base_product(): pl.pallas_call(base_kernel, out_shape=[jax.ShapeDtypeStruct((count, m, fe...  8.94 us
    ppermute x1, starting transfers between devices, per_device(): from_zh = lax.ppermute(same, 'zh', swap_pairs(ZH, 1))  7.19 us
    ppermute x1, starting transfers between devices, per_device(): lax.ppermute(weight, 'kl', swap_pairs(KL, 1))  4.96 us
    unnamed x18, local copies, waits for them, and re-layouts  4.84 us
  transfers between devices with their start and end apart: 16, of which 4 were waited for; matrix products, arithmetic and copies ran while one was open for 5% of the time, Pallas kernels for 9%

profile of v5, /device:TPU:1, one launch (start us, length us, event | category | flops | bytes accessed | tf_op | source)
XLA Modules:
  0.0 133.7 jit_solution(8802333506331356099)
XLA Ops:
  7.2 5.0 %collective-permute-start.4 = (bf16[512,256]{1,0:T(8,128)(2,1)}, bf16[512,256]{1,0:T(8,128)(2,1)S(1)}, u32[]{:S(2)}, u32[]{:S(2)}) collective-permute-start(bf16[512,256]{1,0:T(8,128)(2,1)} %from_ref.1), channel_id=1, source_target_pairs={{0,1},{1,0},{2,3},{3,2},{4,5},{5,4},{6,7},{7,6},{8,9},{9,8},{10,11... | collective-permute-start | bytes 786440 | tf_op jit(solution)/shard_map/ppermute | solution.py:257
  15.0 1.4 %split_rows.1 = (bf16[2,24,2048]{2,1,0:T(8,128)(2,1)S(1)}, bf16[2,24,2048]{2,1,0:T(8,128)(2,1)S(1)}, bf16[16,24,512]{2,1,0:T(8,128)(2,1)}) custom-call(s32[3]{0:T(128)S(1)} %pad_add_fusion.1.at_ref, s32[1,3]{1,0:T(1,128)S(1)} %copy-done.6, bf16[24,8192]{1,0:T(8,128)(2,1)S(1)} %bitcast.78), custom_call_target="tpu_custom_call" | custom-call | bytes 1179648 | tf_op jit(solution)/shard_map/split_rows/pallas_call | solution.py:62
  17.4 15.5 %all-to-all-start = ((bf16[16,24,512]{2,1,0:T(8,128)(2,1)}), bf16[16,24,512]{2,1,0:T(8,128)(2,1)S(1)}, u32[]{:S(2)}, u32[]{:S(2)}) async-start(bf16[16,24,512]{2,1,0:T(8,128)(2,1)} %get-tuple-element.25), calls=%async_computation | async-start | bytes 786432 | tf_op jit(solution)/shard_map/all_to_all | solution.py:20
  32.9 7.2 %collective-permute-start.2 = (bf16[2,24,2048]{2,1,0:T(8,128)(2,1)S(1)}, bf16[2,24,2048]{2,1,0:T(8,128)(2,1)S(1)}, u32[]{:S(2)}, u32[]{:S(2)}) collective-permute-start(bf16[2,24,2048]{2,1,0:T(8,128)(2,1)S(1)} %get-tuple-element.27), channel_id=1, source_target_pairs={{0,256},{256,0},{1,257},{257,1},{2,258},{258,2},{3,259},{259,3},{4... | collective-permute-start | bytes 589832 | tf_op jit(solution)/shard_map/ppermute | solution.py:263
  40.1 4.0 %collective-permute-start = (bf16[2,24,2048]{2,1,0:T(8,128)(2,1)S(1)}, bf16[2,24,2048]{2,1,0:T(8,128)(2,1)S(1)}, u32[]{:S(2)}, u32[]{:S(2)}) collective-permute-start(bf16[2,24,2048]{2,1,0:T(8,128)(2,1)S(1)} %get-tuple-element.26), channel_id=1, source_target_pairs={{0,2},{2,0},{1,3},{3,1},{4,6},{6,4},{5,7},{7,5},{8,10},{10,8},{9,1... | collective-permute-start | bytes 589832 | tf_op jit(solution)/shard_map/ppermute | solution.py:265
  44.1 1.9 %collective-permute-start.1 = (bf16[2,24,2048]{2,1,0:T(8,128)(2,1)S(1)}, bf16[2,24,2048]{2,1,0:T(8,128)(2,1)S(1)}, u32[]{:S(2)}, u32[]{:S(2)}) collective-permute-start(bf16[2,24,2048]{2,1,0:T(8,128)(2,1)S(1)} %get-tuple-element.26), channel_id=1, source_target_pairs={{0,258},{2,256},{256,2},{258,0},{1,259},{3,257},{257,3},{259,1},{4... | collective-permute-start | bytes 589832 | tf_op jit(solution)/shard_map/ppermute | solution.py:264
  46.5 1.5 %fusion = bf16[3,16,512]{2,0,1:T(4,128)(2,1)S(1)} fusion(bf16[32,16,512]{2,1,0:T(8,128)(2,1)} %param.11, s32[3]{0:T(128)S(1)} %bitcast.81), kind=kOutput, calls=%fused_computation.1 | convolution fusion | flops 1572960 | bytes 573452 | tf_op jit(solution)/shard_map/bt,trd->brd/dot_general | solution.py:270
  49.0 5.2 %all-to-all-start.1 = ((f32[8,6,16,128]{3,2,1,0:T(8,128)}), f32[8,6,16,128]{3,2,1,0:T(8,128)S(1)}, u32[]{:S(2)}, u32[]{:S(2)}) async-start(f32[8,6,16,128]{3,2,1,0:T(8,128)} %rank_parts.1), calls=%async_computation.1 | async-start | bytes 786432 | tf_op jit(solution)/shard_map/all_to_all | solution.py:20
  54.3 9.3 %collective-permute-done = bf16[2,24,2048]{2,1,0:T(8,128)(2,1)S(1)} collective-permute-done((bf16[2,24,2048]{2,1,0:T(8,128)(2,1)S(1)}, bf16[2,24,2048]{2,1,0:T(8,128)(2,1)S(1)}, u32[]{:S(2)}, u32[]{:S(2)}) %collective-permute-start) | collective-permute-done | bytes 196640 | tf_op jit(solution)/shard_map/ppermute | solution.py:265
  63.6 1.4 %broadcast_in_dim.4 = bf16[4,2,2,24,2048]{4,3,2,1,0:T(8,128)(2,1)} broadcast(bf16[2,2,24,2048]{3,2,1,0:T(8,128)(2,1)S(1)} %pad_maximum_fusion), dimensions={1,2,3,4} | broadcast | bytes 1966080 | tf_op jit(solution)/shard_map/broadcast_in_dim | solution.py:275
  65.0 3.9 %all-to-all-start.2 = ((bf16[4,2,2,24,2048]{4,3,2,1,0:T(8,128)(2,1)}), bf16[4,2,2,24,2048]{4,3,2,1,0:T(8,128)(2,1)S(1)}, u32[]{:S(2)}, u32[]{:S(2)}) async-start(bf16[4,2,2,24,2048]{4,3,2,1,0:T(8,128)(2,1)} %broadcast_in_dim.4), calls=%async_computation.2 | async-start | bytes 3145728 | tf_op jit(solution)/shard_map/all_to_all | solution.py:20
  70.0 4.6 %collective-permute-start.3 = (f32[6,16,128]{2,1,0:T(8,128)S(1)}, f32[6,16,128]{2,1,0:T(8,128)S(1)}, u32[]{:S(2)}, u32[]{:S(2)}) collective-permute-start(f32[6,16,128]{2,1,0:T(8,128)S(1)} %reduce_sum.9.own_ref), channel_id=1, source_target_pairs={{0,256},{256,0},{1,257},{257,1},{2,258},{258,2},{3,259},{259,3},{4... | collective-permute-start | bytes 147464 | tf_op jit(solution)/shard_map/ppermute | solution.py:278
  74.6 3.4 %collective-permute-start.5 = (bf16[2,2,24,2048]{3,2,1,0:T(8,128)(2,1)S(1)}, bf16[2,2,24,2048]{3,2,1,0:T(8,128)(2,1)}, u32[]{:S(2)}, u32[]{:S(2)}) collective-permute-start(bf16[2,2,24,2048]{3,2,1,0:T(8,128)(2,1)S(1)} %pad_maximum_fusion.1.refs_0_), channel_id=1, source_target_pairs={{0,64},{64,128},{128,192},{192,0},{1,65},{65,129},{129,193},{193,1... | collective-permute-start | bytes 1179656 | tf_op jit(solution)/shard_map/ppermute | solution.py:286
  77.9 3.1 %collective-permute-start.6 = (bf16[2,2,24,2048]{3,2,1,0:T(8,128)(2,1)S(1)}, bf16[2,2,24,2048]{3,2,1,0:T(8,128)(2,1)}, u32[]{:S(2)}, u32[]{:S(2)}) collective-permute-start(bf16[2,2,24,2048]{3,2,1,0:T(8,128)(2,1)S(1)} %pad_maximum_fusion.1.refs_0_), channel_id=1, source_target_pairs={{0,192},{64,0},{128,64},{192,128},{1,193},{65,1},{129,65},{193,129... | collective-permute-start | bytes 1179656 | tf_op jit(solution)/shard_map/ppermute | solution.py:286
  81.1 3.7 %collective-permute-start.7 = (bf16[2,2,24,2048]{3,2,1,0:T(8,128)(2,1)S(1)}, bf16[2,2,24,2048]{3,2,1,0:T(8,128)(2,1)}, u32[]{:S(2)}, u32[]{:S(2)}) collective-permute-start(bf16[2,2,24,2048]{3,2,1,0:T(8,128)(2,1)S(1)} %pad_maximum_fusion.1.refs_0_), channel_id=1, source_target_pairs={{0,128},{64,192},{128,0},{192,64},{1,129},{65,193},{129,1},{193,65... | collective-permute-start | bytes 1179656 | tf_op jit(solution)/shard_map/ppermute | solution.py:286
  86.3 2.8 %all-to-all-done.2.refs_0_ = bf16[4,2,2,24,2048]{4,3,2,1,0:T(8,128)(2,1)S(1)} async-done(((bf16[4,2,2,24,2048]{4,3,2,1,0:T(8,128)(2,1)}), bf16[4,2,2,24,2048]{4,3,2,1,0:T(8,128)(2,1)S(1)}, u32[]{:S(2)}, u32[]{:S(2)}) %all-to-all-start.2) | async-done | bytes 1572896 | tf_op jit(solution)/shard_map/all_to_all | solution.py:20
  89.1 6.8 %all-to-all-start.3 = ((f32[8,13,512]{2,1,0:T(8,128)}), f32[8,13,512]{2,1,0:T(8,128)S(1)}, u32[]{:S(2)}, u32[]{:S(2)}) async-start(f32[8,13,512]{2,1,0:T(8,128)} %copy-done.4), calls=%async_computation.3 | async-start | bytes 524288 | tf_op jit(solution)/shard_map/all_to_all | solution.py:20
  96.1 3.9 %base_product.2 = (bf16[8,24,512]{2,1,0:T(8,128)(2,1)S(1)}, bf16[8,24,512]{2,1,0:T(8,128)(2,1)S(1)}) custom-call(s32[1]{0:T(128)} %bitcast.47.core_ref, bf16[8,2,2,256,512]{4,3,2,1,0:T(8,128)(2,1)} %bitcast.82, bf16[4,2,2,24,2048]{4,3,2,1,0:T(8,128)(2,1)S(1)} %all-to-all-done.2.refs_0_), custom_call_target="tpu_custom_call" | custom-call | flops 1610612736 | bytes 10354688 | tf_op jit(solution)/shard_map/base_product/pallas_call | solution.py:124
  100.0 9.0 %collective-permute-start.10 = (bf16[8,24,512]{2,1,0:T(8,128)(2,1)S(1)}, bf16[8,24,512]{2,1,0:T(8,128)(2,1)S(1)}, u32[]{:S(2)}, u32[]{:S(2)}) collective-permute-start(bf16[8,24,512]{2,1,0:T(8,128)(2,1)S(1)} %get-tuple-element.45), channel_id=1, source_target_pairs={{0,34},{2,32},{32,2},{34,0},{1,35},{3,33},{33,3},{35,1},{4,38},{6,... | collective-permute-start | bytes 589832 | tf_op jit(solution)/shard_map/ppermute | solution.py:291
  109.0 1.9 %collective-permute-start.8 = (bf16[8,24,512]{2,1,0:T(8,128)(2,1)S(1)}, bf16[8,24,512]{2,1,0:T(8,128)(2,1)S(1)}, u32[]{:S(2)}, u32[]{:S(2)}) collective-permute-start(bf16[8,24,512]{2,1,0:T(8,128)(2,1)S(1)} %get-tuple-element.37), channel_id=1, source_target_pairs={{0,2},{2,0},{1,3},{3,1},{4,6},{6,4},{5,7},{7,5},{8,10},{10,8},{9,1... | collective-permute-start | bytes 589832 | tf_op jit(solution)/shard_map/ppermute | solution.py:290
  111.2 5.1 %base_product.3 = (f32[8,24,512]{2,1,0:T(8,128)S(1)}, bf16[8,24,512]{2,1,0:T(8,128)(2,1)S(1)}) custom-call(s32[1]{0:T(128)} %bitcast.47.core_ref, bf16[8,2,2,256,512]{4,3,2,1,0:T(8,128)(2,1)} %bitcast.83, bf16[2,2,24,2048]{3,2,1,0:T(8,128)(2,1)S(1)} %pad_maximum_fusion.1.refs_0_, bf16[2,2,24,2048]{3,2,1,0:T(8,128)(2,1)} %collective-permute-done.5.refs_1_, ...), custom_call_target="tpu_custom_call" | custom-call | flops 1610612736 | bytes 10354688 | tf_op jit(solution)/shard_map/base_product/pallas_call | solution.py:124
  116.3 2.3 %collective-permute-start.9 = (bf16[8,24,512]{2,1,0:T(8,128)(2,1)S(1)}, bf16[8,24,512]{2,1,0:T(8,128)(2,1)S(1)}, u32[]{:S(2)}, u32[]{:S(2)}) collective-permute-start(bf16[8,24,512]{2,1,0:T(8,128)(2,1)S(1)} %get-tuple-element.44), channel_id=1, source_target_pairs={{0,32},{32,0},{1,33},{33,1},{2,34},{34,2},{3,35},{35,3},{4,36},{36... | collective-permute-start | bytes 589832 | tf_op jit(solution)/shard_map/ppermute | solution.py:295
  120.9 4.2 %collective-permute-done.8.refs_1_ = bf16[8,24,512]{2,1,0:T(8,128)(2,1)S(1)} collective-permute-done((bf16[8,24,512]{2,1,0:T(8,128)(2,1)S(1)}, bf16[8,24,512]{2,1,0:T(8,128)(2,1)S(1)}, u32[]{:S(2)}, u32[]{:S(2)}) %collective-permute-start.8) | collective-permute-done | bytes 196640 | tf_op jit(solution)/shard_map/ppermute | solution.py:290
  125.1 1.7 %join_rows.1 = bf16[16,24,512]{2,1,0:T(8,128)(2,1)} custom-call(s32[2,16]{1,0:T(2,128)S(1)} %pad_add_fusion.where_ref, bf16[3,16,128]{2,1,0:T(8,128)(2,1)S(1)} %get-tuple-element.31.proj_ref, bf16[3,16,512]{2,1,0:T(8,128)(2,1)S(1)} %copy.54.down_ref, f32[8,24,512]{2,1,0:T(8,128)S(1)} %get-tuple-element.43.refs_0_, ...), custom_call_target="tpu_custom_call" | custom-call | bytes 1966080 | tf_op jit(solution)/shard_map/join_rows/pallas_call | solution.py:231
  (52 shorter events, 10.6 us)
Async XLA Ops:
  7.2 38.9 %copy-start = (bf16[32,16,512]{2,1,0:T(8,128)(2,1)S(1)}, bf16[32,16,512]{2,1,0:T(8,128)(2,1)}, u32[]{:S(2)}) copy-start(bf16[32,16,512]{2,1,0:T(8,128)(2,1)} %param.10) | copy-start | bytes 1572868
  7.2 77.6 %all-gather.3.cloned.1.call-start = ((), (), s32[]{:S(2)}) async-start(), calls=%async_computation.4 | async-start | bytes 8912896 | tf_op jit(solution)/shard_map/all_gather | solution.py:260
  7.2 9.2 %collective-permute-start.4 = (bf16[512,256]{1,0:T(8,128)(2,1)}, bf16[512,256]{1,0:T(8,128)(2,1)S(1)}, u32[]{:S(2)}, u32[]{:S(2)}) collective-permute-start(bf16[512,256]{1,0:T(8,128)(2,1)} %from_ref.1), channel_id=1, source_target_pairs={{0,1},{1,0},{2,3},{3,2},{4,5},{5,4},{6,7},{7,6},{8,9},{9,8},{10,11... | collective-permute-start | bytes 786440 | tf_op jit(solution)/shard_map/ppermute | solution.py:257
  12.2 1.0 copy-start.3
  13.2 32.9 %copy-start.5 = (s32[1,3]{1,0:T(1,128)S(1)}, s32[1,3]{1,0:T(1,128)}, u32[]{:S(2)}) copy-start(s32[1,3]{1,0:T(1,128)} %ids_ref.1) | copy-start | bytes 40
  13.4 1.0 copy-start.2
  14.4 0.7 copy-start.6
  17.4 30.6 %copy-start.1 = (bf16[1,384,512]{2,1,0:T(8,128)(2,1)S(1)}, bf16[1,384,512]{2,1,0:T(8,128)(2,1)}, u32[]{:S(2)}) copy-start(bf16[1,384,512]{2,1,0:T(8,128)(2,1)} %param.8) | copy-start | bytes 1179652
  17.4 30.6 %all-to-all-start = ((bf16[16,24,512]{2,1,0:T(8,128)(2,1)}), bf16[16,24,512]{2,1,0:T(8,128)(2,1)S(1)}, u32[]{:S(2)}, u32[]{:S(2)}) async-start(bf16[16,24,512]{2,1,0:T(8,128)(2,1)} %get-tuple-element.25), calls=%async_computation | async-start | bytes 786432 | tf_op jit(solution)/shard_map/all_to_all | solution.py:20
  32.9 21.3 %collective-permute-start.2 = (bf16[2,24,2048]{2,1,0:T(8,128)(2,1)S(1)}, bf16[2,24,2048]{2,1,0:T(8,128)(2,1)S(1)}, u32[]{:S(2)}, u32[]{:S(2)}) collective-permute-start(bf16[2,24,2048]{2,1,0:T(8,128)(2,1)S(1)} %get-tuple-element.27), channel_id=1, source_target_pairs={{0,256},{256,0},{1,257},{257,1},{2,258},{258,2},{3,259},{259,3},{4... | collective-permute-start | bytes 589832 | tf_op jit(solution)/shard_map/ppermute | solution.py:263
  40.1 23.5 %collective-permute-start = (bf16[2,24,2048]{2,1,0:T(8,128)(2,1)S(1)}, bf16[2,24,2048]{2,1,0:T(8,128)(2,1)S(1)}, u32[]{:S(2)}, u32[]{:S(2)}) collective-permute-start(bf16[2,24,2048]{2,1,0:T(8,128)(2,1)S(1)} %get-tuple-element.26), channel_id=1, source_target_pairs={{0,2},{2,0},{1,3},{3,1},{4,6},{6,4},{5,7},{7,5},{8,10},{10,8},{9,1... | collective-permute-start | bytes 589832 | tf_op jit(solution)/shard_map/ppermute | solution.py:265
  44.1 19.5 %collective-permute-start.1 = (bf16[2,24,2048]{2,1,0:T(8,128)(2,1)S(1)}, bf16[2,24,2048]{2,1,0:T(8,128)(2,1)S(1)}, u32[]{:S(2)}, u32[]{:S(2)}) collective-permute-start(bf16[2,24,2048]{2,1,0:T(8,128)(2,1)S(1)} %get-tuple-element.26), channel_id=1, source_target_pairs={{0,258},{2,256},{256,2},{258,0},{1,259},{3,257},{257,3},{259,1},{4... | collective-permute-start | bytes 589832 | tf_op jit(solution)/shard_map/ppermute | solution.py:264
  49.0 14.6 %all-to-all-start.1 = ((f32[8,6,16,128]{3,2,1,0:T(8,128)}), f32[8,6,16,128]{3,2,1,0:T(8,128)S(1)}, u32[]{:S(2)}, u32[]{:S(2)}) async-start(f32[8,6,16,128]{3,2,1,0:T(8,128)} %rank_parts.1), calls=%async_computation.1 | async-start | bytes 786432 | tf_op jit(solution)/shard_map/all_to_all | solution.py:20
  63.6 1.4 %copy-start.7 = (f32[8,6,16,128]{3,2,1,0:T(8,128)}, f32[8,6,16,128]{3,2,1,0:T(8,128)S(1)}, u32[]{:S(2)}) copy-start(f32[8,6,16,128]{3,2,1,0:T(8,128)S(1)} %all-to-all-done.1) | copy-start | bytes 1179652
  65.0 24.1 %all-to-all-start.2 = ((bf16[4,2,2,24,2048]{4,3,2,1,0:T(8,128)(2,1)}), bf16[4,2,2,24,2048]{4,3,2,1,0:T(8,128)(2,1)S(1)}, u32[]{:S(2)}, u32[]{:S(2)}) async-start(bf16[4,2,2,24,2048]{4,3,2,1,0:T(8,128)(2,1)} %broadcast_in_dim.4), calls=%async_computation.2 | async-start | bytes 3145728 | tf_op jit(solution)/shard_map/all_to_all | solution.py:20
  70.0 14.8 %collective-permute-start.3 = (f32[6,16,128]{2,1,0:T(8,128)S(1)}, f32[6,16,128]{2,1,0:T(8,128)S(1)}, u32[]{:S(2)}, u32[]{:S(2)}) collective-permute-start(f32[6,16,128]{2,1,0:T(8,128)S(1)} %reduce_sum.9.own_ref), channel_id=1, source_target_pairs={{0,256},{256,0},{1,257},{257,1},{2,258},{258,2},{3,259},{259,3},{4... | collective-permute-start | bytes 147464 | tf_op jit(solution)/shard_map/ppermute | solution.py:278
  74.6 36.4 %collective-permute-start.5 = (bf16[2,2,24,2048]{3,2,1,0:T(8,128)(2,1)S(1)}, bf16[2,2,24,2048]{3,2,1,0:T(8,128)(2,1)}, u32[]{:S(2)}, u32[]{:S(2)}) collective-permute-start(bf16[2,2,24,2048]{3,2,1,0:T(8,128)(2,1)S(1)} %pad_maximum_fusion.1.refs_0_), channel_id=1, source_target_pairs={{0,64},{64,128},{128,192},{192,0},{1,65},{65,129},{129,193},{193,1... | collective-permute-start | bytes 1179656 | tf_op jit(solution)/shard_map/ppermute | solution.py:286
  77.9 33.0 %collective-permute-start.6 = (bf16[2,2,24,2048]{3,2,1,0:T(8,128)(2,1)S(1)}, bf16[2,2,24,2048]{3,2,1,0:T(8,128)(2,1)}, u32[]{:S(2)}, u32[]{:S(2)}) collective-permute-start(bf16[2,2,24,2048]{3,2,1,0:T(8,128)(2,1)S(1)} %pad_maximum_fusion.1.refs_0_), channel_id=1, source_target_pairs={{0,192},{64,0},{128,64},{192,128},{1,193},{65,1},{129,65},{193,129... | collective-permute-start | bytes 1179656 | tf_op jit(solution)/shard_map/ppermute | solution.py:286
  81.1 29.9 %collective-permute-start.7 = (bf16[2,2,24,2048]{3,2,1,0:T(8,128)(2,1)S(1)}, bf16[2,2,24,2048]{3,2,1,0:T(8,128)(2,1)}, u32[]{:S(2)}, u32[]{:S(2)}) collective-permute-start(bf16[2,2,24,2048]{3,2,1,0:T(8,128)(2,1)S(1)} %pad_maximum_fusion.1.refs_0_), channel_id=1, source_target_pairs={{0,128},{64,192},{128,0},{192,64},{1,129},{65,193},{129,1},{193,65... | collective-permute-start | bytes 1179656 | tf_op jit(solution)/shard_map/ppermute | solution.py:286
  85.6 0.7 copy-start.4
  89.1 21.8 %all-to-all-start.3 = ((f32[8,13,512]{2,1,0:T(8,128)}), f32[8,13,512]{2,1,0:T(8,128)S(1)}, u32[]{:S(2)}, u32[]{:S(2)}) async-start(f32[8,13,512]{2,1,0:T(8,128)} %copy-done.4), calls=%async_computation.3 | async-start | bytes 524288 | tf_op jit(solution)/shard_map/all_to_all | solution.py:20
  100.0 20.9 %collective-permute-start.10 = (bf16[8,24,512]{2,1,0:T(8,128)(2,1)S(1)}, bf16[8,24,512]{2,1,0:T(8,128)(2,1)S(1)}, u32[]{:S(2)}, u32[]{:S(2)}) collective-permute-start(bf16[8,24,512]{2,1,0:T(8,128)(2,1)S(1)} %get-tuple-element.45), channel_id=1, source_target_pairs={{0,34},{2,32},{32,2},{34,0},{1,35},{3,33},{33,3},{35,1},{4,38},{6,... | collective-permute-start | bytes 589832 | tf_op jit(solution)/shard_map/ppermute | solution.py:291
  109.0 16.1 %collective-permute-start.8 = (bf16[8,24,512]{2,1,0:T(8,128)(2,1)S(1)}, bf16[8,24,512]{2,1,0:T(8,128)(2,1)S(1)}, u32[]{:S(2)}, u32[]{:S(2)}) collective-permute-start(bf16[8,24,512]{2,1,0:T(8,128)(2,1)S(1)} %get-tuple-element.37), channel_id=1, source_target_pairs={{0,2},{2,0},{1,3},{3,1},{4,6},{6,4},{5,7},{7,5},{8,10},{10,8},{9,1... | collective-permute-start | bytes 589832 | tf_op jit(solution)/shard_map/ppermute | solution.py:290
  116.3 8.8 %collective-permute-start.9 = (bf16[8,24,512]{2,1,0:T(8,128)(2,1)S(1)}, bf16[8,24,512]{2,1,0:T(8,128)(2,1)S(1)}, u32[]{:S(2)}, u32[]{:S(2)}) collective-permute-start(bf16[8,24,512]{2,1,0:T(8,128)(2,1)S(1)} %get-tuple-element.44), channel_id=1, source_target_pairs={{0,32},{32,0},{1,33},{33,1},{2,34},{34,2},{3,35},{35,3},{4,36},{36... | collective-permute-start | bytes 589832 | tf_op jit(solution)/shard_map/ppermute | solution.py:295
Sparse Core Ops, SparseCore 0:
  17.5 65.2 all-gather.2

commit v6 on v5

--- a/solution.py
+++ b/solution.py
@@ -92,24 +92,27 @@
     )(*operands)
 
 
-def base_kernel(core_ref, w_ref, *refs):
-    pieces, outs, held_ref, sems = refs[: -CORE - 2], refs[-CORE - 2 : -2], refs[-2], refs[-1]
-    copies = [pltpu.make_async_copy(w_ref.at[d], held_ref.at[d], sems.at[d]) for d in range(DP)]
-    for copy in copies:
-        copy.start()
+def base_kernel(count, core_ref, w_ref, *refs):
+    pieces, outs, held_ref, sems = refs[: -count - 2], refs[-count - 2 : -2], refs[-2], refs[-1]
+    copies = [
+        [pltpu.make_async_copy(w_ref.at[d, lax.rem(core_ref[0] + i, CORE)], held_ref.at[d, i], sems.at[d, i]) for i in range(count)]
+        for d in range(DP)
+    ]
+    for pair in copies:
+        for copy in pair:
+            copy.start()
     if len(pieces[0].shape) > 4:
         pieces = [pieces[0][i] for i in range(pieces[0].shape[0])]
     zs, _, m, depth = pieces[0].shape
     chunk = w_ref.shape[3]
     rows = [jnp.concatenate([piece[:, h].reshape(zs * m, depth) for piece in pieces], axis=0) for h in range(KL)]
-    totals = [None] * CORE
-    for d, copy in enumerate(copies):
-        copy.wait()
-        for i in range(CORE):
-            at = lax.rem(core_ref[0] + i, CORE)
+    totals = [None] * count
+    for d, pair in enumerate(copies):
+        for i, copy in enumerate(pair):
+            copy.wait()
             for h in range(KL):
                 term = lax.dot_general(
-                    rows[h][:, d * chunk : (d + 1) * chunk], held_ref[d, at, h], (((1,), (0,)), ((), ())), preferred_element_type=F32
+                    rows[h][:, d * chunk : (d + 1) * chunk], held_ref[d, i, h], (((1,), (0,)), ((), ())), preferred_element_type=F32
                 )
                 totals[i] = term if totals[i] is None else totals[i] + term
     for out, total in zip(outs, totals):
@@ -118,18 +121,21 @@
 
 def base_product(core, weights, pieces, dtypes):
     zs, _, m, _ = pieces[0].shape[-4:]
-    count, feats = X * zs, weights.shape[4]
+    rows, feats, count = X * zs, weights.shape[4], len(dtypes)
     vmem = pl.BlockSpec(memory_space=pltpu.VMEM)
     smem = pl.BlockSpec(memory_space=pltpu.SMEM)
     return pl.pallas_call(
-        base_kernel,
-        out_shape=[jax.ShapeDtypeStruct((count, m, feats), dtype) for dtype in dtypes],
+        functools.partial(base_kernel, count),
+        out_shape=[jax.ShapeDtypeStruct((rows, m, feats), dtype) for dtype in dtypes],
         in_specs=[smem, pl.BlockSpec(memory_space=pl.ANY)] + [vmem] * len(pieces),
-        out_specs=[vmem] * CORE,
-        scratch_shapes=[pltpu.VMEM(weights.shape, weights.dtype), pltpu.SemaphoreType.DMA((DP,))],
+        out_specs=[vmem] * count,
+        scratch_shapes=[
+            pltpu.VMEM((DP, count) + weights.shape[2:], weights.dtype),
+            pltpu.SemaphoreType.DMA((DP, count)),
+        ],
         cost_estimate=pl.CostEstimate(
-            flops=2 * count * m * weights.size,
-            bytes_accessed=2 * (sum(p.size for p in pieces) + weights.size + 2 * count * m * feats),
+            flops=count * rows * m * weights.size,
+            bytes_accessed=2 * sum(p.size for p in pieces) + count * (weights.size + 2 * rows * m * feats),
             transcendentals=0,
         ),
         compiler_params=pltpu.CompilerParams(vmem_limit_bytes=4 * VMEM_LIMIT),
@@ -286,11 +292,13 @@
     home = [lax.ppermute(home, "x", shift_pairs(X, offset)) if offset else home for offset in OFFSETS]
     away, grads = lax.optimization_barrier((away, grads))
     core_at = core[None].astype(jnp.int32)
-    send, send_other = base_product(core_at, weights, [away], (BF16, BF16))
+    other_at = 1 - core_at
+    (send,) = base_product(core_at, weights, [away], (BF16,))
     sums = lax.ppermute(send, "kh", swap_pairs(KH, 1))
+    (send_other,) = base_product(other_at, weights, [away], (BF16,))
     sums_other = lax.ppermute(send_other, ("core", "kh"), swap_pairs(CORE * KH, 3))
     got = exchange(grads, "dp")
-    home, send, got = lax.optimization_barrier((home, send, got))
+    home, send_other, got = lax.optimization_barrier((home, send_other, got))
     keep, keep_other = base_product(core_at, weights, home, (F32, BF16))
     keep_other = lax.ppermute(keep_other, "core", swap_pairs(CORE, 1))
     where = [

time: 135 us -> 132 us (0.978)
  waiting for transfers between devices: 16.8 us -> 12.2 us
    ppermute x1, waiting for transfers between devices: 4.21 us -> 0.01 us  [per_device(): sums = lax.ppermute(send, 'kh', swap_pairs(KH, 1))]
    ppermute x1, starting transfers between devices: 8.97 us -> 5.23 us  [per_device(): lax.ppermute(send_other, ('core', 'kh'), swap_pairs(CORE * KH, 3))]
    ppermute x1, starting transfers between devices: 1.92 us -> 5.66 us  [per_device(): sums = lax.ppermute(send, 'kh', swap_pairs(KH, 1))]
    pallas_call x2 -> x3, Pallas kernels: 8.94 us -> 10.2 us  [base_product(): pl.pallas_call(functools.partial(base_kernel, count), out_shape=[jax.Shap...]
    unnamed x18 -> x20, local copies, waits for them, and re-layouts: 4.84 us -> 4.84 us
  transfers between devices with their start and end apart: 16 -> 16, of which waited for: 4 -> 2; matrix products, arithmetic and copies ran while one was open for 5% -> 6% of each run, Pallas kernels for 9% -> 10%
where the time goes in v6:
time: 132 us; the launch traced here: 131 us
  starting transfers between devices  77.5 us (59%)
  Pallas kernels  16.2 us (12%)
  between operations  14.4 us (11%)
  waiting for transfers between devices  12.2 us (9%)
  local copies, waits for them, and re-layouts  7.34 us (6%)
  matrix products  2.23 us (2%)
    all_to_all x4, starting transfers between devices, exchange(): return lax.all_to_all(blocks, axes, split_axis=0, concat_axis=0, tiled=True)  31.4 us
    pallas_call x3, Pallas kernels, base_product(): pl.pallas_call(functools.partial(base_kernel, count), out_shape=[jax.Shap...  10.2 us
    ppermute x3, starting transfers between devices, per_device(): lax.ppermute(home, 'x', shift_pairs(X, offset))  10.2 us
    ppermute x1, waiting for transfers between devices, per_device(): from_kh = lax.ppermute(other, 'kh', swap_pairs(KH, 1))  9.3 us
    ppermute x1, starting transfers between devices, per_device(): from_zh = lax.ppermute(same, 'zh', swap_pairs(ZH, 1))  7.19 us
    ppermute x1, starting transfers between devices, per_device(): sums = lax.ppermute(send, 'kh', swap_pairs(KH, 1))  5.66 us
    ppermute x1, starting transfers between devices, per_device(): lax.ppermute(send_other, ('core', 'kh'), swap_pairs(CORE * KH, 3))  5.23 us
    ppermute x1, starting transfers between devices, per_device(): lax.ppermute(weight, 'kl', swap_pairs(KL, 1))  4.96 us
  transfers between devices with their start and end apart: 16, of which 2 were waited for; matrix products, arithmetic and copies ran while one was open for 6% of the time, Pallas kernels for 10%

profile of v6, /device:TPU:1, one launch (start us, length us, event | category | flops | bytes accessed | tf_op | source)
XLA Modules:
  0.0 131.1 jit_solution(16446790166337797748)
XLA Ops:
  7.2 5.0 %collective-permute-start.4 = (bf16[512,256]{1,0:T(8,128)(2,1)}, bf16[512,256]{1,0:T(8,128)(2,1)S(1)}, u32[]{:S(2)}, u32[]{:S(2)}) collective-permute-start(bf16[512,256]{1,0:T(8,128)(2,1)} %from_ref.1), channel_id=1, source_target_pairs={{0,1},{1,0},{2,3},{3,2},{4,5},{5,4},{6,7},{7,6},{8,9},{9,8},{10,11... | collective-permute-start | bytes 786440 | tf_op jit(solution)/shard_map/ppermute | solution.py:263
  15.0 1.4 %split_rows.1 = (bf16[2,24,2048]{2,1,0:T(8,128)(2,1)S(1)}, bf16[2,24,2048]{2,1,0:T(8,128)(2,1)S(1)}, bf16[16,24,512]{2,1,0:T(8,128)(2,1)}) custom-call(s32[3]{0:T(128)S(1)} %pad_add_fusion.1.at_ref, s32[1,3]{1,0:T(1,128)S(1)} %copy-done.6, bf16[24,8192]{1,0:T(8,128)(2,1)S(1)} %bitcast.78), custom_call_target="tpu_custom_call" | custom-call | bytes 1179648 | tf_op jit(solution)/shard_map/split_rows/pallas_call | solution.py:62
  17.4 15.5 %all-to-all-start = ((bf16[16,24,512]{2,1,0:T(8,128)(2,1)}), bf16[16,24,512]{2,1,0:T(8,128)(2,1)S(1)}, u32[]{:S(2)}, u32[]{:S(2)}) async-start(bf16[16,24,512]{2,1,0:T(8,128)(2,1)} %get-tuple-element.23), calls=%async_computation | async-start | bytes 786432 | tf_op jit(solution)/shard_map/all_to_all | solution.py:20
  32.9 7.2 %collective-permute-start.2 = (bf16[2,24,2048]{2,1,0:T(8,128)(2,1)S(1)}, bf16[2,24,2048]{2,1,0:T(8,128)(2,1)S(1)}, u32[]{:S(2)}, u32[]{:S(2)}) collective-permute-start(bf16[2,24,2048]{2,1,0:T(8,128)(2,1)S(1)} %get-tuple-element.25), channel_id=1, source_target_pairs={{0,256},{256,0},{1,257},{257,1},{2,258},{258,2},{3,259},{259,3},{4... | collective-permute-start | bytes 589832 | tf_op jit(solution)/shard_map/ppermute | solution.py:269
  40.1 4.0 %collective-permute-start = (bf16[2,24,2048]{2,1,0:T(8,128)(2,1)S(1)}, bf16[2,24,2048]{2,1,0:T(8,128)(2,1)S(1)}, u32[]{:S(2)}, u32[]{:S(2)}) collective-permute-start(bf16[2,24,2048]{2,1,0:T(8,128)(2,1)S(1)} %get-tuple-element.24), channel_id=1, source_target_pairs={{0,2},{2,0},{1,3},{3,1},{4,6},{6,4},{5,7},{7,5},{8,10},{10,8},{9,1... | collective-permute-start | bytes 589832 | tf_op jit(solution)/shard_map/ppermute | solution.py:271
  44.1 1.9 %collective-permute-start.1 = (bf16[2,24,2048]{2,1,0:T(8,128)(2,1)S(1)}, bf16[2,24,2048]{2,1,0:T(8,128)(2,1)S(1)}, u32[]{:S(2)}, u32[]{:S(2)}) collective-permute-start(bf16[2,24,2048]{2,1,0:T(8,128)(2,1)S(1)} %get-tuple-element.24), channel_id=1, source_target_pairs={{0,258},{2,256},{256,2},{258,0},{1,259},{3,257},{257,3},{259,1},{4... | collective-permute-start | bytes 589832 | tf_op jit(solution)/shard_map/ppermute | solution.py:270
  46.5 1.5 %fusion = bf16[3,16,512]{2,0,1:T(4,128)(2,1)S(1)} fusion(bf16[32,16,512]{2,1,0:T(8,128)(2,1)} %param.11, s32[3]{0:T(128)S(1)} %bitcast.81), kind=kOutput, calls=%fused_computation.1 | convolution fusion | flops 1572960 | bytes 573452 | tf_op jit(solution)/shard_map/bt,trd->brd/dot_general | solution.py:276
  49.0 5.2 %all-to-all-start.1 = ((f32[8,6,16,128]{3,2,1,0:T(8,128)}), f32[8,6,16,128]{3,2,1,0:T(8,128)S(1)}, u32[]{:S(2)}, u32[]{:S(2)}) async-start(f32[8,6,16,128]{3,2,1,0:T(8,128)} %rank_parts.1), calls=%async_computation.1 | async-start | bytes 786432 | tf_op jit(solution)/shard_map/all_to_all | solution.py:20
  54.3 9.3 %collective-permute-done = bf16[2,24,2048]{2,1,0:T(8,128)(2,1)S(1)} collective-permute-done((bf16[2,24,2048]{2,1,0:T(8,128)(2,1)S(1)}, bf16[2,24,2048]{2,1,0:T(8,128)(2,1)S(1)}, u32[]{:S(2)}, u32[]{:S(2)}) %collective-permute-start) | collective-permute-done | bytes 196640 | tf_op jit(solution)/shard_map/ppermute | solution.py:271
  63.6 1.4 %broadcast_in_dim.4 = bf16[4,2,2,24,2048]{4,3,2,1,0:T(8,128)(2,1)} broadcast(bf16[2,2,24,2048]{3,2,1,0:T(8,128)(2,1)S(1)} %pad_maximum_fusion), dimensions={1,2,3,4} | broadcast | bytes 1966080 | tf_op jit(solution)/shard_map/broadcast_in_dim | solution.py:281
  65.0 3.9 %all-to-all-start.2 = ((bf16[4,2,2,24,2048]{4,3,2,1,0:T(8,128)(2,1)}), bf16[4,2,2,24,2048]{4,3,2,1,0:T(8,128)(2,1)S(1)}, u32[]{:S(2)}, u32[]{:S(2)}) async-start(bf16[4,2,2,24,2048]{4,3,2,1,0:T(8,128)(2,1)} %broadcast_in_dim.4), calls=%async_computation.2 | async-start | bytes 3145728 | tf_op jit(solution)/shard_map/all_to_all | solution.py:20
  70.0 4.6 %collective-permute-start.3 = (f32[6,16,128]{2,1,0:T(8,128)S(1)}, f32[6,16,128]{2,1,0:T(8,128)S(1)}, u32[]{:S(2)}, u32[]{:S(2)}) collective-permute-start(f32[6,16,128]{2,1,0:T(8,128)S(1)} %reduce_sum.9.own_ref), channel_id=1, source_target_pairs={{0,256},{256,0},{1,257},{257,1},{2,258},{258,2},{3,259},{259,3},{4... | collective-permute-start | bytes 147464 | tf_op jit(solution)/shard_map/ppermute | solution.py:284
  74.6 3.4 %collective-permute-start.5 = (bf16[2,2,24,2048]{3,2,1,0:T(8,128)(2,1)S(1)}, bf16[2,2,24,2048]{3,2,1,0:T(8,128)(2,1)}, u32[]{:S(2)}, u32[]{:S(2)}) collective-permute-start(bf16[2,2,24,2048]{3,2,1,0:T(8,128)(2,1)S(1)} %pad_maximum_fusion.1.refs_0_), channel_id=1, source_target_pairs={{0,64},{64,128},{128,192},{192,0},{1,65},{65,129},{129,193},{193,1... | collective-permute-start | bytes 1179656 | tf_op jit(solution)/shard_map/ppermute | solution.py:292
  77.9 3.1 %collective-permute-start.6 = (bf16[2,2,24,2048]{3,2,1,0:T(8,128)(2,1)S(1)}, bf16[2,2,24,2048]{3,2,1,0:T(8,128)(2,1)}, u32[]{:S(2)}, u32[]{:S(2)}) collective-permute-start(bf16[2,2,24,2048]{3,2,1,0:T(8,128)(2,1)S(1)} %pad_maximum_fusion.1.refs_0_), channel_id=1, source_target_pairs={{0,192},{64,0},{128,64},{192,128},{1,193},{65,1},{129,65},{193,129... | collective-permute-start | bytes 1179656 | tf_op jit(solution)/shard_map/ppermute | solution.py:292
  81.1 3.7 %collective-permute-start.7 = (bf16[2,2,24,2048]{3,2,1,0:T(8,128)(2,1)S(1)}, bf16[2,2,24,2048]{3,2,1,0:T(8,128)(2,1)}, u32[]{:S(2)}, u32[]{:S(2)}) collective-permute-start(bf16[2,2,24,2048]{3,2,1,0:T(8,128)(2,1)S(1)} %pad_maximum_fusion.1.refs_0_), channel_id=1, source_target_pairs={{0,128},{64,192},{128,0},{192,64},{1,129},{65,193},{129,1},{193,65... | collective-permute-start | bytes 1179656 | tf_op jit(solution)/shard_map/ppermute | solution.py:292
  86.3 2.8 %all-to-all-done.2.refs_0_ = bf16[4,2,2,24,2048]{4,3,2,1,0:T(8,128)(2,1)S(1)} async-done(((bf16[4,2,2,24,2048]{4,3,2,1,0:T(8,128)(2,1)}), bf16[4,2,2,24,2048]{4,3,2,1,0:T(8,128)(2,1)S(1)}, u32[]{:S(2)}, u32[]{:S(2)}) %all-to-all-start.2) | async-done | bytes 1572896 | tf_op jit(solution)/shard_map/all_to_all | solution.py:20
  89.1 6.8 %all-to-all-start.3 = ((f32[8,13,512]{2,1,0:T(8,128)}), f32[8,13,512]{2,1,0:T(8,128)S(1)}, u32[]{:S(2)}, u32[]{:S(2)}) async-start(f32[8,13,512]{2,1,0:T(8,128)} %copy-done.4), calls=%async_computation.3 | async-start | bytes 524288 | tf_op jit(solution)/shard_map/all_to_all | solution.py:20
  96.1 2.5 %base_product.5 = bf16[8,24,512]{2,1,0:T(8,128)(2,1)S(1)} custom-call(s32[1]{0:T(128)} %bitcast.47.core_ref, bf16[8,2,2,256,512]{4,3,2,1,0:T(8,128)(2,1)} %bitcast.82, bf16[4,2,2,24,2048]{4,3,2,1,0:T(8,128)(2,1)S(1)} %all-to-all-done.2.refs_0_), custom_call_target="tpu_custom_call" | custom-call | flops 805306368 | bytes 5963776 | tf_op jit(solution)/shard_map/base_product/pallas_call | solution.py:127
  98.6 5.7 %collective-permute-start.8 = (bf16[8,24,512]{2,1,0:T(8,128)(2,1)S(1)}, bf16[8,24,512]{2,1,0:T(8,128)(2,1)S(1)}, u32[]{:S(2)}, u32[]{:S(2)}) collective-permute-start(bf16[8,24,512]{2,1,0:T(8,128)(2,1)S(1)} %base_product.5), channel_id=1, source_target_pairs={{0,2},{2,0},{1,3},{3,1},{4,6},{6,4},{5,7},{7,5},{8,10},{10,8},{9,1... | collective-permute-start | bytes 589832 | tf_op jit(solution)/shard_map/ppermute | solution.py:297
  104.3 2.5 %base_product.3 = bf16[8,24,512]{2,1,0:T(8,128)(2,1)S(1)} custom-call(s32[1]{0:T(128)S(6)} %sub.20.core_ref, bf16[8,2,2,256,512]{4,3,2,1,0:T(8,128)(2,1)} %bitcast.83, bf16[4,2,2,24,2048]{4,3,2,1,0:T(8,128)(2,1)S(1)} %all-to-all-done.2.refs_0_), custom_call_target="tpu_custom_call" | custom-call | flops 805306368 | bytes 5963776 | tf_op jit(solution)/shard_map/base_product/pallas_call | solution.py:127
  106.8 5.2 %collective-permute-start.10 = (bf16[8,24,512]{2,1,0:T(8,128)(2,1)S(1)}, bf16[8,24,512]{2,1,0:T(8,128)(2,1)S(1)}, u32[]{:S(2)}, u32[]{:S(2)}) collective-permute-start(bf16[8,24,512]{2,1,0:T(8,128)(2,1)S(1)} %base_product.3), channel_id=1, source_target_pairs={{0,34},{2,32},{32,2},{34,0},{1,35},{3,33},{33,3},{35,1},{4,38},{6,... | collective-permute-start | bytes 589832 | tf_op jit(solution)/shard_map/ppermute | solution.py:299
  113.0 5.2 %base_product.4 = (f32[8,24,512]{2,1,0:T(8,128)S(1)}, bf16[8,24,512]{2,1,0:T(8,128)(2,1)S(1)}) custom-call(s32[1]{0:T(128)} %bitcast.47.core_ref, bf16[8,2,2,256,512]{4,3,2,1,0:T(8,128)(2,1)} %bitcast.84, bf16[2,2,24,2048]{3,2,1,0:T(8,128)(2,1)S(1)} %pad_maximum_fusion.1.refs_0_, bf16[2,2,24,2048]{3,2,1,0:T(8,128)(2,1)} %collective-permute-done.5.refs_1_, ...), custom_call_target="tpu_custom_call" | custom-call | flops 1610612736 | bytes 10354688 | tf_op jit(solution)/shard_map/base_product/pallas_call | solution.py:127
  118.2 2.3 %collective-permute-start.9 = (bf16[8,24,512]{2,1,0:T(8,128)(2,1)S(1)}, bf16[8,24,512]{2,1,0:T(8,128)(2,1)S(1)}, u32[]{:S(2)}, u32[]{:S(2)}) collective-permute-start(bf16[8,24,512]{2,1,0:T(8,128)(2,1)S(1)} %get-tuple-element.41), channel_id=1, source_target_pairs={{0,32},{32,0},{1,33},{33,1},{2,34},{34,2},{3,35},{35,3},{4,36},{36... | collective-permute-start | bytes 589832 | tf_op jit(solution)/shard_map/ppermute | solution.py:303
  122.5 1.8 %join_rows.1 = bf16[16,24,512]{2,1,0:T(8,128)(2,1)} custom-call(s32[2,16]{1,0:T(2,128)S(1)} %pad_add_fusion.where_ref, bf16[3,16,128]{2,1,0:T(8,128)(2,1)S(1)} %get-tuple-element.29.proj_ref, bf16[3,16,512]{2,1,0:T(8,128)(2,1)S(1)} %copy.54.down_ref, f32[8,24,512]{2,1,0:T(8,128)S(1)} %get-tuple-element.40.refs_0_, ...), custom_call_target="tpu_custom_call" | custom-call | bytes 1966080 | tf_op jit(solution)/shard_map/join_rows/pallas_call | solution.py:237
  (55 shorter events, 10.9 us)
Async XLA Ops:
  7.2 38.9 %copy-start = (bf16[32,16,512]{2,1,0:T(8,128)(2,1)S(1)}, bf16[32,16,512]{2,1,0:T(8,128)(2,1)}, u32[]{:S(2)}) copy-start(bf16[32,16,512]{2,1,0:T(8,128)(2,1)} %param.10) | copy-start | bytes 1572868
  7.2 77.6 %all-gather.3.cloned.1.call-start = ((), (), s32[]{:S(2)}) async-start(), calls=%async_computation.4 | async-start | bytes 8912896 | tf_op jit(solution)/shard_map/all_gather | solution.py:266
  7.2 9.2 %collective-permute-start.4 = (bf16[512,256]{1,0:T(8,128)(2,1)}, bf16[512,256]{1,0:T(8,128)(2,1)S(1)}, u32[]{:S(2)}, u32[]{:S(2)}) collective-permute-start(bf16[512,256]{1,0:T(8,128)(2,1)} %from_ref.1), channel_id=1, source_target_pairs={{0,1},{1,0},{2,3},{3,2},{4,5},{5,4},{6,7},{7,6},{8,9},{9,8},{10,11... | collective-permute-start | bytes 786440 | tf_op jit(solution)/shard_map/ppermute | solution.py:263
  12.2 1.0 copy-start.3
  13.2 32.9 %copy-start.5 = (s32[1,3]{1,0:T(1,128)S(1)}, s32[1,3]{1,0:T(1,128)}, u32[]{:S(2)}) copy-start(s32[1,3]{1,0:T(1,128)} %ids_ref.1) | copy-start | bytes 40
  13.4 1.0 copy-start.2
  17.4 30.6 %copy-start.1 = (bf16[1,384,512]{2,1,0:T(8,128)(2,1)S(1)}, bf16[1,384,512]{2,1,0:T(8,128)(2,1)}, u32[]{:S(2)}) copy-start(bf16[1,384,512]{2,1,0:T(8,128)(2,1)} %param.8) | copy-start | bytes 1179652
  17.4 30.6 %all-to-all-start = ((bf16[16,24,512]{2,1,0:T(8,128)(2,1)}), bf16[16,24,512]{2,1,0:T(8,128)(2,1)S(1)}, u32[]{:S(2)}, u32[]{:S(2)}) async-start(bf16[16,24,512]{2,1,0:T(8,128)(2,1)} %get-tuple-element.23), calls=%async_computation | async-start | bytes 786432 | tf_op jit(solution)/shard_map/all_to_all | solution.py:20
  32.9 21.3 %collective-permute-start.2 = (bf16[2,24,2048]{2,1,0:T(8,128)(2,1)S(1)}, bf16[2,24,2048]{2,1,0:T(8,128)(2,1)S(1)}, u32[]{:S(2)}, u32[]{:S(2)}) collective-permute-start(bf16[2,24,2048]{2,1,0:T(8,128)(2,1)S(1)} %get-tuple-element.25), channel_id=1, source_target_pairs={{0,256},{256,0},{1,257},{257,1},{2,258},{258,2},{3,259},{259,3},{4... | collective-permute-start | bytes 589832 | tf_op jit(solution)/shard_map/ppermute | solution.py:269
  40.1 23.5 %collective-permute-start = (bf16[2,24,2048]{2,1,0:T(8,128)(2,1)S(1)}, bf16[2,24,2048]{2,1,0:T(8,128)(2,1)S(1)}, u32[]{:S(2)}, u32[]{:S(2)}) collective-permute-start(bf16[2,24,2048]{2,1,0:T(8,128)(2,1)S(1)} %get-tuple-element.24), channel_id=1, source_target_pairs={{0,2},{2,0},{1,3},{3,1},{4,6},{6,4},{5,7},{7,5},{8,10},{10,8},{9,1... | collective-permute-start | bytes 589832 | tf_op jit(solution)/shard_map/ppermute | solution.py:271
  44.1 19.5 %collective-permute-start.1 = (bf16[2,24,2048]{2,1,0:T(8,128)(2,1)S(1)}, bf16[2,24,2048]{2,1,0:T(8,128)(2,1)S(1)}, u32[]{:S(2)}, u32[]{:S(2)}) collective-permute-start(bf16[2,24,2048]{2,1,0:T(8,128)(2,1)S(1)} %get-tuple-element.24), channel_id=1, source_target_pairs={{0,258},{2,256},{256,2},{258,0},{1,259},{3,257},{257,3},{259,1},{4... | collective-permute-start | bytes 589832 | tf_op jit(solution)/shard_map/ppermute | solution.py:270
  49.0 14.6 %all-to-all-start.1 = ((f32[8,6,16,128]{3,2,1,0:T(8,128)}), f32[8,6,16,128]{3,2,1,0:T(8,128)S(1)}, u32[]{:S(2)}, u32[]{:S(2)}) async-start(f32[8,6,16,128]{3,2,1,0:T(8,128)} %rank_parts.1), calls=%async_computation.1 | async-start | bytes 786432 | tf_op jit(solution)/shard_map/all_to_all | solution.py:20
  63.6 1.4 %copy-start.7 = (f32[8,6,16,128]{3,2,1,0:T(8,128)}, f32[8,6,16,128]{3,2,1,0:T(8,128)S(1)}, u32[]{:S(2)}) copy-start(f32[8,6,16,128]{3,2,1,0:T(8,128)S(1)} %all-to-all-done.1) | copy-start | bytes 1179652
  65.0 24.1 %all-to-all-start.2 = ((bf16[4,2,2,24,2048]{4,3,2,1,0:T(8,128)(2,1)}), bf16[4,2,2,24,2048]{4,3,2,1,0:T(8,128)(2,1)S(1)}, u32[]{:S(2)}, u32[]{:S(2)}) async-start(bf16[4,2,2,24,2048]{4,3,2,1,0:T(8,128)(2,1)} %broadcast_in_dim.4), calls=%async_computation.2 | async-start | bytes 3145728 | tf_op jit(solution)/shard_map/all_to_all | solution.py:20
  70.0 14.8 %collective-permute-start.3 = (f32[6,16,128]{2,1,0:T(8,128)S(1)}, f32[6,16,128]{2,1,0:T(8,128)S(1)}, u32[]{:S(2)}, u32[]{:S(2)}) collective-permute-start(f32[6,16,128]{2,1,0:T(8,128)S(1)} %reduce_sum.9.own_ref), channel_id=1, source_target_pairs={{0,256},{256,0},{1,257},{257,1},{2,258},{258,2},{3,259},{259,3},{4... | collective-permute-start | bytes 147464 | tf_op jit(solution)/shard_map/ppermute | solution.py:284
  74.6 37.5 %collective-permute-start.5 = (bf16[2,2,24,2048]{3,2,1,0:T(8,128)(2,1)S(1)}, bf16[2,2,24,2048]{3,2,1,0:T(8,128)(2,1)}, u32[]{:S(2)}, u32[]{:S(2)}) collective-permute-start(bf16[2,2,24,2048]{3,2,1,0:T(8,128)(2,1)S(1)} %pad_maximum_fusion.1.refs_0_), channel_id=1, source_target_pairs={{0,64},{64,128},{128,192},{192,0},{1,65},{65,129},{129,193},{193,1... | collective-permute-start | bytes 1179656 | tf_op jit(solution)/shard_map/ppermute | solution.py:292
  77.9 34.1 %collective-permute-start.6 = (bf16[2,2,24,2048]{3,2,1,0:T(8,128)(2,1)S(1)}, bf16[2,2,24,2048]{3,2,1,0:T(8,128)(2,1)}, u32[]{:S(2)}, u32[]{:S(2)}) collective-permute-start(bf16[2,2,24,2048]{3,2,1,0:T(8,128)(2,1)S(1)} %pad_maximum_fusion.1.refs_0_), channel_id=1, source_target_pairs={{0,192},{64,0},{128,64},{192,128},{1,193},{65,1},{129,65},{193,129... | collective-permute-start | bytes 1179656 | tf_op jit(solution)/shard_map/ppermute | solution.py:292
  81.1 31.0 %collective-permute-start.7 = (bf16[2,2,24,2048]{3,2,1,0:T(8,128)(2,1)S(1)}, bf16[2,2,24,2048]{3,2,1,0:T(8,128)(2,1)}, u32[]{:S(2)}, u32[]{:S(2)}) collective-permute-start(bf16[2,2,24,2048]{3,2,1,0:T(8,128)(2,1)S(1)} %pad_maximum_fusion.1.refs_0_), channel_id=1, source_target_pairs={{0,128},{64,192},{128,0},{192,64},{1,129},{65,193},{129,1},{193,65... | collective-permute-start | bytes 1179656 | tf_op jit(solution)/shard_map/ppermute | solution.py:292
  85.6 0.7 copy-start.4
  89.1 23.0 %all-to-all-start.3 = ((f32[8,13,512]{2,1,0:T(8,128)}), f32[8,13,512]{2,1,0:T(8,128)S(1)}, u32[]{:S(2)}, u32[]{:S(2)}) async-start(f32[8,13,512]{2,1,0:T(8,128)} %copy-done.4), calls=%async_computation.3 | async-start | bytes 524288 | tf_op jit(solution)/shard_map/all_to_all | solution.py:20
  98.6 23.8 %collective-permute-start.8 = (bf16[8,24,512]{2,1,0:T(8,128)(2,1)S(1)}, bf16[8,24,512]{2,1,0:T(8,128)(2,1)S(1)}, u32[]{:S(2)}, u32[]{:S(2)}) collective-permute-start(bf16[8,24,512]{2,1,0:T(8,128)(2,1)S(1)} %base_product.5), channel_id=1, source_target_pairs={{0,2},{2,0},{1,3},{3,1},{4,6},{6,4},{5,7},{7,5},{8,10},{10,8},{9,1... | collective-permute-start | bytes 589832 | tf_op jit(solution)/shard_map/ppermute | solution.py:297
  106.8 15.7 %collective-permute-start.10 = (bf16[8,24,512]{2,1,0:T(8,128)(2,1)S(1)}, bf16[8,24,512]{2,1,0:T(8,128)(2,1)S(1)}, u32[]{:S(2)}, u32[]{:S(2)}) collective-permute-start(bf16[8,24,512]{2,1,0:T(8,128)(2,1)S(1)} %base_product.3), channel_id=1, source_target_pairs={{0,34},{2,32},{32,2},{34,0},{1,35},{3,33},{33,3},{35,1},{4,38},{6,... | collective-permute-start | bytes 589832 | tf_op jit(solution)/shard_map/ppermute | solution.py:299
  113.0 7.5 %copy-start.8 = (f32[8,12,512]{2,0,1:T(8,128)S(1)}, f32[8,12,512]{2,0,1:T(8,128)}, u32[]{:S(2)}) copy-start(f32[8,12,512]{2,0,1:T(8,128)} %copy.40) | copy-start | bytes 589828
  118.2 4.3 %collective-permute-start.9 = (bf16[8,24,512]{2,1,0:T(8,128)(2,1)S(1)}, bf16[8,24,512]{2,1,0:T(8,128)(2,1)S(1)}, u32[]{:S(2)}, u32[]{:S(2)}) collective-permute-start(bf16[8,24,512]{2,1,0:T(8,128)(2,1)S(1)} %get-tuple-element.41), channel_id=1, source_target_pairs={{0,32},{32,0},{1,33},{33,1},{2,34},{34,2},{3,35},{35,3},{4,36},{36... | collective-permute-start | bytes 589832 | tf_op jit(solution)/shard_map/ppermute | solution.py:303
  (1 other events, 0.7 us)
Sparse Core Ops, SparseCore 0:
  17.5 65.2 all-gather.2
